TPU v7x, 256 devices: a whole 4x4x8 slice. The times are simulated.
256 devices in a mesh: ctx: 32 (over y, z), head: 8 (over x, core).
Axes of the slice: x: 4, y: 4, z: 8, core: 2. Of those that a mesh axis runs over, the one named last changes fastest.
Arguments:
- tokens: bfloat16 [16384, 2560], P('ctx', 'head'), may hold values from -6 to 6
- tangent_tokens: bfloat16 [16384, 2560], P('ctx', 'head'), may hold values from -6 to 6
- log_decay: float32 [16384, 80], P('ctx', 'head'), may hold values from -1.5 to 0, as said below
- tangent_decay: float32 [16384, 80], P('ctx', 'head'), may hold values from -0.096 to 0.096
- w_inner: bfloat16 [2560, 5120], P(None, 'head'), may hold values from -0.125 to 0.125
- w_bmat: bfloat16 [2560, 128], replicated, may hold values from -0.001953125 to 0.001953125
- w_cmat: bfloat16 [2560, 128], replicated, may hold values from -0.125 to 0.125
- conv_inner: float32 [4, 5120], P(None, 'head'), may hold values from -3 to 3
- conv_bc: float32 [4, 256], replicated, may hold values from -3 to 3
- skip_gain: float32 [80], P('head'), may hold values from 0.5 to 2
- w_out: bfloat16 [5120, 2560], P('head'), may hold values from -0.078125 to 0.078125
Outputs:
- output: bfloat16 [16384, 2560], P('ctx', 'head')
- output_tangent: bfloat16 [16384, 2560], P('ctx', 'head')
Inputs may be any that keep to these rules, and one draw needn't show every extreme that they name: `log_decay`: negative; the natural logarithm of the factor by which each head's state is multiplied at each token.
All inputs are finite; a program needn't handle non-finite values.
Results may differ from a plain program's by a relative error of at most 0.019.
Values may be sent and summed in bfloat16 or wider, within the bound.
No kernel may reach another device: no remote copies, remote signals or barrier semaphores. Data moves between devices by JAX's collectives and lax.ppermute only.
A program may use at most 128 MiB of HBM per device.

v0:
```python
import jax
import jax.numpy as jnp
from jax import lax
from jax.sharding import PartitionSpec as P

HEAD_DIM = 64
SPAN = 256


def shifted(block, axis, distance):
    devices = range(lax.axis_size(axis))
    route = [(i - distance, i) for i in devices if i - distance in devices]
    return lax.ppermute(block, axis, route)


def carried_in(part, axis, combine, identity):
    place = lax.axis_index(axis)
    gathered = jax.tree.map(lambda a: lax.all_gather(a, axis), part)
    state = jax.tree.map(lambda a, e: jnp.zeros_like(a) + jnp.asarray(e, a.dtype), part, identity)

    def one(step, state):
        return combine(
            state, jax.tree.map(lambda a: lax.dynamic_index_in_dim(a, step, 0, False), gathered)
        )

    return lax.fori_loop(0, place, one, state)


def depthwise(padded, kernel):
    length = padded.shape[0] - kernel.shape[0] + 1
    summed = kernel[0] * padded[0:length]
    for offset in range(1, kernel.shape[0]):
        summed = summed + kernel[offset] * padded[offset : offset + length]
    return summed


def activate(values):
    return jax.nn.silu(values).astype(jnp.bfloat16)


def span_parts(inputs, writer, reader, decays):
    cumulative = jnp.cumsum(decays, axis=0)
    length = decays.shape[0]
    causal = lax.broadcasted_iota(jnp.int32, (length, length), 0) >= lax.broadcasted_iota(
        jnp.int32, (length, length), 1
    )
    differences = cumulative.T[:, :, None] - cumulative.T[:, None, :]
    weights = jnp.exp(jnp.where(causal[None], differences, -jnp.inf))
    scores = jnp.dot(reader, writer.T, preferred_element_type=jnp.float32)
    mixing = (weights * scores[None]).astype(jnp.bfloat16)
    within = jnp.einsum("hts,shp->thp", mixing, inputs, preferred_element_type=jnp.float32)
    remaining = jnp.exp(cumulative[-1][None, :] - cumulative)
    scaled = (inputs * remaining[:, :, None]).astype(jnp.bfloat16)
    block_state = jnp.einsum("shp,sn->hpn", scaled, writer, preferred_element_type=jnp.float32)
    return (cumulative, within, block_state)


def carried(reader, cumulative, initial):
    readout = jnp.einsum(
        "tn,hpn->thp", reader, initial.astype(jnp.bfloat16), preferred_element_type=jnp.float32
    )
    return jnp.exp(cumulative)[:, :, None] * readout


def combine(earlier, later):
    early_total, early_slope, early_state, early_tangent = earlier
    late_total, late_slope, late_state, late_tangent = later
    retain = jnp.exp(late_total)
    return (
        early_total + late_total,
        early_slope + late_slope,
        retain * early_state + late_state,
        retain * (early_tangent + late_slope * early_state) + late_tangent,
    )


def on_device(
    tokens,
    tangent_tokens,
    log_decay,
    tangent_decay,
    w_inner,
    w_bmat,
    w_cmat,
    conv_inner,
    conv_bc,
    skip_gain,
    w_out,
):
    length = tokens.shape[0]
    width = w_inner.shape[1]
    state_len = w_bmat.shape[1]
    heads_here = width // HEAD_DIM
    margin = conv_inner.shape[0] - 1
    blocks = length // SPAN
    stacked = jnp.concatenate([tokens, tangent_tokens], 0)
    shard_piece = lax.all_gather(stacked, "head", axis=1, tiled=True)
    sums = (
        jnp.dot(shard_piece, w_inner, preferred_element_type=jnp.float32),
        jnp.dot(shard_piece, w_bmat, preferred_element_type=jnp.float32),
        jnp.dot(shard_piece, w_cmat, preferred_element_type=jnp.float32),
    )
    projected = jnp.concatenate([summand.astype(jnp.bfloat16) for summand in sums], 1)
    edges = jnp.stack([projected[length - margin : length], projected[2 * length - margin :]])
    previous = shifted(edges, "ctx", 1)
    kernel = jnp.concatenate([conv_inner, conv_bc], 1)
    primal_conv = depthwise(jnp.concatenate([previous[0], projected[:length]], 0), kernel)
    tangent_conv = depthwise(jnp.concatenate([previous[1], projected[length:]], 0), kernel)
    mixed, mixed_dot = jax.jvp(activate, (primal_conv,), (tangent_conv,))

    def separate(values):
        inputs = values[:, :width].reshape(blocks, SPAN, heads_here, HEAD_DIM)
        writer = values[:, width : width + state_len].reshape(blocks, SPAN, state_len)
        reader = values[:, width + state_len :].reshape(blocks, SPAN, state_len)
        return (inputs, writer, reader)

    inputs, writer, reader = separate(mixed)
    inputs_dot, writer_dot, reader_dot = separate(mixed_dot)
    decays = log_decay.reshape(blocks, SPAN, heads_here)
    decays_dot = tangent_decay.reshape(blocks, SPAN, heads_here)
    (cumulative, within, block_state), (cumulative_dot, within_dot, block_dot) = jax.jvp(
        jax.vmap(span_parts),
        (inputs, writer, reader, decays),
        (inputs_dot, writer_dot, reader_dot, decays_dot),
    )

    def summarize(cumulative, block_state):
        summed = cumulative[0, -1]
        running = block_state[0]
        summed = summed + cumulative[1, -1]
        running = jnp.exp(cumulative[1, -1])[:, None, None] * running + block_state[1]
        return (summed[:, None, None], running)

    (decay_sum, own_state), (decay_sum_dot, own_dot) = jax.jvp(
        summarize, (cumulative, block_state), (cumulative_dot, block_dot)
    )
    message = (decay_sum, decay_sum_dot, own_state, own_dot)
    empty = tuple((jnp.zeros_like(member) for member in message))
    arriving = carried_in(message, "ctx", combine, empty)
    entry_state = arriving[2]
    entry_dot = arriving[3]

    def finish(initial, cumulative, within, block_state, inputs, reader):
        outputs = []
        for position in range(cumulative.shape[0]):
            combined = (
                within[position]
                + carried(reader[position], cumulative[position], initial)
                + skip_gain[None, :, None] * inputs[position]
            )
            outputs.append(combined.astype(jnp.bfloat16))
            if position + 1 < cumulative.shape[0]:
                initial = (
                    jnp.exp(cumulative[position, -1])[:, None, None] * initial
                    + block_state[position]
                )
        return jnp.stack(outputs)

    inner, inner_dot = jax.jvp(
        finish,
        (entry_state, cumulative, within, block_state, inputs, reader),
        (entry_dot, cumulative_dot, within_dot, block_dot, inputs_dot, reader_dot),
    )
    flattened = jnp.concatenate([inner.reshape(length, width), inner_dot.reshape(length, width)], 0)
    partial_term = jnp.dot(flattened, w_out, preferred_element_type=jnp.float32).astype(
        jnp.bfloat16
    )
    summed = (
        lax.psum_scatter(partial_term, "head", scatter_dimension=1, tiled=True)
        .astype(jnp.float32)
        .astype(jnp.bfloat16)
    )
    return (summed[:length], summed[length:])


def solution(mesh):
    in_specs = (
        P("ctx", "head"),
        P("ctx", "head"),
        P("ctx", "head"),
        P("ctx", "head"),
        P(None, "head"),
        P(),
        P(),
        P(None, "head"),
        P(),
        P("head"),
        P("head", None),
    )
    out_specs = (P("ctx", "head"), P("ctx", "head"))
    return jax.shard_map(
        on_device, mesh=mesh, in_specs=in_specs, out_specs=out_specs, check_vma=False
    )
```

profile of v0, /device:TPU:32, one launch (start us, length us, event | category | flops | bytes accessed | tf_op | source)
XLA Modules:
  0.0 472.6 jit_solution(4515868981488050816)
XLA Ops:
  7.3 2.1 pad_maximum_fusion.3
  16.0 35.6 %all-gather.6.cloned.1.call-done = bf16[1024,2560]{0,1:T(8,128)(2,1)} async-done(((bf16[1024,320]{0,1:T(8,128)(2,1)}), bf16[1024,2560]{0,1:T(8,128)(2,1)}) %all-gather.6.cloned.1.call-update) | async-done | bytes 5242896 | tf_op jit(solution)/shard_map/all_gather | solution.py:97
  51.6 3.7 convolution_convert_fusion.2
  57.9 3.8 convolution_convert_fusion.1
  62.1 3.6 collective-permute-start
  65.9 10.8 %collective-permute-done = bf16[2,3,896]{1,2,0:T(8,128)(2,1)S(1)} collective-permute-done((bf16[2,3,896]{1,2,0:T(8,128)(2,1)S(1)}, bf16[2,3,896]{1,2,0:T(8,128)(2,1)S(1)}, u32[]{:S(2)}, u32[]{:S(2)}) %collective-permute-start) | collective-permute-done | bytes 10784 | tf_op jit(solution)/shard_map/ppermute | solution.py:13
  76.7 3.5 fusion.28
  85.8 2.7 reshape.236
  88.4 2.7 reshape.227
  91.8 1.5 fusion.67
  93.4 1.9 fusion.54
  98.3 1.3 copy.155
  101.8 1.2 mul.375
  103.0 43.3 %all-gather = f32[32,1,10]{2,1,0:T(1,128)} all-gather(f32[1,1,10]{2,1,0:T(1,128)} %copy.161), channel_id=2, replica_groups=mesh['ctx'=32,'head'=8] {'ctx'}, dimensions={0}, use_global_device_ids=true | all-gather | bytes 1320 | tf_op jit(solution)/shard_map/all_gather | solution.py:18
  146.3 39.7 %all-gather.1 = f32[32,1,10]{2,1,0:T(1,128)} all-gather(f32[1,1,10]{2,1,0:T(1,128)S(1)} %copy.170), channel_id=3, replica_groups=mesh['ctx'=32,'head'=8] {'ctx'}, dimensions={0}, use_global_device_ids=true | all-gather | bytes 1320 | tf_op jit(solution)/shard_map/all_gather | solution.py:18
  187.4 1.4 fusion.92
  190.6 1.6 copy.214
  192.2 1.2 fusion.105
  193.4 1.2 fusion.106
  194.7 2.0 fusion.101
  197.9 1.4 fusion.3
  199.3 2.5 fusion.29
  201.7 3.4 fusion.31
  206.3 109.4 %all-gather.10.cloned.1.call-done = f32[32,10,64,128]{3,2,1,0:T(8,128)} async-done(((f32[1,10,64,128]{3,2,1,0:T(8,128)}), f32[32,10,64,128]{3,2,1,0:T(8,128)}) %all-gather.10.cloned.1.call-update) | async-done | bytes 10485776 | tf_op jit(solution)/shard_map/all_gather | solution.py:18
  317.2 2.9 while.16
  317.9 2.3 bitcast_add_fusion.5
  320.1 1.2 fusion.77
  321.4 1.2 fusion.89
  327.3 1.3 fusion.48
  331.4 6.1 %convolution_convert_fusion = bf16[1024,2560]{0,1:T(8,128)(2,1)} fusion(bf16[640,2560]{1,0:T(8,128)(2,1)S(1)} %copy-done, bf16[512,640]{0,1:T(8,128)(2,1)S(1)} %bitcast.185, bf16[512,640]{0,1:T(8,128)(2,1)S(1)} %bitcast.186), kind=kOutput, calls=%fused_computation.7 | convolution fusion | flops 3360686080 | bytes 9830400 | tf_op jit(solution)/shard_map/dot_general | solution.py:165
  337.6 126.5 %reduce-scatter.2.cloned.1.call-done = bf16[1024,320]{0,1:T(8,128)(2,1)} async-done(((bf16[1024,2560]{0,1:T(8,128)(2,1)}), bf16[1024,320]{0,1:T(8,128)(2,1)}) %reduce-scatter.2.cloned.1.call-update) | async-done | bytes 655376 | tf_op jit(solution)/shard_map/reduce_scatter | solution.py:169
  464.1 1.9 fusion.104
  (161 shorter events, 35.9 us)
Async XLA Ops:
  7.2 324.3 %copy-start = (bf16[640,2560]{1,0:T(8,128)(2,1)S(1)}, bf16[640,2560]{1,0:T(8,128)(2,1)}, u32[]{:S(2)}) copy-start(bf16[640,2560]{1,0:T(8,128)(2,1)} %param.23) | copy-start | bytes 9830404
  7.2 3.9 copy-start.28
  7.2 7.8 %copy-start.30 = (f32[4,640]{1,0:T(4,128)S(1)}, f32[4,640]{1,0:T(4,128)}, u32[]{:S(2)}) copy-start(f32[4,640]{1,0:T(4,128)} %param.20) | copy-start | bytes 30724
  7.2 7.8 %copy-start.33 = (f32[4,256]{1,0:T(4,128)S(1)}, f32[4,256]{1,0:T(4,128)}, u32[]{:S(2)}) copy-start(f32[4,256]{1,0:T(4,128)} %param.21) | copy-start | bytes 12292
  7.2 44.3 %all-gather.6.cloned.1.call-start = ((), (), s32[]{:S(2)}) async-start(), calls=%async_computation.1 | async-start | bytes 5898240 | tf_op jit(solution)/shard_map/all_gather | solution.py:97
  9.4 196.9 %all-gather.8.cloned.1.call-start = ((), (), s32[]{:S(2)}) async-start(), calls=%async_computation.2 | async-start | bytes 10813440 | tf_op jit(solution)/shard_map/all_gather | solution.py:18
  11.1 44.2 %copy-start.21 = (f32[2,10,256]{2,0,1:T(2,128)}, f32[2,10,256]{2,0,1:T(2,128)S(1)}, u32[]{:S(2)}) copy-start(f32[2,10,256]{2,0,1:T(2,128)S(1)} %reduce_window_sum.43) | copy-start | bytes 61444
  12.7 42.6 %copy-start.19 = (f32[2,10,256]{2,1,0:T(8,128)}, f32[2,10,256]{2,1,0:T(8,128)S(1)}, u32[]{:S(2)}) copy-start(f32[2,10,256]{2,1,0:T(8,128)S(1)} %reshape.256) | copy-start | bytes 61444
  51.6 4.2 copy-start.38
  51.6 4.4 copy-start.40
  62.1 14.6 %collective-permute-start = (bf16[2,3,896]{1,2,0:T(8,128)(2,1)S(1)}, bf16[2,3,896]{1,2,0:T(8,128)(2,1)S(1)}, u32[]{:S(2)}, u32[]{:S(2)}) collective-permute-start(bf16[2,3,896]{1,2,0:T(8,128)(2,1)S(1)} %pad_maximum_fusion.6), channel_id=1, source_target_pairs={{0,8},{8,16},{16,24},{24,32},{32,40},{40,48},{48,56},{56,64},{64,7... | collective-permute-start | bytes 32264 | tf_op jit(solution)/shard_map/ppermute | solution.py:13
  80.3 3.1 copy-start.5
  80.8 3.3 copy-start.3
  91.8 3.5 copy-start.6
  91.8 3.5 copy-start.18
  91.8 3.5 copy-start.22
  93.3 3.2 copy-start.35
  93.3 3.2 copy-start.37
  97.6 218.1 %all-gather.10.cloned.1.call-start = ((), (), s32[]{:S(2)}) async-start(), calls=%async_computation.3 | async-start | bytes 10813440 | tf_op jit(solution)/shard_map/all_gather | solution.py:18
  98.3 365.8 %reduce-scatter.2.cloned.1.call-start = ((), (), s32[]{:S(2)}) async-start(), calls=%async_computation.4 | async-start | bytes 5898240 | tf_op jit(solution)/shard_map/reduce_scatter | solution.py:169
  192.2 4.5 copy-start.4
  194.6 3.2 copy-start.17
  194.6 3.2 copy-start.26
  194.6 3.2 copy-start.29
  199.2 2.5 copy-start.20
  317.2 2.9 copy-start.32
  320.1 3.6 copy-start.1
  321.4 4.6 copy-start.2
  321.4 4.6 copy-start.14
  321.4 4.6 copy-start.16
  321.4 4.6 copy-start.25
  321.4 4.6 copy-start.31
  (14 other events, 26.0 us)
Sparse Core Ops, SparseCore 0:
  9.9 41.6 all-gather.5
  97.7 108.5 all-gather.7
  209.5 106.1 all-gather.9
  337.7 126.3 reduce-scatter.1
where the time goes:
time: 475 us; the launch traced here: 473 us
  waiting for transfers between devices  284 us (60%)
  blocking collectives  83 us (17%)
  matrix products  35.1 us (7%)
  local copies, waits for them, and re-layouts  31.6 us (7%)
  other arithmetic  20.3 us (4%)
  between operations  14.6 us (3%)
    reduce_scatter x1, waiting for transfers between devices, on_device(): lax.psum_scatter(partial_term, 'head', scatter_dimension=1, tiled=True)  127 us
    all_gather x2, waiting for transfers between devices, carried_in(): gathered = jax.tree.map(lambda a: lax.all_gather(a, axis), part)  111 us
    all_gather x2, blocking collectives, carried_in(): gathered = jax.tree.map(lambda a: lax.all_gather(a, axis), part)  83 us
    all_gather x1, waiting for transfers between devices, on_device(): shard_piece = lax.all_gather(stacked, 'head', axis=1, tiled=True)  35.6 us
    ppermute x1, waiting for transfers between devices, shifted(): return lax.ppermute(block, axis, route)  10.8 us
  transfers between devices with their start and end apart: 5, of which 5 were waited for; matrix products, arithmetic and copies ran while one was open for 6% of the time, Pallas kernels for 0%

commit v1 on v0

v1 whole, which is shorter than its diff:
```python
import functools

import jax
import jax.numpy as jnp
from jax import lax
from jax.experimental import pallas as pl
from jax.experimental.pallas import tpu as pltpu
from jax.sharding import PartitionSpec as P

HEAD_DIM = 64
SPAN = 256
MIB = 1 << 20
BF16 = jnp.bfloat16
F32 = jnp.float32
HIGHEST = lax.Precision.HIGHEST

NN = (((1,), (0,)), ((), ()))
NT = (((1,), (1,)), ((), ()))
TN = (((0,), (0,)), ((), ()))


def mm(a, b, dims=NN, precision=None):
    return lax.dot_general(a, b, dims, precision=precision, preferred_element_type=F32)


def call(body, out, scratch=(), flops=0, bytes_accessed=0, smem=(), count=0, limit=40):
    in_specs = [
        pl.BlockSpec(memory_space=pltpu.SMEM if i in smem else pltpu.VMEM) for i in range(count)
    ]
    out_specs = jax.tree.map(lambda _: pl.BlockSpec(memory_space=pltpu.VMEM), out)
    return pl.pallas_call(
        body,
        out_shape=out,
        in_specs=in_specs,
        out_specs=out_specs,
        scratch_shapes=list(scratch),
        cost_estimate=pl.CostEstimate(
            flops=flops, bytes_accessed=bytes_accessed, transcendentals=0
        ),
        compiler_params=pltpu.CompilerParams(vmem_limit_bytes=limit * MIB),
    )


def spread(rows, width):
    head = lax.broadcasted_iota(jnp.int32, (rows, width), 0)
    lane = lax.broadcasted_iota(jnp.int32, (rows, width), 1)
    return jnp.where(lane // HEAD_DIM == head, 1.0, 0.0).astype(F32)


def decay_body(dec, cum, cumd, rem, remd, ecum, cum_t, cumd_t, vec, tot):
    s = lax.broadcasted_iota(jnp.int32, (SPAN, SPAN), 0)
    t = lax.broadcasted_iota(jnp.int32, (SPAN, SPAN), 1)
    upper = jnp.where(s <= t, 1.0, 0.0).astype(F32)
    lower = jnp.where(t <= s, 1.0, 0.0).astype(F32)
    ends = []
    for b in range(dec.shape[1] // SPAN):
        lanes = slice(b * SPAN, (b + 1) * SPAN)
        both = dec[:, lanes]
        c = mm(both, upper, NN, HIGHEST)
        c_t = mm(lower, both, NT, HIGHEST)
        p, d = c[:16], c[16:]
        cum[:, lanes] = p
        cumd[:, lanes] = d
        ecum[:, lanes] = jnp.exp(p)
        r = jnp.exp(p[:, SPAN - 1 :] - p)
        rem[:, lanes] = r
        remd[:, lanes] = r * (d[:, SPAN - 1 :] - d)
        cum_t[lanes, :] = c_t[:, :16]
        cumd_t[lanes, :] = c_t[:, 16:]
        ends.append(c_t[SPAN - 1 :, :])
    rows = jnp.concatenate(
        [ends[0][:, :16], ends[0][:, 16:], ends[1][:, :16], ends[1][:, 16:]]
        + [jnp.zeros((4, 16), F32)],
        0,
    )
    wide = mm(rows, spread(16, vec.shape[1]), NN, HIGHEST)
    row = lax.broadcasted_iota(jnp.int32, wide.shape, 0)
    vec[...] = jnp.where((row == 0) | (row == 2), jnp.exp(wide), wide)
    total = ends[0] + ends[1]
    tot[...] = jnp.zeros(tot.shape, F32)
    tot[0:1, 0:16] = total[:, :16]
    tot[1:2, 0:16] = total[:, 16:]


def totals_body(total, slope, retain_out, slope_out):
    one_hot = spread(total.shape[1], retain_out.shape[1])
    retain_out[...] = jnp.exp(mm(total[...], one_hot, NN, HIGHEST))
    slope_out[...] = mm(slope[...], one_hot, NN, HIGHEST)


def project(order, pieces, w_t, full, ext, halo):
    rows = pieces[0].shape[0]
    for i, piece in enumerate(pieces):
        full[pl.ds(pl.multiple_of(order[i] * rows, rows), rows), :] = piece[...]
    margin = halo.shape[1]
    ext[:, :margin] = halo[...].astype(F32)
    for b in range(full.shape[1] // SPAN):
        summed = mm(w_t[...], full[:, b * SPAN : (b + 1) * SPAN])
        ext[:, margin + b * SPAN : margin + (b + 1) * SPAN] = summed.astype(BF16).astype(F32)


def conv_slab(ext, taps, rows, margin):
    slab = ext[rows, :]
    count = taps.shape[1]
    kernel = taps[rows, :]
    summed = None
    for k in range(count):
        back = count - 1 - k
        moved = pltpu.roll(slab, back, 1) if back else slab
        term = kernel[:, k : k + 1] * moved[:, margin:]
        summed = term if summed is None else summed + term
    return summed


def primal_body(order, *refs):
    pieces, (w_t, halo, taps, mixed, gate, full, ext) = refs[:8], refs[8:]
    project(order, pieces, w_t, full, ext, halo)

    @pl.loop(0, mixed.shape[0] // 64)
    def _(i):
        rows = pl.ds(pl.multiple_of(i * 64, 64), 64)
        v = conv_slab(ext, taps, rows, halo.shape[1])
        sig = 1.0 / (1.0 + jnp.exp(-v))
        mixed[rows, :] = (v * sig).astype(BF16)
        gate[rows, :] = sig * (1.0 + v * (1.0 - sig))


def interleave(back):
    r = lax.broadcasted_iota(jnp.int32, (256, 256), 1 if back else 0)
    k = lax.broadcasted_iota(jnp.int32, (256, 256), 0 if back else 1)
    source = 4 * (r >> 3) + (r & 3) + 128 * ((r >> 2) & 1)
    return jnp.where(k == source, 1.0, 0.0).astype(BF16)


def tangent_body(order, *refs):
    pieces, refs = refs[:8], refs[8:]
    (w_t, halo, taps, mixed, gate, rem, remd, vec) = refs[:8]
    (mixed_dot, message, state0, state0_dot, full, ext, scaled) = refs[8:]
    project(order, pieces, w_t, full, ext, halo)

    @pl.loop(0, mixed.shape[0] // 64)
    def _(i):
        rows = pl.ds(pl.multiple_of(i * 64, 64), 64)
        v = conv_slab(ext, taps, rows, halo.shape[1])
        mixed_dot[rows, :] = (gate[rows, :] * v).astype(BF16)

    width = vec.shape[1]
    states = []
    for b in range(2):
        lanes = slice(b * SPAN, (b + 1) * SPAN)
        for h in range(width // HEAD_DIM):
            rows = slice(h * HEAD_DIM, (h + 1) * HEAD_DIM)
            value = mixed[rows, lanes].astype(F32)
            r = rem[h : h + 1, lanes]
            scaled[rows, SPAN:] = (value * r).astype(BF16)
            scaled[rows, :SPAN] = (
                mixed_dot[rows, lanes].astype(F32) * r + value * remd[h : h + 1, lanes]
            ).astype(BF16)
        writer = mixed[width : width + 128, lanes]
        writer_dot = mixed_dot[width : width + 128, lanes]
        state = mm(writer, scaled[:, SPAN:], NT)
        state_dot = mm(writer, scaled[:, :SPAN], NT) + mm(writer_dot, scaled[:, SPAN:], NT)
        states.append((state, state_dot))
    (s0, d0), (s1, d1) = states
    state0[...] = s0
    state0_dot[...] = d0
    retain = vec[2:3, :]
    own = retain * s0 + s1
    own_dot = retain * (d0 + vec[3:4, :] * s0) + d1
    stacked = jnp.concatenate([own.astype(BF16), own_dot.astype(BF16)], 0)
    message[...] = mm(interleave(False), stacked).astype(BF16)


def within_body(mixed, mixed_dot, cum, cumd, cum_t, cumd_t, gain, within, within_dot, sc, scd):
    width = within.shape[0]
    state = (mixed.shape[0] - width) // 2
    s = lax.broadcasted_iota(jnp.int32, (SPAN, SPAN), 0)
    t = lax.broadcasted_iota(jnp.int32, (SPAN, SPAN), 1)
    causal = s <= t
    for b in range(2):
        lanes = slice(b * SPAN, (b + 1) * SPAN)
        writer, reader = mixed[width : width + state, lanes], mixed[width + state :, lanes]
        writer_dot = mixed_dot[width : width + state, lanes]
        reader_dot = mixed_dot[width + state :, lanes]
        sc[...] = mm(writer, reader, TN)
        scd[...] = mm(writer_dot, reader, TN) + mm(writer, reader_dot, TN)
        for h in range(width // HEAD_DIM):
            rows = slice(h * HEAD_DIM, (h + 1) * HEAD_DIM)
            diff = cum[h : h + 1, lanes] - cum_t[lanes, h : h + 1]
            diff_dot = cumd[h : h + 1, lanes] - cumd_t[lanes, h : h + 1]
            weight = jnp.exp(jnp.where(causal, diff, -jnp.inf))
            mix = (weight * sc[...]).astype(BF16)
            mix_dot = (weight * (scd[...] + diff_dot * sc[...])).astype(BF16)
            value, value_dot = mixed[rows, lanes], mixed_dot[rows, lanes]
            both = mm(jnp.concatenate([value, value_dot], 0), mix)
            other = mm(value, mix_dot)
            skip = gain[0:1, h : h + 1]
            within[rows, lanes] = both[:HEAD_DIM] + skip * value.astype(F32)
            within_dot[rows, lanes] = (both[HEAD_DIM:] + other) + skip * value_dot.astype(F32)


def scan_body(arrived, retain, slope, leaving):
    steps, rows, width = arrived.shape
    low = lax.broadcasted_iota(jnp.int32, (rows, width), 0) >= rows // 2
    state = jnp.zeros((rows, width), F32)
    for j in range(steps):
        leaving[j] = state.astype(BF16)
        r = retain[j : j + 1, :]
        pushed = jnp.where(low, pltpu.roll(state, rows // 2, 0) * slope[j : j + 1, :], 0.0)
        state = r * (state + pushed) + arrived[j].astype(F32)


def out_product(order, w_t, gathered, values, out):
    count, rows, _ = out.shape
    for d in range(count):
        gathered[d * rows : (d + 1) * rows, :] = w_t[
            pl.ds(pl.multiple_of(order[d] * rows, rows), rows), :
        ]
    for b in range(values.shape[1] // SPAN):
        lanes = slice(b * SPAN, (b + 1) * SPAN)
        result = mm(gathered[...], values[:, lanes]).astype(BF16)
        for d in range(count):
            out[d, :, lanes] = result[d * rows : (d + 1) * rows]


def readout_body(
    order, entry, mixed, mixed_dot, within, within_dot, cumd, ecum, vec, state0, state0_dot, w_t,
    inner, inner_dot, out, gathered
):
    width = within.shape[0]
    n = state0.shape[0]
    both = mm(interleave(True), entry[...])
    for b in range(2):
        lanes = slice(b * SPAN, (b + 1) * SPAN)
        rounded = both.astype(BF16)
        reader, reader_dot = mixed[width + n :, lanes], mixed_dot[width + n :, lanes]
        read = mm(rounded[:n], reader, TN)
        read_dot = mm(rounded[:n], reader_dot, TN) + mm(rounded[n:], reader, TN)
        for h in range(width // HEAD_DIM):
            rows = slice(h * HEAD_DIM, (h + 1) * HEAD_DIM)
            e = ecum[h : h + 1, lanes]
            d = cumd[h : h + 1, lanes]
            inner[rows, lanes] = (within[rows, lanes] + e * read[rows]).astype(BF16)
            inner_dot[rows, lanes] = (
                within_dot[rows, lanes] + e * (read_dot[rows] + d * read[rows])
            ).astype(BF16)
        if b == 0:
            retain, slope = vec[0:1, :], vec[1:2, :]
            first, second = both[:n], both[n:]
            both = jnp.concatenate(
                [
                    retain * first + state0[...],
                    retain * (second + slope * first) + state0_dot[...],
                ],
                0,
            )
    out_product(order, w_t, gathered, inner, out)


def product_body(order, w_t, values, out, gathered):
    out_product(order, w_t, gathered, values, out)


def add_body(kept, received, *outs):
    for d, out in enumerate(outs):
        out[...] = (kept[d].astype(F32) + received[d].astype(F32)).astype(BF16)


def total_body(a, b, c, d, out):
    out[...] = (
        (a[...].astype(F32) + b[...].astype(F32)) + (c[...].astype(F32) + d[...].astype(F32))
    ).astype(BF16)


def on_device(
    tokens,
    tangent_tokens,
    log_decay,
    tangent_decay,
    w_inner,
    w_bmat,
    w_cmat,
    conv_inner,
    conv_bc,
    skip_gain,
    w_out,
):
    length, piece = tokens.shape
    width = w_inner.shape[1]
    state_len = w_bmat.shape[1]
    channels = width + 2 * state_len
    heads = width // HEAD_DIM
    model = w_inner.shape[0]
    n_ctx, n_head = lax.axis_size("ctx"), lax.axis_size("head")
    chips = n_head // 2
    margin = conv_inner.shape[0] - 1
    shape = jax.ShapeDtypeStruct
    place = lax.axis_index("head")
    chip, core = place // 2, place % 2

    def along(values, distance):
        route = [
            (2 * i + j, 2 * ((i + distance) % chips) + j) for i in range(chips) for j in range(2)
        ]
        return lax.ppermute(values, "head", route)

    def swap(values):
        return lax.ppermute(values, "head", [(i, i ^ 1) for i in range(n_head)])

    first, second = tokens.T, tangent_tokens.T
    first_up, first_down = along(first, 1), along(first, -1)
    second_up, second_down = along(second, 1), along(second, -1)
    first_far = along(first_up, 1)
    second_far = along(second_down, -1)
    firsts = [first, first_up, first_down, first_far]
    seconds = [second, second_up, second_down, second_far]
    firsts = firsts + [swap(v) for v in firsts]
    seconds = seconds + [swap(v) for v in seconds]
    chip_of = [chip, chip - 1, chip + 1, chip + 2]
    order = jnp.stack(
        [(i + chips) % chips * 2 + core for i in chip_of]
        + [(i + chips) % chips * 2 + (1 - core) for i in chip_of]
    ).astype(jnp.int32)

    gap = jnp.zeros((1, piece), BF16)
    edge = jnp.concatenate([tokens[length - margin :], gap, tangent_tokens[length - margin :], gap])
    edge = lax.ppermute(edge, "ctx", [(i, i + 1) for i in range(n_ctx - 1)])
    edge = lax.all_to_all(jnp.broadcast_to(edge[None], (n_head, *edge.shape)), "head", 0, 0)
    edge = edge.transpose(1, 0, 2).reshape(edge.shape[1], model)
    fill = jnp.zeros((128 - margin, model), BF16)
    before = jnp.concatenate([fill, edge[:margin], fill, edge[margin + 1 : 2 * margin + 1]])
    w_t = jnp.concatenate([w_inner, w_bmat, w_cmat], 1).T
    halo = jnp.dot(w_t, before.T, preferred_element_type=F32).astype(BF16)
    taps = jnp.concatenate([conv_inner, conv_bc], 1).T
    wout_t = w_out.T

    pad = ((0, 16 - heads), (0, 0))
    dec = jnp.concatenate([jnp.pad(log_decay.T, pad), jnp.pad(tangent_decay.T, pad)], 0)
    rows = shape((16, length), F32)
    columns = shape((length, 16), F32)
    cum, cumd, rem, remd, ecum, cum_t, cumd_t, vec, tot = call(
        decay_body,
        [rows] * 5 + [columns] * 2 + [shape((8, width), F32), shape((8, 128), F32)],
        count=1,
        flops=10**8,
        bytes_accessed=10**6,
    )(dec)
    tots = lax.all_to_all(jnp.broadcast_to(tot[None], (n_ctx, *tot.shape)), "ctx", 0, 0)
    retain, slope = call(
        totals_body, [shape((n_ctx, width), F32)] * 2, count=2, flops=10**7, bytes_accessed=10**6
    )(tots[:, 0], tots[:, 1])

    scratch = [pltpu.VMEM((model, length), BF16), pltpu.VMEM((channels, length + 128), F32)]
    cost = dict(flops=2 * channels * model * length, bytes_accessed=12 * MIB)
    mixed, gate = call(
        primal_body,
        [shape((channels, length), BF16), shape((channels, length), F32)],
        scratch,
        count=12,
        smem=(0,),
        **cost,
    )(order, *firsts, w_t, halo[:, :128], taps)
    state = shape((state_len, width), F32)
    mixed_dot, message, state0, state0_dot = call(
        tangent_body,
        [shape((channels, length), BF16), shape((2 * state_len, width), BF16), state, state],
        scratch + [pltpu.VMEM((width, 2 * SPAN), BF16)],
        count=17,
        smem=(0,),
        **cost,
    )(order, *seconds, w_t, halo[:, 128:], taps, mixed, gate, rem, remd, vec)

    share = 2 * state_len // n_ctx
    arrived = lax.all_to_all(message.reshape(n_ctx, share, width), "ctx", 0, 0)
    gains = jnp.pad(skip_gain[None], ((0, 0), (0, 16 - heads)))
    wide = shape((width, length), F32)
    within, within_dot = call(
        within_body,
        [wide, wide],
        [pltpu.VMEM((SPAN, SPAN), F32)] * 2,
        count=7,
        flops=10**10 // 2,
        bytes_accessed=8 * MIB,
    )(mixed, mixed_dot, cum, cumd, cum_t, cumd_t, gains)
    leaving = call(
        scan_body, shape((n_ctx, share, width), BF16), count=3, flops=10**8, bytes_accessed=MIB
    )(arrived, retain, slope)
    entry = lax.all_to_all(leaving, "ctx", 0, 0).reshape(2 * state_len, width)

    ring = [(chip + d) % chips for d in range(chips)]
    send_order = jnp.stack([i * 2 + (1 - core) for i in ring]).astype(jnp.int32)
    keep_order = jnp.stack([i * 2 + core for i in ring]).astype(jnp.int32)
    half = shape((chips, piece, length), BF16)
    gathered = [pltpu.VMEM((chips * piece, width), BF16)]
    cost = dict(flops=2 * chips * piece * width * length, bytes_accessed=6 * MIB)
    values = shape((width, length), BF16)
    inner, inner_dot, send = call(
        readout_body, [values, values, half], gathered, count=12, smem=(0,), **cost
    )(
        send_order, entry, mixed, mixed_dot, within, within_dot, cumd, ecum, vec, state0,
        state0_dot, wout_t,
    )
    product = call(product_body, half, gathered, count=3, smem=(0,), **cost)
    add = call(
        add_body, [shape((piece, length), BF16)] * chips, count=2, bytes_accessed=4 * MIB, flops=10**6
    )
    total = call(
        total_body, shape((piece, length), BF16), count=4, bytes_accessed=2 * MIB, flops=10**6
    )

    def finish(send, values):
        received = swap(send)
        own, *others = add(product(keep_order, wout_t, values), received)
        return total(own, *[along(v, d + 1) for d, v in enumerate(others)]).T

    send_dot = product(send_order, wout_t, inner_dot)
    return finish(send, inner), finish(send_dot, inner_dot)


def solution(mesh):
    in_specs = (
        P("ctx", "head"),
        P("ctx", "head"),
        P("ctx", "head"),
        P("ctx", "head"),
        P(None, "head"),
        P(),
        P(),
        P(None, "head"),
        P(),
        P("head"),
        P("head", None),
    )
    out_specs = (P("ctx", "head"), P("ctx", "head"))
    return jax.shard_map(
        on_device, mesh=mesh, in_specs=in_specs, out_specs=out_specs, check_vma=False
    )
```

time: 475 us -> 177 us (0.37)
  waiting for transfers between devices: 284 us -> 45.9 us
  blocking collectives: 83 us -> 0 us
  starting transfers between devices: 3.8 us -> 49.2 us
  Pallas kernels: 0 us -> 36.1 us
  matrix products: 35.1 us -> 3.48 us
  other arithmetic: 20.3 us -> 4.07 us
  between operations: 14.6 us -> 1.25 us
    all_gather x3 -> x0, waiting for transfers between devices: 146 us -> none  [the longest x2 111 us: carried_in(): gathered = jax.tree.map(lambda a: lax.all_gather(a, axis), part)]
    reduce_scatter x1 -> x0, waiting for transfers between devices: 127 us -> none  [on_device(): lax.psum_scatter(partial_term, 'head', scatter_dimension=1, tiled=True)]
    all_gather x2 -> x0, blocking collectives: 83 us -> none  [carried_in(): gathered = jax.tree.map(lambda a: lax.all_gather(a, axis), part)]
    pallas_call x0 -> x14, Pallas kernels: none -> 36.1 us  [the longest x1 8.54 us: on_device(): call(tangent_body, [shape((channels, length), BF16), shape((2 * state_len...]
    dot_general x19 -> x1, matrix products: 35.1 us -> 3.48 us  [on_device(): halo = jnp.dot(w_t, before.T, preferred_element_type=F32).astype(BF16)]
    all_to_all x0 -> x4, starting transfers between devices: none -> 29 us  [the longest x1 10.5 us: on_device(): lax.all_to_all(jnp.broadcast_to(tot[None], (n_ctx, *tot.shape)), 'ctx', 0...]
    unnamed x86 -> x72, local copies, waits for them, and re-layouts: 4.13 us -> 32.2 us
    ppermute x1 -> x23, waiting for transfers between devices: 10.8 us -> 28.8 us  [the longest x12 28.8 us: along(): return lax.ppermute(values, 'head', route)]
  transfers between devices with their start and end apart: 5 -> 27, of which waited for: 5 -> 8; matrix products, arithmetic and copies ran while one was open for 6% -> 14% of each run, Pallas kernels for 0% -> 15%
where the time goes in v1:
time: 177 us; the launch traced here: 176 us
  starting transfers between devices  49.2 us (28%)
  waiting for transfers between devices  45.9 us (26%)
  local copies, waits for them, and re-layouts  36.1 us (20%)
  Pallas kernels  36.1 us (20%)
  other arithmetic  4.07 us (2%)
  matrix products  3.48 us (2%)
    unnamed x72, local copies, waits for them, and re-layouts  32.2 us
    ppermute x12, waiting for transfers between devices, along(): return lax.ppermute(values, 'head', route)  28.8 us
    ppermute x12, starting transfers between devices, along(): return lax.ppermute(values, 'head', route)  14.1 us
    all_to_all x1, waiting for transfers between devices, on_device(): arrived = lax.all_to_all(message.reshape(n_ctx, share, width), 'ctx', 0, 0)  13.9 us
    all_to_all x1, starting transfers between devices, on_device(): lax.all_to_all(jnp.broadcast_to(tot[None], (n_ctx, *tot.shape)), 'ctx', 0...  10.5 us
    all_to_all x1, starting transfers between devices, on_device(): arrived = lax.all_to_all(message.reshape(n_ctx, share, width), 'ctx', 0, 0)  9.79 us
    pallas_call x1, Pallas kernels, on_device(): call(tangent_body, [shape((channels, length), BF16), shape((2 * state_len...  8.54 us
    pallas_call x1, Pallas kernels, on_device(): call(primal_body, [shape((channels, length), BF16), shape((channels, leng...  7.32 us
  transfers between devices with their start and end apart: 27, of which 8 were waited for; matrix products, arithmetic and copies ran while one was open for 14% of the time, Pallas kernels for 15%

profile of v1, /device:TPU:32, one launch (start us, length us, event | category | flops | bytes accessed | tf_op | source)
XLA Modules:
  0.0 176.1 jit_solution(13072094711877220431)
XLA Ops:
  0.6 1.6 collective-permute-start.8
  2.2 1.7 collective-permute-start.9
  6.2 3.8 %collective-permute-start.7 = (bf16[8,320]{1,0:T(8,128)(2,1)S(1)}, bf16[8,320]{1,0:T(8,128)(2,1)S(1)}, u32[]{:S(2)}, u32[]{:S(2)}) collective-permute-start(bf16[8,320]{1,0:T(8,128)(2,1)S(1)} %pad_maximum_fusion.5), channel_id=1, source_target_pairs={{0,8},{8,16},{16,24},{24,32},{32,40},{40,48},{48,56},{56,64},{64,7... | collective-permute-start | bytes 15368 | tf_op jit(solution)/shard_map/ppermute | solution.py:327
  10.0 1.6 collective-permute-start.1
  11.7 5.7 %copy.30 = bf16[2560,640]{0,1:T(8,128)(2,1)} copy(bf16[2560,640]{1,0:T(8,128)(2,1)} %param.15) | data formatting | bytes 6553600 | tf_op args[4]
  17.6 2.4 %copy.32 = bf16[2560,128]{0,1:T(8,128)(2,1)} copy(bf16[2560,128]{1,0:T(8,128)(2,1)} %param.17) | data formatting | bytes 1310720 | tf_op args[6]
  20.1 3.9 %fusion.1.refs_8_ = bf16[896,2560]{1,0:T(8,128)(2,1)} fusion(bf16[2560,128]{0,1:T(8,128)(2,1)} %copy.32, bf16[2560,128]{0,1:T(8,128)(2,1)S(1)} %copy.31, bf16[2560,640]{0,1:T(8,128)(2,1)} %copy.30), kind=kLoop, calls=%fused_computation.2 | loop fusion | flops 13762560 | bytes 9175040 | tf_op jit(solution)/shard_map/transpose | solution.py:332
  25.2 4.0 %all-to-all-start = ((bf16[8,8,320]{2,1,0:T(8,128)(2,1)}), bf16[8,8,320]{2,1,0:T(8,128)(2,1)S(1)}, u32[]{:S(2)}, u32[]{:S(2)}) async-start(bf16[8,8,320]{2,1,0:T(8,128)(2,1)} %broadcast_in_dim.23), calls=%async_computation | async-start | bytes 98304 | tf_op jit(solution)/shard_map/all_to_all | solution.py:328
  29.2 2.1 %collective-permute-start.10 = (bf16[320,512]{1,0:T(8,128)(2,1)S(1)}, bf16[320,512]{1,0:T(8,128)(2,1)S(1)}, u32[]{:S(2)}, u32[]{:S(2)}) collective-permute-start(bf16[320,512]{1,0:T(8,128)(2,1)S(1)} %collective-permute-done.8.refs_1_), channel_id=1, source_target_pairs={{0,2},{1,3},{2,4},{3,5},{4,6},{5,7},{6,0},{7,1},{8,10},{9,11},{10,... | collective-permute-start | bytes 983048 | tf_op jit(solution)/shard_map/ppermute | solution.py:305
  33.5 2.9 %all-to-all-done = bf16[8,8,320]{2,1,0:T(8,128)(2,1)S(1)} async-done(((bf16[8,8,320]{2,1,0:T(8,128)(2,1)}), bf16[8,8,320]{2,1,0:T(8,128)(2,1)S(1)}, u32[]{:S(2)}, u32[]{:S(2)}) %all-to-all-start) | async-done | bytes 40992 | tf_op jit(solution)/shard_map/all_to_all | solution.py:328
  37.1 10.5 %all-to-all-start.2 = ((f32[32,8,128]{2,1,0:T(8,128)}), f32[32,8,128]{2,1,0:T(8,128)S(1)}, u32[]{:S(2)}, u32[]{:S(2)}) async-start(f32[32,8,128]{2,1,0:T(8,128)} %broadcast_in_dim.24), calls=%async_computation.2 | async-start | bytes 262144 | tf_op jit(solution)/shard_map/all_to_all | solution.py:348
  48.7 3.5 %fusion.9 = bf16[896,256]{1,0:T(8,128)(2,1)S(1)} fusion(bf16[3,2560]{1,0:T(4,128)(2,1)S(1)} %slice.35, bf16[125,2560]{1,0:T(8,128)(2,1)S(1)} %broadcast_in_dim.10, bf16[3,2560]{1,0:T(4,128)(2,1)S(1)} %slice.33, bf16[2560,128]{0,1:T(8,128)(2,1)} %copy.32, bf16[2560,128]{0,1:T(8,128)(2,1)} %copy-done.24, bf16[2560,640]{0,1:T(8,128)(2,1)} %copy.30), kind=kOutput, calls=%fused_computation.10 | convolution fusion | flops 1193639936 | bytes 5716992 | tf_op jit(solution)/shard_map/dot_general | solution.py:333
  53.2 4.9 %collective-permute-done.2.refs_3_ = bf16[320,512]{1,0:T(8,128)(2,1)S(1)} collective-permute-done((bf16[320,512]{1,0:T(8,128)(2,1)S(1)}, bf16[320,512]{1,0:T(8,128)(2,1)S(1)}, u32[]{:S(2)}, u32[]{:S(2)}) %collective-permute-start.2) | collective-permute-done | bytes 327712 | tf_op jit(solution)/shard_map/ppermute | solution.py:305
  58.2 7.3 %shard_map.122 = (bf16[896,512]{1,0:T(8,128)(2,1)S(1)}, f32[896,512]{1,0:T(8,128)S(1)}) custom-call(s32[8]{0:T(128)S(1)} %stack.69.order, bf16[320,512]{1,0:T(8,128)(2,1)S(1)} %bitcast.49, bf16[320,512]{1,0:T(8,128)(2,1)S(1)} %collective-permute-done.8.refs_1_, bf16[320,512]{1,0:T(8,128)(2,1)S(1)} %collective-permute-done.9.refs_2_, ...), custom_call_target="tpu_custom_call" | custom-call | flops 2348810240 | bytes 12582912 | tf_op jit(solution)/shard_map/pallas_call | solution.py:355
  65.6 8.5 %shard_map.124 = (bf16[896,512]{1,0:T(8,128)(2,1)S(1)}, bf16[256,640]{1,0:T(8,128)(2,1)}, f32[128,640]{1,0:T(8,128)S(1)}, f32[128,640]{1,0:T(8,128)S(1)}) custom-call(s32[8]{0:T(128)S(1)} %stack.69.order, bf16[320,512]{1,0:T(8,128)(2,1)S(1)} %bitcast.45, bf16[320,512]{1,0:T(8,128)(2,1)S(1)} %collective-permute-done.refs_1_, ...), custom_call_target="tpu_custom_call" | custom-call | flops 2348810240 | bytes 12582912 | tf_op jit(solution)/shard_map/pallas_call | solution.py:364
  77.5 9.8 %all-to-all-start.1 = ((bf16[32,8,640]{2,1,0:T(8,128)(2,1)}), bf16[32,8,640]{2,1,0:T(8,128)(2,1)S(1)}, u32[]{:S(2)}, u32[]{:S(2)}) async-start(bf16[32,8,640]{2,1,0:T(8,128)(2,1)} %bitcast.22), calls=%async_computation.1 | async-start | bytes 655360 | tf_op jit(solution)/shard_map/all_to_all | solution.py:374
  87.7 13.9 %all-to-all-done.1.arrived = bf16[32,8,640]{2,1,0:T(8,128)(2,1)S(1)} async-done(((bf16[32,8,640]{2,1,0:T(8,128)(2,1)}), bf16[32,8,640]{2,1,0:T(8,128)(2,1)S(1)}, u32[]{:S(2)}, u32[]{:S(2)}) %all-to-all-start.1) | async-done | bytes 327712 | tf_op jit(solution)/shard_map/all_to_all | solution.py:374
  102.5 4.7 %all-to-all-start.3 = ((bf16[32,8,640]{2,1,0:T(8,128)(2,1)}), bf16[32,8,640]{2,1,0:T(8,128)(2,1)}, u32[]{:S(2)}, u32[]{:S(2)}) async-start(bf16[32,8,640]{2,1,0:T(8,128)(2,1)} %shard_map.126), calls=%async_computation.3 | async-start | bytes 655360 | tf_op jit(solution)/shard_map/all_to_all | solution.py:388
  107.3 4.2 %copy.29 = bf16[640,2560]{0,1:T(8,128)(2,1)S(1)} copy(bf16[640,2560]{1,0:T(8,128)(2,1)} %param.21) | data formatting | bytes 6553600 | tf_op args[10]
  115.8 2.4 %shard_map.127 = (f32[640,512]{1,0:T(8,128)S(1)}, f32[640,512]{1,0:T(8,128)S(1)}) custom-call(bf16[896,512]{1,0:T(8,128)(2,1)S(1)} %copy-done.1, bf16[896,512]{1,0:T(8,128)(2,1)S(1)} %copy-done.10, f32[16,512]{1,0:T(8,128)S(1)} %get-tuple-element.42.cum, f32[16,512]{1,0:T(8,128)S(1)} %get-tuple-element.43.cumd, f32[512,16]{1,0:T(8,128)S(1)} %copy-done.21, ...), custom_call_target="tpu_custom_call" | custom-call | flops 5000000000 | bytes 8388608 | tf_op jit(solution)/shard_map/pallas_call | solution.py:377
  127.7 4.2 %shard_map.128 = (bf16[640,512]{1,0:T(8,128)(2,1)S(1)}, bf16[640,512]{1,0:T(8,128)(2,1)S(1)}, bf16[4,320,512]{2,1,0:T(8,128)(2,1)}) custom-call(s32[4]{0:T(128)S(1)} %pad_add_fusion.1.order, bf16[256,640]{1,0:T(8,128)(2,1)} %bitcast.25.entry, bf16[896,512]{1,0:T(8,128)(2,1)S(1)} %copy-done.2, bf16[896,512]{1,0:T(8,128)(2,1)S(1)} %copy-done.11, ...), custom_call_target="tpu_custom_call" | custom-call | flops 838860800 | bytes 6291456 | tf_op jit(solution)/shard_map/pallas_call | solution.py:397
  131.9 2.8 %shard_map.133 = bf16[4,320,512]{2,1,0:T(8,128)(2,1)} custom-call(s32[4]{0:T(128)S(1)} %pad_add_fusion.1.order, bf16[2560,640]{1,0:T(8,128)(2,1)S(1)} %bitcast.35, bf16[640,512]{1,0:T(8,128)(2,1)S(1)} %get-tuple-element.57.values), custom_call_target="tpu_custom_call" | custom-call | flops 838860800 | bytes 6291456 | tf_op jit(solution)/shard_map/pallas_call | solution.py:416
  137.3 1.7 shard_map.132.kept
  139.0 1.6 shard_map.134
  140.7 1.7 shard_map.129.kept
  142.5 3.0 %collective-permute-start.21 = (bf16[320,512]{1,0:T(8,128)(2,1)S(1)}, bf16[320,512]{1,0:T(8,128)(2,1)S(1)}, u32[]{:S(2)}, u32[]{:S(2)}) collective-permute-start(bf16[320,512]{1,0:T(8,128)(2,1)S(1)} %get-tuple-element.60), channel_id=1, source_target_pairs={{0,4},{1,5},{2,6},{3,7},{4,0},{5,1},{6,2},{7,3},{8,12},{9,13},{10,... | collective-permute-start | bytes 983048 | tf_op jit(solution)/shard_map/ppermute | solution.py:305
  145.9 1.6 shard_map.130
  147.5 1.7 collective-permute-start.16
  150.5 9.0 %collective-permute-done.20.b = bf16[320,512]{1,0:T(8,128)(2,1)S(1)} collective-permute-done((bf16[320,512]{1,0:T(8,128)(2,1)S(1)}, bf16[320,512]{1,0:T(8,128)(2,1)S(1)}, u32[]{:S(2)}, u32[]{:S(2)}) %collective-permute-start.20) | collective-permute-done | bytes 327712 | tf_op jit(solution)/shard_map/ppermute | solution.py:305
  159.5 2.7 %collective-permute-done.22.d = bf16[320,512]{1,0:T(8,128)(2,1)S(1)} collective-permute-done((bf16[320,512]{1,0:T(8,128)(2,1)S(1)}, bf16[320,512]{1,0:T(8,128)(2,1)S(1)}, u32[]{:S(2)}, u32[]{:S(2)}) %collective-permute-start.22) | collective-permute-done | bytes 327712 | tf_op jit(solution)/shard_map/ppermute | solution.py:305
  163.1 9.6 %collective-permute-done.16.b = bf16[320,512]{1,0:T(8,128)(2,1)S(1)} collective-permute-done((bf16[320,512]{1,0:T(8,128)(2,1)S(1)}, bf16[320,512]{1,0:T(8,128)(2,1)S(1)}, u32[]{:S(2)}, u32[]{:S(2)}) %collective-permute-start.16) | collective-permute-done | bytes 327712 | tf_op jit(solution)/shard_map/ppermute | solution.py:305
  172.7 2.5 %collective-permute-done.18.d = bf16[320,512]{1,0:T(8,128)(2,1)S(1)} collective-permute-done((bf16[320,512]{1,0:T(8,128)(2,1)S(1)}, bf16[320,512]{1,0:T(8,128)(2,1)S(1)}, u32[]{:S(2)}, u32[]{:S(2)}) %collective-permute-start.18) | collective-permute-done | bytes 327712 | tf_op jit(solution)/shard_map/ppermute | solution.py:305
  (132 shorter events, 33.1 us)
Async XLA Ops:
  0.6 28.6 %collective-permute-start.8 = (bf16[320,512]{1,0:T(8,128)(2,1)}, bf16[320,512]{1,0:T(8,128)(2,1)S(1)}, u32[]{:S(2)}, u32[]{:S(2)}) collective-permute-start(bf16[320,512]{1,0:T(8,128)(2,1)} %bitcast.46), channel_id=1, source_target_pairs={{0,2},{1,3},{2,4},{3,5},{4,6},{5,7},{6,0},{7,1},{8,10},{9,11},{10,... | collective-permute-start | bytes 983048 | tf_op jit(solution)/shard_map/ppermute | solution.py:305
  2.2 45.6 %collective-permute-start.9 = (bf16[320,512]{1,0:T(8,128)(2,1)}, bf16[320,512]{1,0:T(8,128)(2,1)S(1)}, u32[]{:S(2)}, u32[]{:S(2)}) collective-permute-start(bf16[320,512]{1,0:T(8,128)(2,1)} %bitcast.47), channel_id=1, source_target_pairs={{0,6},{1,7},{2,0},{3,1},{4,2},{5,3},{6,4},{7,5},{8,14},{9,15},{10,... | collective-permute-start | bytes 983048 | tf_op jit(solution)/shard_map/ppermute | solution.py:305
  3.9 44.0 %collective-permute-start.11 = (bf16[320,512]{1,0:T(8,128)(2,1)}, bf16[320,512]{1,0:T(8,128)(2,1)S(1)}, u32[]{:S(2)}, u32[]{:S(2)}) collective-permute-start(bf16[320,512]{1,0:T(8,128)(2,1)} %bitcast.48), channel_id=1, source_target_pairs={{0,1},{1,0},{2,3},{3,2},{4,5},{5,4},{6,7},{7,6},{8,9},{9,8},{10,11... | collective-permute-start | bytes 983048 | tf_op jit(solution)/shard_map/ppermute | solution.py:308
  6.2 17.8 %collective-permute-start.7 = (bf16[8,320]{1,0:T(8,128)(2,1)S(1)}, bf16[8,320]{1,0:T(8,128)(2,1)S(1)}, u32[]{:S(2)}, u32[]{:S(2)}) collective-permute-start(bf16[8,320]{1,0:T(8,128)(2,1)S(1)} %pad_maximum_fusion.5), channel_id=1, source_target_pairs={{0,8},{8,16},{16,24},{24,32},{32,40},{40,48},{48,56},{56,64},{64,7... | collective-permute-start | bytes 15368 | tf_op jit(solution)/shard_map/ppermute | solution.py:327
  10.0 38.4 %collective-permute-start.1 = (bf16[320,512]{1,0:T(8,128)(2,1)}, bf16[320,512]{1,0:T(8,128)(2,1)S(1)}, u32[]{:S(2)}, u32[]{:S(2)}) collective-permute-start(bf16[320,512]{1,0:T(8,128)(2,1)} %bitcast.42), channel_id=1, source_target_pairs={{0,6},{1,7},{2,0},{3,1},{4,2},{5,3},{6,4},{7,5},{8,14},{9,15},{10,... | collective-permute-start | bytes 983048 | tf_op jit(solution)/shard_map/ppermute | solution.py:305
  17.6 11.6 %copy-start.24 = (bf16[2560,128]{0,1:T(8,128)(2,1)}, bf16[2560,128]{0,1:T(8,128)(2,1)S(1)}, u32[]{:S(2)}) copy-start(bf16[2560,128]{0,1:T(8,128)(2,1)S(1)} %copy.31) | copy-start | bytes 1966084
  20.1 11.3 %copy-start.28 = (f32[4,640]{1,0:T(4,128)S(1)}, f32[4,640]{1,0:T(4,128)}, u32[]{:S(2)}) copy-start(f32[4,640]{1,0:T(4,128)} %param.18) | copy-start | bytes 30724
  20.1 11.2 %copy-start.29 = (f32[4,256]{1,0:T(4,128)S(1)}, f32[4,256]{1,0:T(4,128)}, u32[]{:S(2)}) copy-start(f32[4,256]{1,0:T(4,128)} %param.19) | copy-start | bytes 12292
  24.0 28.2 %collective-permute-start = (bf16[320,512]{1,0:T(8,128)(2,1)S(1)}, bf16[320,512]{1,0:T(8,128)(2,1)S(1)}, u32[]{:S(2)}, u32[]{:S(2)}) collective-permute-start(bf16[320,512]{1,0:T(8,128)(2,1)S(1)} %bitcast.43), channel_id=1, source_target_pairs={{0,2},{1,3},{2,4},{3,5},{4,6},{5,7},{6,0},{7,1},{8,10},{9,11},{10,... | collective-permute-start | bytes 983048 | tf_op jit(solution)/shard_map/ppermute | solution.py:305
  25.2 11.2 %all-to-all-start = ((bf16[8,8,320]{2,1,0:T(8,128)(2,1)}), bf16[8,8,320]{2,1,0:T(8,128)(2,1)S(1)}, u32[]{:S(2)}, u32[]{:S(2)}) async-start(bf16[8,8,320]{2,1,0:T(8,128)(2,1)} %broadcast_in_dim.23), calls=%async_computation | async-start | bytes 98304 | tf_op jit(solution)/shard_map/all_to_all | solution.py:328
  29.2 19.2 %collective-permute-start.10 = (bf16[320,512]{1,0:T(8,128)(2,1)S(1)}, bf16[320,512]{1,0:T(8,128)(2,1)S(1)}, u32[]{:S(2)}, u32[]{:S(2)}) collective-permute-start(bf16[320,512]{1,0:T(8,128)(2,1)S(1)} %collective-permute-done.8.refs_1_), channel_id=1, source_target_pairs={{0,2},{1,3},{2,4},{3,5},{4,6},{5,7},{6,0},{7,1},{8,10},{9,11},{10,... | collective-permute-start | bytes 983048 | tf_op jit(solution)/shard_map/ppermute | solution.py:305
  33.5 14.4 %copy-start.20 = (f32[512,16]{1,0:T(8,128)}, f32[512,16]{1,0:T(8,128)S(1)}, u32[]{:S(2)}) copy-start(f32[512,16]{1,0:T(8,128)S(1)} %get-tuple-element.44.cum_t) | copy-start | bytes 98308
  37.1 40.4 %all-to-all-start.2 = ((f32[32,8,128]{2,1,0:T(8,128)}), f32[32,8,128]{2,1,0:T(8,128)S(1)}, u32[]{:S(2)}, u32[]{:S(2)}) async-start(f32[32,8,128]{2,1,0:T(8,128)} %broadcast_in_dim.24), calls=%async_computation.2 | async-start | bytes 262144 | tf_op jit(solution)/shard_map/all_to_all | solution.py:348
  47.8 4.9 %collective-permute-start.12 = (bf16[320,512]{1,0:T(8,128)(2,1)S(1)}, bf16[320,512]{1,0:T(8,128)(2,1)S(1)}, u32[]{:S(2)}, u32[]{:S(2)}) collective-permute-start(bf16[320,512]{1,0:T(8,128)(2,1)S(1)} %collective-permute-done.8.refs_1_), channel_id=1, source_target_pairs={{0,1},{1,0},{2,3},{3,2},{4,5},{5,4},{6,7},{7,6},{8,9},{9,8},{10,11... | collective-permute-start | bytes 983048 | tf_op jit(solution)/shard_map/ppermute | solution.py:308
  47.9 4.9 %collective-permute-start.13 = (bf16[320,512]{1,0:T(8,128)(2,1)S(1)}, bf16[320,512]{1,0:T(8,128)(2,1)S(1)}, u32[]{:S(2)}, u32[]{:S(2)}) collective-permute-start(bf16[320,512]{1,0:T(8,128)(2,1)S(1)} %collective-permute-done.9.refs_2_), channel_id=1, source_target_pairs={{0,1},{1,0},{2,3},{3,2},{4,5},{5,4},{6,7},{7,6},{8,9},{9,8},{10,11... | collective-permute-start | bytes 983048 | tf_op jit(solution)/shard_map/ppermute | solution.py:308
  48.4 9.7 %collective-permute-start.2 = (bf16[320,512]{1,0:T(8,128)(2,1)S(1)}, bf16[320,512]{1,0:T(8,128)(2,1)S(1)}, u32[]{:S(2)}, u32[]{:S(2)}) collective-permute-start(bf16[320,512]{1,0:T(8,128)(2,1)S(1)} %collective-permute-done.1.refs_2_), channel_id=1, source_target_pairs={{0,6},{1,7},{2,0},{3,1},{4,2},{5,3},{6,4},{7,5},{8,14},{9,15},{10,... | collective-permute-start | bytes 983048 | tf_op jit(solution)/shard_map/ppermute | solution.py:305
  48.4 9.8 %collective-permute-start.14 = (bf16[320,512]{1,0:T(8,128)(2,1)S(1)}, bf16[320,512]{1,0:T(8,128)(2,1)S(1)}, u32[]{:S(2)}, u32[]{:S(2)}) collective-permute-start(bf16[320,512]{1,0:T(8,128)(2,1)S(1)} %collective-permute-done.10.refs_3_), channel_id=1, source_target_pairs={{0,1},{1,0},{2,3},{3,2},{4,5},{5,4},{6,7},{7,6},{8,9},{9,8},{10,11... | collective-permute-start | bytes 983048 | tf_op jit(solution)/shard_map/ppermute | solution.py:308
  48.6 9.6 %slice-start = ((s8[4587520]{0:T(1024)(128)(4,1)}), s8[4194304]{0:T(1024)(128)(4,1)S(1)}, s32[]{:S(2)}) async-start(s8[4587520]{0:T(1024)(128)(4,1)} %bitcast.38), calls=%async_computation.4 | async-start | bytes 8388608
  52.2 13.4 %collective-permute-start.3 = (bf16[320,512]{1,0:T(8,128)(2,1)S(1)}, bf16[320,512]{1,0:T(8,128)(2,1)S(1)}, u32[]{:S(2)}, u32[]{:S(2)}) collective-permute-start(bf16[320,512]{1,0:T(8,128)(2,1)S(1)} %bitcast.44), channel_id=1, source_target_pairs={{0,1},{1,0},{2,3},{3,2},{4,5},{5,4},{6,7},{7,6},{8,9},{9,8},{10,11... | collective-permute-start | bytes 983048 | tf_op jit(solution)/shard_map/ppermute | solution.py:308
  52.7 12.9 %collective-permute-start.5 = (bf16[320,512]{1,0:T(8,128)(2,1)S(1)}, bf16[320,512]{1,0:T(8,128)(2,1)S(1)}, u32[]{:S(2)}, u32[]{:S(2)}) collective-permute-start(bf16[320,512]{1,0:T(8,128)(2,1)S(1)} %collective-permute-done.1.refs_2_), channel_id=1, source_target_pairs={{0,1},{1,0},{2,3},{3,2},{4,5},{5,4},{6,7},{7,6},{8,9},{9,8},{10,11... | collective-permute-start | bytes 983048 | tf_op jit(solution)/shard_map/ppermute | solution.py:308
  52.8 12.8 %collective-permute-start.4 = (bf16[320,512]{1,0:T(8,128)(2,1)S(1)}, bf16[320,512]{1,0:T(8,128)(2,1)S(1)}, u32[]{:S(2)}, u32[]{:S(2)}) collective-permute-start(bf16[320,512]{1,0:T(8,128)(2,1)S(1)} %collective-permute-done.refs_1_), channel_id=1, source_target_pairs={{0,1},{1,0},{2,3},{3,2},{4,5},{5,4},{6,7},{7,6},{8,9},{9,8},{10,11... | collective-permute-start | bytes 983048 | tf_op jit(solution)/shard_map/ppermute | solution.py:308
  58.1 7.4 %collective-permute-start.6 = (bf16[320,512]{1,0:T(8,128)(2,1)S(1)}, bf16[320,512]{1,0:T(8,128)(2,1)S(1)}, u32[]{:S(2)}, u32[]{:S(2)}) collective-permute-start(bf16[320,512]{1,0:T(8,128)(2,1)S(1)} %collective-permute-done.2.refs_3_), channel_id=1, source_target_pairs={{0,1},{1,0},{2,3},{3,2},{4,5},{5,4},{6,7},{7,6},{8,9},{9,8},{10,11... | collective-permute-start | bytes 983048 | tf_op jit(solution)/shard_map/ppermute | solution.py:308
  77.5 24.0 %all-to-all-start.1 = ((bf16[32,8,640]{2,1,0:T(8,128)(2,1)}), bf16[32,8,640]{2,1,0:T(8,128)(2,1)S(1)}, u32[]{:S(2)}, u32[]{:S(2)}) async-start(bf16[32,8,640]{2,1,0:T(8,128)(2,1)} %bitcast.22), calls=%async_computation.1 | async-start | bytes 655360 | tf_op jit(solution)/shard_map/all_to_all | solution.py:374
  102.5 18.3 %all-to-all-start.3 = ((bf16[32,8,640]{2,1,0:T(8,128)(2,1)}), bf16[32,8,640]{2,1,0:T(8,128)(2,1)}, u32[]{:S(2)}, u32[]{:S(2)}) async-start(bf16[32,8,640]{2,1,0:T(8,128)(2,1)} %shard_map.126), calls=%async_computation.3 | async-start | bytes 655360 | tf_op jit(solution)/shard_map/all_to_all | solution.py:388
  135.6 3.4 %collective-permute-start.19 = (bf16[4,320,512]{2,1,0:T(8,128)(2,1)}, bf16[4,320,512]{2,1,0:T(8,128)(2,1)}, u32[]{:S(2)}, u32[]{:S(2)}) collective-permute-start(bf16[4,320,512]{2,1,0:T(8,128)(2,1)} %shard_map.133), channel_id=1, source_target_pairs={{0,1},{1,0},{2,3},{3,2},{4,5},{5,4},{6,7},{7,6},{8,9},{9,8},{10,11... | collective-permute-start | bytes 3932168 | tf_op jit(solution)/shard_map/ppermute | solution.py:308
  135.6 10.3 %collective-permute-start.15 = (bf16[4,320,512]{2,1,0:T(8,128)(2,1)}, bf16[4,320,512]{2,1,0:T(8,128)(2,1)}, u32[]{:S(2)}, u32[]{:S(2)}) collective-permute-start(bf16[4,320,512]{2,1,0:T(8,128)(2,1)} %get-tuple-element.52), channel_id=1, source_target_pairs={{0,1},{1,0},{2,3},{3,2},{4,5},{5,4},{6,7},{7,6},{8,9},{9,8},{10,11... | collective-permute-start | bytes 3932168 | tf_op jit(solution)/shard_map/ppermute | solution.py:308
  140.6 18.9 %collective-permute-start.20 = (bf16[320,512]{1,0:T(8,128)(2,1)S(1)}, bf16[320,512]{1,0:T(8,128)(2,1)S(1)}, u32[]{:S(2)}, u32[]{:S(2)}) collective-permute-start(bf16[320,512]{1,0:T(8,128)(2,1)S(1)} %get-tuple-element.59), channel_id=1, source_target_pairs={{0,2},{1,3},{2,4},{3,5},{4,6},{5,7},{6,0},{7,1},{8,10},{9,11},{10,... | collective-permute-start | bytes 983048 | tf_op jit(solution)/shard_map/ppermute | solution.py:305
  142.5 17.0 %collective-permute-start.21 = (bf16[320,512]{1,0:T(8,128)(2,1)S(1)}, bf16[320,512]{1,0:T(8,128)(2,1)S(1)}, u32[]{:S(2)}, u32[]{:S(2)}) collective-permute-start(bf16[320,512]{1,0:T(8,128)(2,1)S(1)} %get-tuple-element.60), channel_id=1, source_target_pairs={{0,4},{1,5},{2,6},{3,7},{4,0},{5,1},{6,2},{7,3},{8,12},{9,13},{10,... | collective-permute-start | bytes 983048 | tf_op jit(solution)/shard_map/ppermute | solution.py:305
  145.5 16.7 %collective-permute-start.22 = (bf16[320,512]{1,0:T(8,128)(2,1)S(1)}, bf16[320,512]{1,0:T(8,128)(2,1)S(1)}, u32[]{:S(2)}, u32[]{:S(2)}) collective-permute-start(bf16[320,512]{1,0:T(8,128)(2,1)S(1)} %get-tuple-element.61), channel_id=1, source_target_pairs={{0,6},{1,7},{2,0},{3,1},{4,2},{5,3},{6,4},{7,5},{8,14},{9,15},{10,... | collective-permute-start | bytes 983048 | tf_op jit(solution)/shard_map/ppermute | solution.py:305
  147.5 25.2 %collective-permute-start.16 = (bf16[320,512]{1,0:T(8,128)(2,1)S(1)}, bf16[320,512]{1,0:T(8,128)(2,1)S(1)}, u32[]{:S(2)}, u32[]{:S(2)}) collective-permute-start(bf16[320,512]{1,0:T(8,128)(2,1)S(1)} %get-tuple-element.54), channel_id=1, source_target_pairs={{0,2},{1,3},{2,4},{3,5},{4,6},{5,7},{6,0},{7,1},{8,10},{9,11},{10,... | collective-permute-start | bytes 983048 | tf_op jit(solution)/shard_map/ppermute | solution.py:305
  149.2 23.5 %collective-permute-start.17 = (bf16[320,512]{1,0:T(8,128)(2,1)S(1)}, bf16[320,512]{1,0:T(8,128)(2,1)S(1)}, u32[]{:S(2)}, u32[]{:S(2)}) collective-permute-start(bf16[320,512]{1,0:T(8,128)(2,1)S(1)} %get-tuple-element.55), channel_id=1, source_target_pairs={{0,4},{1,5},{2,6},{3,7},{4,0},{5,1},{6,2},{7,3},{8,12},{9,13},{10,... | collective-permute-start | bytes 983048 | tf_op jit(solution)/shard_map/ppermute | solution.py:305
  159.5 15.7 %collective-permute-start.18 = (bf16[320,512]{1,0:T(8,128)(2,1)S(1)}, bf16[320,512]{1,0:T(8,128)(2,1)S(1)}, u32[]{:S(2)}, u32[]{:S(2)}) collective-permute-start(bf16[320,512]{1,0:T(8,128)(2,1)S(1)} %get-tuple-element.56), channel_id=1, source_target_pairs={{0,6},{1,7},{2,0},{3,1},{4,2},{5,3},{6,4},{7,5},{8,14},{9,15},{10,... | collective-permute-start | bytes 983048 | tf_op jit(solution)/shard_map/ppermute | solution.py:305
  (28 other events, 68.0 us)

commit v2 on v1

v2 whole, which is shorter than its diff:
```python
import functools

import jax
import jax.numpy as jnp
from jax import lax
from jax.experimental import pallas as pl
from jax.experimental.pallas import tpu as pltpu
from jax.sharding import PartitionSpec as P

HEAD_DIM = 64
SPAN = 256
MIB = 1 << 20
BIG = 56
BF16 = jnp.bfloat16
F32 = jnp.float32
HIGHEST = lax.Precision.HIGHEST

NN = (((1,), (0,)), ((), ()))
NT = (((1,), (1,)), ((), ()))
TN = (((0,), (0,)), ((), ()))


def mm(a, b, dims=NN, precision=None):
    return lax.dot_general(a, b, dims, precision=precision, preferred_element_type=F32)


def call(body, out, scratch=(), smem=(), near=(), held=(), pinned=(), count=0, work=(0, 0), limit=16):
    outs = list(out)
    n_out, n_scratch = len(outs), len(scratch)
    far = [i for i in range(count) if i not in smem and i not in held and i not in near]
    far_out = list(range(n_out)) if pinned is True else list(pinned)

    def kernel(*refs):
        ins, res = list(refs[:count]), list(refs[count : count + n_out])
        rest = refs[count + n_out :]
        own, rest = list(rest[:n_scratch]), list(rest[n_scratch:])
        copies, late = [], []
        for k, i in enumerate(far):
            copies.append(pltpu.make_async_copy(ins[i], rest[k], rest[-1].at[k]))
            ins[i] = rest[k]
        for k, i in enumerate(far_out, len(far)):
            late.append(pltpu.make_async_copy(rest[k], res[i], rest[-1].at[k]))
            res[i] = rest[k]
        for copy in copies:
            copy.start()
        if held:
            body(copies, *ins, *res, *own)
        else:
            for copy in copies:
                copy.wait()
            body(*ins, *res, *own)
        for copy in late:
            copy.start()
        for copy in late:
            copy.wait()

    def space(i):
        return pltpu.SMEM if i in smem else pltpu.VMEM if i in near else pltpu.HBM

    def run(*args):
        assert len(args) == count
        buffers = [pltpu.VMEM(args[i].shape, args[i].dtype) for i in far]
        buffers += [pltpu.VMEM(outs[i].shape, outs[i].dtype) for i in far_out]
        if buffers:
            buffers.append(pltpu.SemaphoreType.DMA((len(buffers),)))
        return pl.pallas_call(
            kernel,
            out_shape=[
                pltpu.HBM(v.shape, v.dtype) if i in far_out else v for i, v in enumerate(outs)
            ],
            in_specs=[pl.BlockSpec(memory_space=space(i)) for i in range(count)],
            out_specs=[
                pl.BlockSpec(memory_space=pltpu.HBM if i in far_out else pltpu.VMEM)
                for i in range(n_out)
            ],
            scratch_shapes=list(scratch) + buffers,
            cost_estimate=pl.CostEstimate(
                flops=work[0], bytes_accessed=work[1], transcendentals=0
            ),
            compiler_params=pltpu.CompilerParams(vmem_limit_bytes=limit * MIB),
        )(*args)

    return run


def spread(rows, width):
    head = lax.broadcasted_iota(jnp.int32, (rows, width), 0)
    lane = lax.broadcasted_iota(jnp.int32, (rows, width), 1)
    return jnp.where(lane // HEAD_DIM == head, 1.0, 0.0).astype(F32)


CUM, CUM_DOT, REM, REM_DOT, CUM_EXP = 0, 16, 32, 48, 64


def decay_body(dec, table, columns, vec, tail):
    s = lax.broadcasted_iota(jnp.int32, (SPAN, SPAN), 0)
    t = lax.broadcasted_iota(jnp.int32, (SPAN, SPAN), 1)
    upper = jnp.where(s <= t, 1.0, 0.0).astype(F32)
    lower = jnp.where(t <= s, 1.0, 0.0).astype(F32)
    ends = []
    for b in range(dec.shape[1] // SPAN):
        lanes = slice(b * SPAN, (b + 1) * SPAN)
        both = dec[:, lanes]
        c = mm(both, upper, NN, HIGHEST)
        c_t = mm(lower, both, NT, HIGHEST)
        p, d = c[:16], c[16:]
        table[CUM : CUM + 16, lanes] = p
        table[CUM_DOT : CUM_DOT + 16, lanes] = d
        table[CUM_EXP : CUM_EXP + 16, lanes] = jnp.exp(p)
        r = jnp.exp(p[:, SPAN - 1 :] - p)
        table[REM : REM + 16, lanes] = r
        table[REM_DOT : REM_DOT + 16, lanes] = r * (d[:, SPAN - 1 :] - d)
        columns[lanes, :] = c_t
        ends.append(c_t[SPAN - 1 :, :])
    rows = jnp.concatenate(
        [ends[0][:, :16], ends[0][:, 16:], ends[1][:, :16], ends[1][:, 16:]]
        + [jnp.zeros((4, 16), F32)],
        0,
    )
    wide = mm(rows, spread(16, vec.shape[1]), NN, HIGHEST)
    row = lax.broadcasted_iota(jnp.int32, wide.shape, 0)
    vec[...] = jnp.where((row == 0) | (row == 2), jnp.exp(wide), wide)
    rest = ends[0] + ends[1]
    tail[...] = jnp.zeros(tail.shape, F32)
    for i in range(3):
        term = rest.astype(BF16).astype(F32)
        tail[i : i + 1, 0:32] = term
        rest = rest - term


def edge_body(copies, first, second, out, last):
    for i, ref in enumerate((first, second)):
        pltpu.sync_copy(ref.at[:, ref.shape[1] - 128 :], last.at[i])
    row = lax.broadcasted_iota(jnp.int32, (16, 128), 0)
    lane = lax.broadcasted_iota(jnp.int32, (16, 128), 1)
    total = None
    for i in range(2):
        hit = (lane == row - 8 * i + 120) & (lane > 124) & (row >> 3 == i)
        term = mm(jnp.where(hit, 1.0, 0.0).astype(BF16), last[i], NT)
        total = term if total is None else total + term
    out[...] = total.astype(BF16)


def weight_body(w_inner, w_bmat, w_cmat, w_all):
    width, state = w_inner.shape[1], w_bmat.shape[1]
    w_all[:, :width] = w_inner[...]
    w_all[:, width : width + state] = w_bmat[...]
    w_all[:, width + state :] = w_cmat[...]


def gather(order, pieces, full, sems):
    rows = pieces[0].shape[0]
    arriving = [
        pltpu.make_async_copy(
            piece, full.at[pl.ds(pl.multiple_of(order[i] * rows, rows), rows), :], sems.at[i]
        )
        for i, piece in enumerate(pieces)
    ]
    for copy in arriving:
        copy.start()
    return arriving


def project(full, w_all, ext, halo):
    ext[0:8, :] = halo
    for b in range(full.shape[1] // SPAN):
        summed = mm(full[:, b * SPAN : (b + 1) * SPAN], w_all[...], TN)
        ext[8 + b * SPAN : 8 + (b + 1) * SPAN, :] = summed.astype(BF16).astype(F32)


CHUNK = 64


def convolve(ext, taps, b, store):
    count = taps.shape[0]
    for c in range(taps.shape[1] // 128):
        lanes = slice(c * 128, (c + 1) * 128)
        kernel = [jnp.broadcast_to(taps[k : k + 1, lanes], (CHUNK, 128)) for k in range(count)]
        for r in range(b * SPAN, (b + 1) * SPAN, CHUNK):
            summed = None
            for k in range(count):
                at = r + 9 - count + k
                term = kernel[k] * ext[at : at + CHUNK, lanes]
                summed = term if summed is None else summed + term
            store(slice(r, r + CHUNK), lanes, summed)


def turn(rows, out):
    s = lax.broadcasted_iota(jnp.int32, (SPAN, SPAN), 0)
    t = lax.broadcasted_iota(jnp.int32, (SPAN, SPAN), 1)
    one = jnp.where(s == t, 1.0, 0.0).astype(BF16)

    def block(b):
        lanes = slice(b * SPAN, (b + 1) * SPAN)
        out[:, lanes] = mm(rows[lanes, :], one, TN).astype(BF16)

    return block


def to_owners(values):
    n, width = values.shape
    halves = [values[:, : width // 2], values[:, width // 2 :]]
    stacked = jnp.stack([v.reshape(n // 8, 8, width // 2) for v in halves], 1)
    return stacked.reshape(2 * n, width // 2)


def from_owners(values):
    n, width = values.shape
    split = values.reshape(n // 16, 2, 8, width)
    return jnp.concatenate([split[:, i].reshape(n // 2, width) for i in range(2)], 1)


def primal_body(copies, order, *refs):
    pieces, (w_all, edge, taps, table, vec) = refs[:8], refs[8:13]
    mixed, gate, halo, state0, own, full, ext, rows, scaled, sems = refs[13:]
    arriving = gather(order, pieces, full, sems)
    for copy in copies:
        copy.wait()
    halo[...] = mm(edge[...], w_all[...]).astype(BF16).astype(F32)
    for copy in arriving:
        copy.wait()
    project(full, w_all, ext, halo[0:8, :])

    def store(at, lanes, v):
        sig = 1.0 / (1.0 + jnp.exp(-v))
        rows[at, lanes] = (v * sig).astype(BF16)
        gate[at, lanes] = sig * (1.0 + v * (1.0 - sig))

    block = turn(rows, mixed)
    for b in range(2):
        convolve(ext, taps, b, store)
        block(b)

    width = vec.shape[1]
    states = []
    for b in range(2):
        lanes = slice(b * SPAN, (b + 1) * SPAN)
        for h in range(width // HEAD_DIM):
            rows = slice(h * HEAD_DIM, (h + 1) * HEAD_DIM)
            value = mixed[rows, lanes].astype(F32)
            scaled[rows, :] = (value * table[REM + h : REM + h + 1, lanes]).astype(BF16)
        states.append(mm(mixed[width : width + 128, lanes], scaled[...], NT))
    state0[...] = states[0]
    own[...] = vec[2:3, :] * states[0] + states[1]


def tangent_body(copies, order, *refs):
    pieces, (w_all, halo, taps, table, vec) = refs[:8], refs[8:13]
    mixed, gate, state0, own, tail, mixed_dot, state0_dot, message = refs[13:21]
    full, ext, rows, scaled, sems = refs[21:]
    arriving = gather(order, pieces, full, sems)
    for copy in copies:
        copy.wait()
    for copy in arriving:
        copy.wait()
    project(full, w_all, ext, halo[8:16, :])

    def store(at, lanes, v):
        rows[at, lanes] = (gate[at, lanes] * v).astype(BF16)

    block = turn(rows, mixed_dot)
    for b in range(2):
        convolve(ext, taps, b, store)
        block(b)

    width = vec.shape[1]
    states = []
    for b in range(2):
        lanes = slice(b * SPAN, (b + 1) * SPAN)
        for h in range(width // HEAD_DIM):
            rows = slice(h * HEAD_DIM, (h + 1) * HEAD_DIM)
            value = mixed[rows, lanes].astype(F32)
            r = table[REM + h : REM + h + 1, lanes]
            scaled[rows, SPAN:] = (value * r).astype(BF16)
            scaled[rows, :SPAN] = (
                mixed_dot[rows, lanes].astype(F32) * r
                + value * table[REM_DOT + h : REM_DOT + h + 1, lanes]
            ).astype(BF16)
        writer = mixed[width : width + 128, lanes]
        writer_dot = mixed_dot[width : width + 128, lanes]
        states.append(mm(writer, scaled[:, :SPAN], NT) + mm(writer_dot, scaled[:, SPAN:], NT))
    state0_dot[...] = states[0]
    own_dot = vec[2:3, :] * (states[0] + vec[3:4, :] * state0[...]) + states[1]
    message[:, : width // 2] = to_owners(own[...]).astype(BF16)
    message[:, width // 2 : width] = to_owners(own_dot).astype(BF16)
    both = jnp.concatenate([tail[...], tail[...]], 0).astype(BF16)
    for j in range(message.shape[0] // 16):
        message[16 * j : 16 * j + 16, width:] = both


def within_body(mixed, mixed_dot, table, columns, gain, within, within_dot, sc, scd):
    width = within.shape[0]
    state = (mixed.shape[0] - width) // 2
    s = lax.broadcasted_iota(jnp.int32, (SPAN, SPAN), 0)
    t = lax.broadcasted_iota(jnp.int32, (SPAN, SPAN), 1)
    causal = s <= t
    for b in range(2):
        lanes = slice(b * SPAN, (b + 1) * SPAN)
        writer, reader = mixed[width : width + state, lanes], mixed[width + state :, lanes]
        writer_dot = mixed_dot[width : width + state, lanes]
        reader_dot = mixed_dot[width + state :, lanes]
        sc[...] = mm(writer, reader, TN)
        scd[...] = mm(writer_dot, reader, TN) + mm(writer, reader_dot, TN)
        for h in range(width // HEAD_DIM):
            rows = slice(h * HEAD_DIM, (h + 1) * HEAD_DIM)
            diff = table[CUM + h : CUM + h + 1, lanes] - columns[lanes, h : h + 1]
            diff_dot = (
                table[CUM_DOT + h : CUM_DOT + h + 1, lanes] - columns[lanes, 16 + h : 17 + h]
            )
            weight = jnp.exp(jnp.where(causal, diff, -jnp.inf))
            mix = (weight * sc[...]).astype(BF16)
            mix_dot = (weight * (scd[...] + diff_dot * sc[...])).astype(BF16)
            value, value_dot = mixed[rows, lanes], mixed_dot[rows, lanes]
            both = mm(jnp.concatenate([value, value_dot], 0), mix)
            other = mm(value, mix_dot)
            skip = gain[0:1, h : h + 1]
            within[rows, lanes] = both[:HEAD_DIM] + skip * value.astype(F32)
            within_dot[rows, lanes] = (both[HEAD_DIM:] + other) + skip * value_dot.astype(F32)


def unpack(half, width, which):
    lane = lax.broadcasted_iota(jnp.int32, (128, width), 0)
    head = lax.broadcasted_iota(jnp.int32, (128, width), 1) // HEAD_DIM + half * (width // HEAD_DIM)
    return jnp.where(lane == head + 16 * which, 1.0, 0.0).astype(BF16)


def scan_body(half, arrived, leaving, states, retain, slope):
    rows, whole = 8, leaving.shape[1]
    width = whole // 2
    steps = arrived.shape[0] // rows
    tails = arrived[:, whole:]
    for which, out in ((0, retain), (1, slope)):
        terms = mm(tails, unpack(half[0], width, which)).reshape(steps, rows, width)
        out[...] = (terms[:, 0] + terms[:, 1]) + terms[:, 2]
    retain[...] = jnp.exp(retain[...])
    states[...] = arrived[:, :whole].astype(F32)
    state = jnp.zeros((rows, width), F32)
    state_dot = jnp.zeros((rows, width), F32)
    for j in range(steps):
        own = slice(j * rows, (j + 1) * rows)
        arriving, arriving_dot = states[own, :width], states[own, width:]
        states[own, :width] = state
        states[own, width:] = state_dot
        r = retain[j : j + 1, :]
        state_dot = r * (state_dot + slope[j : j + 1, :] * state) + arriving_dot
        state = r * state + arriving
    leaving[...] = states[...].astype(BF16)


def arrange_body(order, w_t, keep, send):
    rows = w_t.shape[0] // order.shape[0]
    for d in range(order.shape[0] // 2):
        own = slice(d * rows, (d + 1) * rows)
        keep[own, :] = w_t[pl.ds(pl.multiple_of(order[2 * d] * rows, rows), rows), :]
        send[own, :] = w_t[pl.ds(pl.multiple_of(order[2 * d + 1] * rows, rows), rows), :]


def product_body(keep, received, own, other, *outs):
    rows = outs[0].shape[0]
    for b in range(own.shape[1] // SPAN):
        lanes = slice(b * SPAN, (b + 1) * SPAN)
        result = mm(keep[...], own[:, lanes]) + mm(received[...], other[:, lanes])
        for d, out in enumerate(outs):
            out[:, lanes] = result[d * rows : (d + 1) * rows].astype(BF16)


def read_body(arrived, reader, within, table, vec, state0, inner):
    width = within.shape[0]
    entry = from_owners(arrived[:, : width // 2].astype(F32))
    for b in range(2):
        lanes = slice(b * SPAN, (b + 1) * SPAN)
        read = mm(entry.astype(BF16), reader[:, lanes], TN)
        for h in range(width // HEAD_DIM):
            rows = slice(h * HEAD_DIM, (h + 1) * HEAD_DIM)
            e = table[CUM_EXP + h : CUM_EXP + h + 1, lanes]
            inner[rows, lanes] = (within[rows, lanes] + e * read[rows]).astype(BF16)
        if b == 0:
            entry = vec[0:1, :] * entry + state0[...]


def read_dot_body(arrived, readers, readers_dot, within, table, vec, s0, s0_dot, inner):
    width = within.shape[0]
    entry = from_owners(arrived[:, : width // 2].astype(F32))
    entry_dot = from_owners(arrived[:, width // 2 :].astype(F32))
    for b in range(2):
        lanes = slice(b * SPAN, (b + 1) * SPAN)
        reader, reader_dot = readers[:, lanes], readers_dot[:, lanes]
        rounded = entry.astype(BF16)
        read = mm(rounded, reader, TN)
        read_dot = mm(rounded, reader_dot, TN) + mm(entry_dot.astype(BF16), reader, TN)
        for h in range(width // HEAD_DIM):
            rows = slice(h * HEAD_DIM, (h + 1) * HEAD_DIM)
            e = table[CUM_EXP + h : CUM_EXP + h + 1, lanes]
            d = table[CUM_DOT + h : CUM_DOT + h + 1, lanes]
            inner[rows, lanes] = (
                within[rows, lanes] + e * (read_dot[rows] + d * read[rows])
            ).astype(BF16)
        if b == 0:
            retain, slope = vec[0:1, :], vec[1:2, :]
            entry_dot = retain * (entry_dot + slope * entry) + s0_dot[...]
            entry = retain * entry + s0[...]


def total_body(*refs):
    out = refs[-1]
    summed = refs[0][...].astype(F32)
    for ref in refs[1:-1]:
        summed = summed + ref[...].astype(F32)
    out[...] = summed.astype(BF16)


def on_device(
    tokens,
    tangent_tokens,
    log_decay,
    tangent_decay,
    w_inner,
    w_bmat,
    w_cmat,
    conv_inner,
    conv_bc,
    skip_gain,
    w_out,
):
    length, piece = tokens.shape
    model, width = w_inner.shape
    state_len = w_bmat.shape[1]
    channels = width + 2 * state_len
    heads = width // HEAD_DIM
    n_ctx, n_head = lax.axis_size("ctx"), lax.axis_size("head")
    chips = n_head // 2
    margin = conv_inner.shape[0] - 1
    shape = jax.ShapeDtypeStruct
    place = lax.axis_index("head")
    chip, core = place // 2, place % 2

    def along(values, distance):
        route = [
            (2 * i + j, 2 * ((i + distance) % chips) + j) for i in range(chips) for j in range(2)
        ]
        return lax.ppermute(values, "head", route)

    def swap(values):
        return lax.ppermute(values, "head", [(i, i ^ 1) for i in range(n_head)])

    def exchange(values):
        blocks = values.reshape(n_ctx, values.shape[0] // n_ctx, values.shape[1])
        return lax.all_to_all(blocks, "ctx", 0, 0).reshape(values.shape)

    first, second = tokens.T, tangent_tokens.T
    first_up, first_down, second_down = along(first, 1), along(first, -1), along(second, -1)
    pad = ((0, 16 - heads), (0, 0))
    dec = jnp.concatenate([jnp.pad(log_decay.T, pad), jnp.pad(tangent_decay.T, pad)], 0)
    table, columns, vec, tail = call(
        decay_body,
        [shape((80, length), F32), shape((length, 32), F32)]
        + [shape((8, width), F32), shape((8, 128), F32)],
        pinned=True,
        count=1,
        work=(10**8, 10**6),
    )(dec)
    first_up, table = lax.optimization_barrier((first_up, table))
    first_far = along(first_up, 1)
    later, first_far = lax.optimization_barrier((second, first_far))
    second_up = along(later, 1)
    second_far = along(second_down, -1)
    firsts = [first, first_up, first_down, first_far]
    seconds = [second, second_up, second_down, second_far]
    firsts = firsts + [swap(v) for v in firsts]
    seconds = seconds + [swap(v) for v in seconds]
    chip_of = [chip, chip - 1, chip + 1, chip + 2]
    order = jnp.stack(
        [(i + chips) % chips * 2 + core for i in chip_of]
        + [(i + chips) % chips * 2 + (1 - core) for i in chip_of]
    ).astype(jnp.int32)

    (edge,) = call(
        edge_body,
        [shape((16, piece), BF16)],
        [pltpu.VMEM((2, piece, 128), BF16)],
        held=(0, 1),
        count=2,
        work=(10**7, MIB // 4),
    )(first, second)
    edge = lax.ppermute(edge, "ctx", [(i, i + 1) for i in range(n_ctx - 1)])
    edge = lax.all_to_all(jnp.broadcast_to(edge[None], (n_head, *edge.shape)), "head", 0, 0)
    edge = edge.transpose(1, 0, 2).reshape(edge.shape[1], model)
    taps = jnp.concatenate([conv_inner, conv_bc], 1)
    (w_all,) = call(
        weight_body,
        [shape((model, channels), BF16)],
        near=(0, 1, 2),
        count=3,
        work=(10**6, 9 * MIB),
    )(w_inner, w_bmat, w_cmat)

    def scratch(spans):
        return [
            pltpu.VMEM((model, length), BF16),
            pltpu.VMEM((length + 8, channels), F32),
            pltpu.VMEM((length, channels), BF16),
            pltpu.VMEM((width, spans * SPAN), BF16),
            pltpu.SemaphoreType.DMA((8,)),
        ]

    work = (2 * channels * model * length, 12 * MIB)
    mix = shape((channels, length), BF16)
    state = shape((state_len, width), F32)
    mixed, gate, halo, state0, own = call(
        primal_body,
        [mix, shape((length, channels), F32), shape((16, channels), F32), state, state],
        scratch(1),
        near=(9,),
        held=tuple(range(1, 9)),
        pinned=(0, 3),
        count=14,
        smem=(0,),
        work=work,
        limit=20,
    )(order, *firsts, w_all, edge, taps, table, vec)
    mixed_dot, state0_dot, message = call(
        tangent_body,
        [mix, state, shape((2 * state_len, width + 128), BF16)],
        scratch(2),
        near=(9, 10, 15, 17),
        held=tuple(range(1, 9)),
        pinned=True,
        count=19,
        smem=(0,),
        work=work,
        limit=20,
    )(order, *seconds, w_all, halo, taps, table, vec, mixed, gate, state0, own, tail)

    arrived = exchange(message)
    gains = jnp.pad(skip_gain[None], ((0, 0), (0, 16 - heads)))
    wide = shape((width, length), F32)
    within, within_dot = call(
        within_body,
        [wide, wide],
        [pltpu.VMEM((SPAN, SPAN), F32)] * 2,
        pinned=True,
        count=5,
        work=(5 * 10**9, 8 * MIB),
        limit=BIG,
    )(mixed, mixed_dot, table, columns, gains)
    half = (lax.axis_index("ctx") % 2).astype(jnp.int32)[None]
    line = pltpu.VMEM((n_ctx, width // 2), F32)
    (leaving,) = call(
        scan_body,
        [shape((2 * state_len, width), BF16)],
        [pltpu.VMEM((2 * state_len, width), F32), line, line],
        near=(1,),
        count=2,
        smem=(0,),
        work=(10**8, MIB),
    )(half, arrived)
    entry = exchange(leaving)

    ring = [(chip + d) % chips for d in range(chips)]
    slices = jnp.stack([2 * i + j for i in ring for j in (core, 1 - core)]).astype(jnp.int32)
    side = shape((model // 2, width), BF16)
    keep, send = call(
        arrange_body, [side, side], near=(1,), count=2, smem=(0,), work=(10**6, 6 * MIB)
    )(slices, w_out.T)
    received = swap(send)
    values = shape((width, length), BF16)
    bc = width + state_len
    (inner,) = call(read_body, [values], count=6, work=(10**9, 4 * MIB), limit=BIG)(
        entry, mixed[bc:], within, table, vec, state0
    )
    inner, entry = lax.optimization_barrier((inner, entry))
    (inner_dot,) = call(read_dot_body, [values], count=8, work=(10**9, 6 * MIB), limit=BIG)(
        entry, mixed[bc:], mixed_dot[bc:], within_dot, table, vec, state0, state0_dot
    )
    term = shape((piece, length), BF16)
    product = call(
        product_body,
        [term] * chips,
        near=(0, 1, 2, 3),
        count=4,
        work=(2 * chips * piece * 2 * width * length, 6 * MIB),
    )

    def total(*terms):
        count = len(terms)
        body = call(total_body, [term], near=range(count), count=count, work=(10**6, 2 * MIB))
        return body(*terms)[0]

    def finish(values, way):
        terms = product(keep, received, values, swap(values))
        far = along(terms[2], way)
        near, back = (terms[1], terms[3]) if way == 1 else (terms[3], terms[1])
        back = along(back, -way)
        near = along(total(near, far), way)
        return total(terms[0], near, back).T

    return finish(inner, 1), finish(inner_dot, -1)


def solution(mesh):
    in_specs = (
        P("ctx", "head"),
        P("ctx", "head"),
        P("ctx", "head"),
        P("ctx", "head"),
        P(None, "head"),
        P(),
        P(),
        P(None, "head"),
        P(),
        P("head"),
        P("head", None),
    )
    out_specs = (P("ctx", "head"), P("ctx", "head"))
    return jax.shard_map(
        on_device, mesh=mesh, in_specs=in_specs, out_specs=out_specs, check_vma=False
    )
```

time: 177 us -> 154 us (0.87)
  starting transfers between devices: 49.2 us -> 40.6 us
  local copies, waits for them, and re-layouts: 36.1 us -> 27.8 us
  Pallas kernels: 36.1 us -> 42.2 us
  waiting for transfers between devices: 45.9 us -> 40.5 us
  matrix products: 3.48 us -> 0 us
  other arithmetic: 4.07 us -> 0.78 us
    unnamed x72 -> x54, local copies, waits for them, and re-layouts: 32.2 us -> 23.2 us
    all_to_all x3 -> x2, starting transfers between devices: 25 us -> 16.1 us  [exchange(): return lax.all_to_all(blocks, 'ctx', 0, 0).reshape(values.shape)]
    pallas_call x14 -> x16, Pallas kernels: 36.1 us -> 42.2 us  [run(): pl.pallas_call(kernel, out_shape=[pltpu.HBM(v.shape, v.dtype) if i in far...]
    ppermute x12, waiting for transfers between devices: 28.8 us -> 24 us  [along(): return lax.ppermute(values, 'head', route)]
    transpose x1 -> x0, other arithmetic: 3.87 us -> none  [on_device(): w_t = jnp.concatenate([w_inner, w_bmat, w_cmat], 1).T]
    dot_general x1 -> x0, matrix products: 3.48 us -> none  [on_device(): halo = jnp.dot(w_t, before.T, preferred_element_type=F32).astype(BF16)]
    all_to_all x3 -> x2, waiting for transfers between devices: 14.2 us -> 11 us  [exchange(): return lax.all_to_all(blocks, 'ctx', 0, 0).reshape(values.shape)]
    ppermute x10 -> x11, waiting for transfers between devices: 0.03 us -> 1.82 us  [swap(): return lax.ppermute(values, 'head', [(i, i ^ 1) for i in range(n_head)])]
  transfers between devices with their start and end apart: 27 -> 27, of which waited for: 8 -> 12; matrix products, arithmetic and copies ran while one was open for 14% -> 6% of each run, Pallas kernels for 15% -> 22%
where the time goes in v2:
time: 154 us; the launch traced here: 153 us
  Pallas kernels  42.2 us (27%)
  starting transfers between devices  40.6 us (26%)
  waiting for transfers between devices  40.5 us (26%)
  local copies, waits for them, and re-layouts  27.8 us (18%)
    pallas_call x16, Pallas kernels, run(): pl.pallas_call(kernel, out_shape=[pltpu.HBM(v.shape, v.dtype) if i in far...  42.2 us
    ppermute x12, waiting for transfers between devices, along(): return lax.ppermute(values, 'head', route)  24 us
    unnamed x54, local copies, waits for them, and re-layouts  23.2 us
    all_to_all x2, starting transfers between devices, exchange(): return lax.all_to_all(blocks, 'ctx', 0, 0).reshape(values.shape)  16.1 us
    ppermute x12, starting transfers between devices, along(): return lax.ppermute(values, 'head', route)  15.1 us
    all_to_all x2, waiting for transfers between devices, exchange(): return lax.all_to_all(blocks, 'ctx', 0, 0).reshape(values.shape)  11 us
    ppermute x1, starting transfers between devices, on_device(): edge = lax.ppermute(edge, 'ctx', [(i, i + 1) for i in range(n_ctx - 1)])  3.85 us
    all_to_all x1, waiting for transfers between devices, on_device(): lax.all_to_all(jnp.broadcast_to(edge[None], (n_head, *edge.shape)), 'head...  3.69 us
  transfers between devices with their start and end apart: 27, of which 12 were waited for; matrix products, arithmetic and copies ran while one was open for 6% of the time, Pallas kernels for 22%

profile of v2, /device:TPU:32, one launch (start us, length us, event | category | flops | bytes accessed | tf_op | source)
XLA Modules:
  0.0 153.0 jit_solution(13646903185852179809)
XLA Ops:
  2.2 1.7 %collective-permute-start.10 = (bf16[320,512]{1,0:T(8,128)(2,1)}, bf16[320,512]{1,0:T(8,128)(2,1)S(1)}, u32[]{:S(2)}, u32[]{:S(2)}) collective-permute-start(bf16[320,512]{1,0:T(8,128)(2,1)} %bitcast.30), channel_id=1, source_target_pairs={{0,6},{1,7},{2,0},{3,1},{4,2},{5,3},{6,4},{7,5},{8,14},{9,15},{10,... | collective-permute-start | bytes 983048 | tf_op jit(solution)/shard_map/ppermute | solution.py:441
  6.3 1.8 %shard_map.123 = (f32[80,512]{1,0:T(8,128)}, f32[512,32]{1,0:T(8,128)}, f32[8,640]{1,0:T(8,128)}, f32[8,128]{1,0:T(8,128)}) custom-call(f32[32,512]{1,0:T(8,128)S(1)} %select_maximum_fusion.refs_0_), custom_call_target="tpu_custom_call" | custom-call | flops 100000000 | bytes 1000000 | tf_op jit(solution)/shard_map/pallas_call | solution.py:66
  8.1 3.5 %collective-permute-done.1.refs_2_ = bf16[320,512]{1,0:T(8,128)(2,1)S(1)} collective-permute-done((bf16[320,512]{1,0:T(8,128)(2,1)}, bf16[320,512]{1,0:T(8,128)(2,1)S(1)}, u32[]{:S(2)}, u32[]{:S(2)}) %collective-permute-start.1) | collective-permute-done | bytes 327712 | tf_op jit(solution)/shard_map/ppermute | solution.py:441
  13.9 3.8 %collective-permute-start.15 = (bf16[16,320]{1,0:T(8,128)(2,1)S(1)}, bf16[16,320]{1,0:T(8,128)(2,1)S(1)}, u32[]{:S(2)}, u32[]{:S(2)}) collective-permute-start(bf16[16,320]{1,0:T(8,128)(2,1)S(1)} %shard_map.125), channel_id=1, source_target_pairs={{0,8},{8,16},{16,24},{24,32},{32,40},{40,48},{48,56},{56,64},{64,7... | collective-permute-start | bytes 30728 | tf_op jit(solution)/shard_map/ppermute | solution.py:485
  18.6 2.9 %collective-permute-done.2.refs_4_ = bf16[320,512]{1,0:T(8,128)(2,1)} collective-permute-done((bf16[320,512]{1,0:T(8,128)(2,1)S(1)}, bf16[320,512]{1,0:T(8,128)(2,1)}, u32[]{:S(2)}, u32[]{:S(2)}) %collective-permute-start.2) | collective-permute-done | bytes 327712 | tf_op jit(solution)/shard_map/ppermute | solution.py:441
  21.8 1.7 %collective-permute-start.3 = (bf16[320,512]{1,0:T(8,128)(2,1)}, bf16[320,512]{1,0:T(8,128)(2,1)S(1)}, u32[]{:S(2)}, u32[]{:S(2)}) collective-permute-start(bf16[320,512]{1,0:T(8,128)(2,1)} %bitcast.16.refs_1_), channel_id=1, source_target_pairs={{0,2},{1,3},{2,4},{3,5},{4,6},{5,7},{6,0},{7,1},{8,10},{9,11},{10,... | collective-permute-start | bytes 983048 | tf_op jit(solution)/shard_map/ppermute | solution.py:441
  24.3 1.9 %copy-done.2 = bf16[2560,640]{1,0:T(8,128)(2,1)S(1)} copy-done((bf16[2560,640]{1,0:T(8,128)(2,1)S(1)}, bf16[2560,640]{1,0:T(8,128)(2,1)}, u32[]{:S(2)}) %copy-start.2) | copy-done | bytes 3276824
  29.0 2.1 %copy-done = bf16[2560,896]{1,0:T(8,128)(2,1)} copy-done((bf16[2560,896]{1,0:T(8,128)(2,1)}, bf16[2560,896]{1,0:T(8,128)(2,1)S(1)}, u32[]{:S(2)}) %copy-start) | copy-done | bytes 4587544
  31.7 3.4 %all-to-all-start = ((bf16[8,16,320]{2,1,0:T(8,128)(2,1)}), bf16[8,16,320]{2,1,0:T(8,128)(2,1)S(1)}, u32[]{:S(2)}, u32[]{:S(2)}) async-start(bf16[8,16,320]{2,1,0:T(8,128)(2,1)} %broadcast_in_dim.13), calls=%async_computation | async-start | bytes 196608 | tf_op jit(solution)/shard_map/all_to_all | solution.py:486
  37.1 3.7 %all-to-all-done = bf16[8,16,320]{2,1,0:T(8,128)(2,1)S(1)} async-done(((bf16[8,16,320]{2,1,0:T(8,128)(2,1)}), bf16[8,16,320]{2,1,0:T(8,128)(2,1)S(1)}, u32[]{:S(2)}, u32[]{:S(2)}) %all-to-all-start) | async-done | bytes 81952 | tf_op jit(solution)/shard_map/all_to_all | solution.py:486
  41.0 2.3 %copy-done.1 = bf16[2560,896]{1,0:T(8,128)(2,1)S(1)} copy-done((bf16[2560,896]{1,0:T(8,128)(2,1)S(1)}, bf16[2560,896]{1,0:T(8,128)(2,1)}, u32[]{:S(2)}) %copy-start.1) | copy-done | bytes 4587544
  46.2 8.4 %shard_map.126 = (bf16[896,512]{1,0:T(8,128)(2,1)}, f32[512,896]{1,0:T(8,128)S(1)}, f32[16,896]{1,0:T(8,128)S(1)}, f32[128,640]{1,0:T(8,128)}, f32[128,640]{1,0:T(8,128)S(1)}) custom-call(s32[8]{0:T(128)S(1)} %stack.65.refs_0_, bf16[320,512]{1,0:T(8,128)(2,1)S(1)} %bitcast.33, bf16[320,512]{1,0:T(8,128)(2,1)S(1)} %collective-permute-done.1.refs_2_, ...), custom_call_target="tpu_custom_call" | custom-call | flops 2348810240 | bytes 12582912 | tf_op jit(solution)/shard_map/pallas_call | solution.py:66
  56.8 7.6 %shard_map.127 = (bf16[896,512]{1,0:T(8,128)(2,1)}, f32[128,640]{1,0:T(8,128)}, bf16[256,768]{1,0:T(8,128)(2,1)}) custom-call(s32[8]{0:T(128)S(1)} %stack.65.refs_0_, bf16[320,512]{1,0:T(8,128)(2,1)} %bitcast.16.refs_1_, bf16[320,512]{1,0:T(8,128)(2,1)S(1)} %collective-permute-done.3.refs_2_, bf16[320,512]{1,0:T(8,128)(2,1)S(1)} %collective-permute-done.4.refs_3_, ...), custom_call_target="tpu_custom_call" | custom-call | flops 2348810240 | bytes 12582912 | tf_op jit(solution)/shard_map/pallas_call | solution.py:66
  64.5 11.4 %all-to-all-start.1 = ((bf16[32,8,768]{2,1,0:T(8,128)(2,1)}), bf16[32,8,768]{2,1,0:T(8,128)(2,1)}, u32[]{:S(2)}, u32[]{:S(2)}) async-start(bf16[32,8,768]{2,1,0:T(8,128)(2,1)} %bitcast.34), calls=%async_computation.1 | async-start | bytes 786432 | tf_op jit(solution)/shard_map/all_to_all | solution.py:448
  76.0 4.2 %copy.14 = bf16[640,2560]{0,1:T(8,128)(2,1)S(1)} copy(bf16[640,2560]{1,0:T(8,128)(2,1)} %param.21) | data formatting | bytes 6553600 | tf_op args[10]
  80.3 2.0 %shard_map.122 = (bf16[1280,640]{1,0:T(8,128)(2,1)S(1)}, bf16[1280,640]{1,0:T(8,128)(2,1)}) custom-call(s32[8]{0:T(128)S(1)} %stack.58.refs_0_, bf16[2560,640]{1,0:T(8,128)(2,1)S(1)} %bitcast.28), custom_call_target="tpu_custom_call" | custom-call | flops 1000000 | bytes 6291456 | tf_op jit(solution)/shard_map/pallas_call | solution.py:66
  83.4 7.3 %all-to-all-done.1 = bf16[32,8,768]{2,1,0:T(8,128)(2,1)} async-done(((bf16[32,8,768]{2,1,0:T(8,128)(2,1)}), bf16[32,8,768]{2,1,0:T(8,128)(2,1)}, u32[]{:S(2)}, u32[]{:S(2)}) %all-to-all-start.1) | async-done | bytes 393248 | tf_op jit(solution)/shard_map/all_to_all | solution.py:448
  90.8 2.3 %shard_map.128 = bf16[256,640]{1,0:T(8,128)(2,1)} custom-call(s32[1]{0:T(128)} %bitcast.9.refs_0_, bf16[256,768]{1,0:T(8,128)(2,1)} %bitcast.22.refs_1_), custom_call_target="tpu_custom_call" | custom-call | flops 100000000 | bytes 1048576 | tf_op jit(solution)/shard_map/pallas_call | solution.py:66
  93.1 4.7 %all-to-all-start.2 = ((bf16[32,8,640]{2,1,0:T(8,128)(2,1)}), bf16[32,8,640]{2,1,0:T(8,128)(2,1)S(1)}, u32[]{:S(2)}, u32[]{:S(2)}) async-start(bf16[32,8,640]{2,1,0:T(8,128)(2,1)} %bitcast.23), calls=%async_computation.2 | async-start | bytes 655360 | tf_op jit(solution)/shard_map/all_to_all | solution.py:448
  101.5 5.7 %shard_map.129 = (f32[640,512]{1,0:T(8,128)}, f32[640,512]{1,0:T(8,128)}) custom-call(bf16[896,512]{1,0:T(8,128)(2,1)} %get-tuple-element.41.refs_14_.refs_0_, bf16[896,512]{1,0:T(8,128)(2,1)} %get-tuple-element.47.refs_1_, f32[80,512]{1,0:T(8,128)} %get-tuple-element.38.refs_12_.refs_2_.refs_3_.refs_4_, f32[512,32]{1,0:T(8,128)} %get-tuple-element.48.refs_3_, ...), custom_call_target="tpu_custom_call" | custom-call | flops 5000000000 | bytes 8388608 | tf_op jit(solution)/shard_map/pallas_call | solution.py:66
  107.1 3.7 %all-to-all-done.2 = bf16[32,8,640]{2,1,0:T(8,128)(2,1)S(1)} async-done(((bf16[32,8,640]{2,1,0:T(8,128)(2,1)}), bf16[32,8,640]{2,1,0:T(8,128)(2,1)S(1)}, u32[]{:S(2)}, u32[]{:S(2)}) %all-to-all-start.2) | async-done | bytes 327712 | tf_op jit(solution)/shard_map/all_to_all | solution.py:448
  111.5 2.9 %shard_map.130.refs_2_ = bf16[640,512]{1,0:T(8,128)(2,1)} custom-call(bf16[256,640]{1,0:T(8,128)(2,1)} %bitcast.38, bf16[128,512]{1,0:T(8,128)(2,1)} %slice.7.refs_1_, f32[640,512]{1,0:T(8,128)} %get-tuple-element.49.refs_2_, f32[80,512]{1,0:T(8,128)} %get-tuple-element.38.refs_12_.refs_2_.refs_3_.refs_4_, ...), custom_call_target="tpu_custom_call" | custom-call | flops 1000000000 | bytes 4194304 | tf_op jit(solution)/shard_map/pallas_call | solution.py:66
  114.5 3.8 %shard_map.134.refs_2_ = bf16[640,512]{1,0:T(8,128)(2,1)} custom-call(bf16[256,640]{1,0:T(8,128)(2,1)} %bitcast.39, bf16[128,512]{1,0:T(8,128)(2,1)} %slice.7.refs_1_, bf16[128,512]{1,0:T(8,128)(2,1)} %slice.8.refs_2_, f32[640,512]{1,0:T(8,128)} %get-tuple-element.56.refs_3_, f32[80,512]{1,0:T(8,128)} %get-tuple-element.38.refs_12_.refs_2_.refs_3_.refs_4_, ...), custom_call_target="tpu_custom_call" | custom-call | flops 1000000000 | bytes 6291456 | tf_op jit(solution)/shard_map/pallas_call | solution.py:66
  118.9 1.8 %collective-permute-done.20.refs_3_ = bf16[640,512]{1,0:T(8,128)(2,1)S(1)} collective-permute-done((bf16[640,512]{1,0:T(8,128)(2,1)}, bf16[640,512]{1,0:T(8,128)(2,1)S(1)}, u32[]{:S(2)}, u32[]{:S(2)}) %collective-permute-start.20) | collective-permute-done | bytes 655392 | tf_op jit(solution)/shard_map/ppermute | solution.py:444
  121.8 2.2 %shard_map.135 = (bf16[320,512]{1,0:T(8,128)(2,1)S(1)}, bf16[320,512]{1,0:T(8,128)(2,1)S(1)}, bf16[320,512]{1,0:T(8,128)(2,1)S(1)}, bf16[320,512]{1,0:T(8,128)(2,1)S(1)}) custom-call(bf16[1280,640]{1,0:T(8,128)(2,1)S(1)} %copy-done.13, bf16[1280,640]{1,0:T(8,128)(2,1)S(1)} %collective-permute-done.refs_1_, bf16[640,512]{1,0:T(8,128)(2,1)S(1)} %copy-done.15, ...), custom_call_target="tpu_custom_call" | custom-call | flops 1677721600 | bytes 6291456 | tf_op jit(solution)/shard_map/pallas_call | solution.py:66
  125.2 2.2 %shard_map.131 = (bf16[320,512]{1,0:T(8,128)(2,1)S(1)}, bf16[320,512]{1,0:T(8,128)(2,1)S(1)}, bf16[320,512]{1,0:T(8,128)(2,1)S(1)}, bf16[320,512]{1,0:T(8,128)(2,1)S(1)}) custom-call(bf16[1280,640]{1,0:T(8,128)(2,1)S(1)} %copy-done.13, bf16[1280,640]{1,0:T(8,128)(2,1)S(1)} %collective-permute-done.refs_1_, bf16[640,512]{1,0:T(8,128)(2,1)S(1)} %copy-done.14, ...), custom_call_target="tpu_custom_call" | custom-call | flops 1677721600 | bytes 6291456 | tf_op jit(solution)/shard_map/pallas_call | solution.py:66
  128.9 2.7 %collective-permute-start.19 = (bf16[320,512]{1,0:T(8,128)(2,1)S(1)}, bf16[320,512]{1,0:T(8,128)(2,1)S(1)}, u32[]{:S(2)}, u32[]{:S(2)}) collective-permute-start(bf16[320,512]{1,0:T(8,128)(2,1)S(1)} %get-tuple-element.54), channel_id=1, source_target_pairs={{0,6},{1,7},{2,0},{3,1},{4,2},{5,3},{6,4},{7,5},{8,14},{9,15},{10,... | collective-permute-start | bytes 983048 | tf_op jit(solution)/shard_map/ppermute | solution.py:441
  131.6 3.0 %collective-permute-done.21.refs_1_ = bf16[320,512]{1,0:T(8,128)(2,1)S(1)} collective-permute-done((bf16[320,512]{1,0:T(8,128)(2,1)S(1)}, bf16[320,512]{1,0:T(8,128)(2,1)S(1)}, u32[]{:S(2)}, u32[]{:S(2)}) %collective-permute-start.21) | collective-permute-done | bytes 327712 | tf_op jit(solution)/shard_map/ppermute | solution.py:441
  134.7 2.4 %collective-permute-start.22 = (bf16[320,512]{1,0:T(8,128)(2,1)S(1)}, bf16[320,512]{1,0:T(8,128)(2,1)S(1)}, u32[]{:S(2)}, u32[]{:S(2)}) collective-permute-start(bf16[320,512]{1,0:T(8,128)(2,1)S(1)} %shard_map.136), channel_id=1, source_target_pairs={{0,6},{1,7},{2,0},{3,1},{4,2},{5,3},{6,4},{7,5},{8,14},{9,15},{10,... | collective-permute-start | bytes 983048 | tf_op jit(solution)/shard_map/ppermute | solution.py:441
  137.1 2.2 %collective-permute-done.17.refs_1_ = bf16[320,512]{1,0:T(8,128)(2,1)S(1)} collective-permute-done((bf16[320,512]{1,0:T(8,128)(2,1)S(1)}, bf16[320,512]{1,0:T(8,128)(2,1)S(1)}, u32[]{:S(2)}, u32[]{:S(2)}) %collective-permute-start.17) | collective-permute-done | bytes 327712 | tf_op jit(solution)/shard_map/ppermute | solution.py:441
  139.4 6.9 %collective-permute-done.23.refs_2_ = bf16[320,512]{1,0:T(8,128)(2,1)S(1)} collective-permute-done((bf16[320,512]{1,0:T(8,128)(2,1)S(1)}, bf16[320,512]{1,0:T(8,128)(2,1)S(1)}, u32[]{:S(2)}, u32[]{:S(2)}) %collective-permute-start.23) | collective-permute-done | bytes 327712 | tf_op jit(solution)/shard_map/ppermute | solution.py:441
  148.7 3.5 %collective-permute-done.18.refs_1_ = bf16[320,512]{1,0:T(8,128)(2,1)S(1)} collective-permute-done((bf16[320,512]{1,0:T(8,128)(2,1)S(1)}, bf16[320,512]{1,0:T(8,128)(2,1)S(1)}, u32[]{:S(2)}, u32[]{:S(2)}) %collective-permute-start.18) | collective-permute-done | bytes 327712 | tf_op jit(solution)/shard_map/ppermute | solution.py:441
  (102 shorter events, 32.3 us)
Async XLA Ops:
  0.6 10.9 %collective-permute-start.1 = (bf16[320,512]{1,0:T(8,128)(2,1)}, bf16[320,512]{1,0:T(8,128)(2,1)S(1)}, u32[]{:S(2)}, u32[]{:S(2)}) collective-permute-start(bf16[320,512]{1,0:T(8,128)(2,1)} %bitcast.29), channel_id=1, source_target_pairs={{0,2},{1,3},{2,4},{3,5},{4,6},{5,7},{6,0},{7,1},{8,10},{9,11},{10,... | collective-permute-start | bytes 983048 | tf_op jit(solution)/shard_map/ppermute | solution.py:441
  2.2 15.5 %collective-permute-start.10 = (bf16[320,512]{1,0:T(8,128)(2,1)}, bf16[320,512]{1,0:T(8,128)(2,1)S(1)}, u32[]{:S(2)}, u32[]{:S(2)}) collective-permute-start(bf16[320,512]{1,0:T(8,128)(2,1)} %bitcast.30), channel_id=1, source_target_pairs={{0,6},{1,7},{2,0},{3,1},{4,2},{5,3},{6,4},{7,5},{8,14},{9,15},{10,... | collective-permute-start | bytes 983048 | tf_op jit(solution)/shard_map/ppermute | solution.py:441
  3.9 14.7 %collective-permute-start.4 = (bf16[320,512]{1,0:T(8,128)(2,1)}, bf16[320,512]{1,0:T(8,128)(2,1)S(1)}, u32[]{:S(2)}, u32[]{:S(2)}) collective-permute-start(bf16[320,512]{1,0:T(8,128)(2,1)} %bitcast.16.refs_1_), channel_id=1, source_target_pairs={{0,6},{1,7},{2,0},{3,1},{4,2},{5,3},{6,4},{7,5},{8,14},{9,15},{10,... | collective-permute-start | bytes 983048 | tf_op jit(solution)/shard_map/ppermute | solution.py:441
  11.6 9.9 %collective-permute-start.2 = (bf16[320,512]{1,0:T(8,128)(2,1)S(1)}, bf16[320,512]{1,0:T(8,128)(2,1)}, u32[]{:S(2)}, u32[]{:S(2)}) collective-permute-start(bf16[320,512]{1,0:T(8,128)(2,1)S(1)} %collective-permute-done.1.refs_2_), channel_id=1, source_target_pairs={{0,2},{1,3},{2,4},{3,5},{4,6},{5,7},{6,0},{7,1},{8,10},{9,11},{10,... | collective-permute-start | bytes 983048 | tf_op jit(solution)/shard_map/ppermute | solution.py:441
  11.9 11.6 %collective-permute-start.11 = (bf16[320,512]{1,0:T(8,128)(2,1)}, bf16[320,512]{1,0:T(8,128)(2,1)S(1)}, u32[]{:S(2)}, u32[]{:S(2)}) collective-permute-start(bf16[320,512]{1,0:T(8,128)(2,1)} %bitcast.31), channel_id=1, source_target_pairs={{0,1},{1,0},{2,3},{3,2},{4,5},{5,4},{6,7},{7,6},{8,9},{9,8},{10,11... | collective-permute-start | bytes 983048 | tf_op jit(solution)/shard_map/ppermute | solution.py:444
  13.9 7.9 %collective-permute-start.15 = (bf16[16,320]{1,0:T(8,128)(2,1)S(1)}, bf16[16,320]{1,0:T(8,128)(2,1)S(1)}, u32[]{:S(2)}, u32[]{:S(2)}) collective-permute-start(bf16[16,320]{1,0:T(8,128)(2,1)S(1)} %shard_map.125), channel_id=1, source_target_pairs={{0,8},{8,16},{16,24},{24,32},{32,40},{40,48},{48,56},{56,64},{64,7... | collective-permute-start | bytes 30728 | tf_op jit(solution)/shard_map/ppermute | solution.py:485
  17.8 11.2 %copy-start.16 = (bf16[320,512]{1,0:T(8,128)(2,1)}, bf16[320,512]{1,0:T(8,128)(2,1)S(1)}, u32[]{:S(2)}) copy-start(bf16[320,512]{1,0:T(8,128)(2,1)S(1)} %collective-permute-done.10.refs_3_) | copy-start | bytes 983044
  17.8 17.3 %collective-permute-start.12 = (bf16[320,512]{1,0:T(8,128)(2,1)S(1)}, bf16[320,512]{1,0:T(8,128)(2,1)S(1)}, u32[]{:S(2)}, u32[]{:S(2)}) collective-permute-start(bf16[320,512]{1,0:T(8,128)(2,1)S(1)} %collective-permute-done.1.refs_2_), channel_id=1, source_target_pairs={{0,1},{1,0},{2,3},{3,2},{4,5},{5,4},{6,7},{7,6},{8,9},{9,8},{10,11... | collective-permute-start | bytes 983048 | tf_op jit(solution)/shard_map/ppermute | solution.py:444
  18.6 17.7 %collective-permute-start.13 = (bf16[320,512]{1,0:T(8,128)(2,1)S(1)}, bf16[320,512]{1,0:T(8,128)(2,1)}, u32[]{:S(2)}, u32[]{:S(2)}) collective-permute-start(bf16[320,512]{1,0:T(8,128)(2,1)S(1)} %collective-permute-done.10.refs_3_), channel_id=1, source_target_pairs={{0,1},{1,0},{2,3},{3,2},{4,5},{5,4},{6,7},{7,6},{8,9},{9,8},{10,11... | collective-permute-start | bytes 983048 | tf_op jit(solution)/shard_map/ppermute | solution.py:444
  21.5 14.9 %collective-permute-start.5 = (bf16[320,512]{1,0:T(8,128)(2,1)S(1)}, bf16[320,512]{1,0:T(8,128)(2,1)S(1)}, u32[]{:S(2)}, u32[]{:S(2)}) collective-permute-start(bf16[320,512]{1,0:T(8,128)(2,1)S(1)} %collective-permute-done.4.refs_3_), channel_id=1, source_target_pairs={{0,6},{1,7},{2,0},{3,1},{4,2},{5,3},{6,4},{7,5},{8,14},{9,15},{10,... | collective-permute-start | bytes 983048 | tf_op jit(solution)/shard_map/ppermute | solution.py:441
  21.8 15.0 %collective-permute-start.3 = (bf16[320,512]{1,0:T(8,128)(2,1)}, bf16[320,512]{1,0:T(8,128)(2,1)S(1)}, u32[]{:S(2)}, u32[]{:S(2)}) collective-permute-start(bf16[320,512]{1,0:T(8,128)(2,1)} %bitcast.16.refs_1_), channel_id=1, source_target_pairs={{0,2},{1,3},{2,4},{3,5},{4,6},{5,7},{6,0},{7,1},{8,10},{9,11},{10,... | collective-permute-start | bytes 983048 | tf_op jit(solution)/shard_map/ppermute | solution.py:441
  24.2 16.7 %collective-permute-start.14 = (bf16[320,512]{1,0:T(8,128)(2,1)}, bf16[320,512]{1,0:T(8,128)(2,1)}, u32[]{:S(2)}, u32[]{:S(2)}) collective-permute-start(bf16[320,512]{1,0:T(8,128)(2,1)} %collective-permute-done.2.refs_4_), channel_id=1, source_target_pairs={{0,1},{1,0},{2,3},{3,2},{4,5},{5,4},{6,7},{7,6},{8,9},{9,8},{10,11... | collective-permute-start | bytes 983048 | tf_op jit(solution)/shard_map/ppermute | solution.py:444
  28.4 12.5 %copy-start.8 = (bf16[512,320]{0,1:T(8,128)(2,1)S(1)}, bf16[512,320]{0,1:T(8,128)(2,1)}, u32[]{:S(2)}) copy-start(bf16[512,320]{0,1:T(8,128)(2,1)} %param.11) | copy-start | bytes 983044
  28.4 12.6 %copy-start.9 = (f32[80,512]{1,0:T(8,128)S(1)}, f32[80,512]{1,0:T(8,128)}, u32[]{:S(2)}) copy-start(f32[80,512]{1,0:T(8,128)} %get-tuple-element.38.refs_12_.refs_2_.refs_3_.refs_4_) | copy-start | bytes 491524
  28.4 12.6 %copy-start.10 = (f32[8,640]{1,0:T(8,128)S(1)}, f32[8,640]{1,0:T(8,128)}, u32[]{:S(2)}) copy-start(f32[8,640]{1,0:T(8,128)} %get-tuple-element.39.refs_13_.refs_4_.refs_5_) | copy-start | bytes 61444
  31.7 9.1 %all-to-all-start = ((bf16[8,16,320]{2,1,0:T(8,128)(2,1)}), bf16[8,16,320]{2,1,0:T(8,128)(2,1)S(1)}, u32[]{:S(2)}, u32[]{:S(2)}) async-start(bf16[8,16,320]{2,1,0:T(8,128)(2,1)} %broadcast_in_dim.13), calls=%async_computation | async-start | bytes 196608 | tf_op jit(solution)/shard_map/all_to_all | solution.py:486
  35.9 18.8 %collective-permute-start.6 = (bf16[320,512]{1,0:T(8,128)(2,1)}, bf16[320,512]{1,0:T(8,128)(2,1)S(1)}, u32[]{:S(2)}, u32[]{:S(2)}) collective-permute-start(bf16[320,512]{1,0:T(8,128)(2,1)} %bitcast.16.refs_1_), channel_id=1, source_target_pairs={{0,1},{1,0},{2,3},{3,2},{4,5},{5,4},{6,7},{7,6},{8,9},{9,8},{10,11... | collective-permute-start | bytes 983048 | tf_op jit(solution)/shard_map/ppermute | solution.py:444
  36.3 18.3 %collective-permute-start.8 = (bf16[320,512]{1,0:T(8,128)(2,1)S(1)}, bf16[320,512]{1,0:T(8,128)(2,1)S(1)}, u32[]{:S(2)}, u32[]{:S(2)}) collective-permute-start(bf16[320,512]{1,0:T(8,128)(2,1)S(1)} %collective-permute-done.4.refs_3_), channel_id=1, source_target_pairs={{0,1},{1,0},{2,3},{3,2},{4,5},{5,4},{6,7},{7,6},{8,9},{9,8},{10,11... | collective-permute-start | bytes 983048 | tf_op jit(solution)/shard_map/ppermute | solution.py:444
  36.4 18.3 %collective-permute-start.9 = (bf16[320,512]{1,0:T(8,128)(2,1)S(1)}, bf16[320,512]{1,0:T(8,128)(2,1)S(1)}, u32[]{:S(2)}, u32[]{:S(2)}) collective-permute-start(bf16[320,512]{1,0:T(8,128)(2,1)S(1)} %collective-permute-done.5.refs_4_), channel_id=1, source_target_pairs={{0,1},{1,0},{2,3},{3,2},{4,5},{5,4},{6,7},{7,6},{8,9},{9,8},{10,11... | collective-permute-start | bytes 983048 | tf_op jit(solution)/shard_map/ppermute | solution.py:444
  36.8 17.8 %collective-permute-start.7 = (bf16[320,512]{1,0:T(8,128)(2,1)S(1)}, bf16[320,512]{1,0:T(8,128)(2,1)S(1)}, u32[]{:S(2)}, u32[]{:S(2)}) collective-permute-start(bf16[320,512]{1,0:T(8,128)(2,1)S(1)} %collective-permute-done.3.refs_2_), channel_id=1, source_target_pairs={{0,1},{1,0},{2,3},{3,2},{4,5},{5,4},{6,7},{7,6},{8,9},{9,8},{10,11... | collective-permute-start | bytes 983048 | tf_op jit(solution)/shard_map/ppermute | solution.py:444
  64.5 26.3 %all-to-all-start.1 = ((bf16[32,8,768]{2,1,0:T(8,128)(2,1)}), bf16[32,8,768]{2,1,0:T(8,128)(2,1)}, u32[]{:S(2)}, u32[]{:S(2)}) async-start(bf16[32,8,768]{2,1,0:T(8,128)(2,1)} %bitcast.34), calls=%async_computation.1 | async-start | bytes 786432 | tf_op jit(solution)/shard_map/all_to_all | solution.py:448
  80.3 17.5 %copy-start.25 = (f32[10]{0:T(128)S(1)}, f32[10]{0:T(128)}, u32[]{:S(2)}) copy-start(f32[10]{0:T(128)} %param.20) | copy-start | bytes 124
  83.4 35.4 %collective-permute-start = (bf16[1280,640]{1,0:T(8,128)(2,1)}, bf16[1280,640]{1,0:T(8,128)(2,1)S(1)}, u32[]{:S(2)}, u32[]{:S(2)}) collective-permute-start(bf16[1280,640]{1,0:T(8,128)(2,1)} %get-tuple-element.33), channel_id=1, source_target_pairs={{0,1},{1,0},{2,3},{3,2},{4,5},{5,4},{6,7},{7,6},{8,9},{9,8},{10,11... | collective-permute-start | bytes 4915208 | tf_op jit(solution)/shard_map/ppermute | solution.py:444
  93.1 17.8 %all-to-all-start.2 = ((bf16[32,8,640]{2,1,0:T(8,128)(2,1)}), bf16[32,8,640]{2,1,0:T(8,128)(2,1)S(1)}, u32[]{:S(2)}, u32[]{:S(2)}) async-start(bf16[32,8,640]{2,1,0:T(8,128)(2,1)} %bitcast.23), calls=%async_computation.2 | async-start | bytes 655360 | tf_op jit(solution)/shard_map/all_to_all | solution.py:448
  118.3 2.4 %collective-permute-start.20 = (bf16[640,512]{1,0:T(8,128)(2,1)}, bf16[640,512]{1,0:T(8,128)(2,1)S(1)}, u32[]{:S(2)}, u32[]{:S(2)}) collective-permute-start(bf16[640,512]{1,0:T(8,128)(2,1)} %shard_map.134.refs_2_), channel_id=1, source_target_pairs={{0,1},{1,0},{2,3},{3,2},{4,5},{5,4},{6,7},{7,6},{8,9},{9,8},{10,11... | collective-permute-start | bytes 1966088 | tf_op jit(solution)/shard_map/ppermute | solution.py:444
  118.4 6.8 %collective-permute-start.16 = (bf16[640,512]{1,0:T(8,128)(2,1)S(1)}, bf16[640,512]{1,0:T(8,128)(2,1)S(1)}, u32[]{:S(2)}, u32[]{:S(2)}) collective-permute-start(bf16[640,512]{1,0:T(8,128)(2,1)S(1)} %copy-done.14), channel_id=1, source_target_pairs={{0,1},{1,0},{2,3},{3,2},{4,5},{5,4},{6,7},{7,6},{8,9},{9,8},{10,11... | collective-permute-start | bytes 1966088 | tf_op jit(solution)/shard_map/ppermute | solution.py:444
  124.0 10.6 %collective-permute-start.21 = (bf16[320,512]{1,0:T(8,128)(2,1)S(1)}, bf16[320,512]{1,0:T(8,128)(2,1)S(1)}, u32[]{:S(2)}, u32[]{:S(2)}) collective-permute-start(bf16[320,512]{1,0:T(8,128)(2,1)S(1)} %get-tuple-element.60), channel_id=1, source_target_pairs={{0,6},{1,7},{2,0},{3,1},{4,2},{5,3},{6,4},{7,5},{8,14},{9,15},{10,... | collective-permute-start | bytes 983048 | tf_op jit(solution)/shard_map/ppermute | solution.py:441
  127.4 11.9 %collective-permute-start.17 = (bf16[320,512]{1,0:T(8,128)(2,1)S(1)}, bf16[320,512]{1,0:T(8,128)(2,1)S(1)}, u32[]{:S(2)}, u32[]{:S(2)}) collective-permute-start(bf16[320,512]{1,0:T(8,128)(2,1)S(1)} %get-tuple-element.53), channel_id=1, source_target_pairs={{0,2},{1,3},{2,4},{3,5},{4,6},{5,7},{6,0},{7,1},{8,10},{9,11},{10,... | collective-permute-start | bytes 983048 | tf_op jit(solution)/shard_map/ppermute | solution.py:441
  128.4 17.9 %collective-permute-start.23 = (bf16[320,512]{1,0:T(8,128)(2,1)S(1)}, bf16[320,512]{1,0:T(8,128)(2,1)S(1)}, u32[]{:S(2)}, u32[]{:S(2)}) collective-permute-start(bf16[320,512]{1,0:T(8,128)(2,1)S(1)} %get-tuple-element.61), channel_id=1, source_target_pairs={{0,2},{1,3},{2,4},{3,5},{4,6},{5,7},{6,0},{7,1},{8,10},{9,11},{10,... | collective-permute-start | bytes 983048 | tf_op jit(solution)/shard_map/ppermute | solution.py:441
  128.9 19.8 %collective-permute-start.19 = (bf16[320,512]{1,0:T(8,128)(2,1)S(1)}, bf16[320,512]{1,0:T(8,128)(2,1)S(1)}, u32[]{:S(2)}, u32[]{:S(2)}) collective-permute-start(bf16[320,512]{1,0:T(8,128)(2,1)S(1)} %get-tuple-element.54), channel_id=1, source_target_pairs={{0,6},{1,7},{2,0},{3,1},{4,2},{5,3},{6,4},{7,5},{8,14},{9,15},{10,... | collective-permute-start | bytes 983048 | tf_op jit(solution)/shard_map/ppermute | solution.py:441
  134.7 13.2 %collective-permute-start.22 = (bf16[320,512]{1,0:T(8,128)(2,1)S(1)}, bf16[320,512]{1,0:T(8,128)(2,1)S(1)}, u32[]{:S(2)}, u32[]{:S(2)}) collective-permute-start(bf16[320,512]{1,0:T(8,128)(2,1)S(1)} %shard_map.136), channel_id=1, source_target_pairs={{0,6},{1,7},{2,0},{3,1},{4,2},{5,3},{6,4},{7,5},{8,14},{9,15},{10,... | collective-permute-start | bytes 983048 | tf_op jit(solution)/shard_map/ppermute | solution.py:441
  139.4 12.8 %collective-permute-start.18 = (bf16[320,512]{1,0:T(8,128)(2,1)S(1)}, bf16[320,512]{1,0:T(8,128)(2,1)S(1)}, u32[]{:S(2)}, u32[]{:S(2)}) collective-permute-start(bf16[320,512]{1,0:T(8,128)(2,1)S(1)} %shard_map.132), channel_id=1, source_target_pairs={{0,2},{1,3},{2,4},{3,5},{4,6},{5,7},{6,0},{7,1},{8,10},{9,11},{10,... | collective-permute-start | bytes 983048 | tf_op jit(solution)/shard_map/ppermute | solution.py:441
  (21 other events, 48.9 us)

commit v3 on v2

v3 whole, which is shorter than its diff:
```python
import functools

import jax
import jax.numpy as jnp
from jax import lax
from jax.experimental import pallas as pl
from jax.experimental.pallas import tpu as pltpu
from jax.sharding import PartitionSpec as P

HEAD_DIM = 64
SPAN = 256
MIB = 1 << 20
BIG = 56
CHIPS = 4
AROUND = (0, CHIPS - 1, 1, 2)
BF16 = jnp.bfloat16
F32 = jnp.float32
HIGHEST = lax.Precision.HIGHEST

NN = (((1,), (0,)), ((), ()))
NT = (((1,), (1,)), ((), ()))
TN = (((0,), (0,)), ((), ()))


def mm(a, b, dims=NN, precision=None):
    return lax.dot_general(a, b, dims, precision=precision, preferred_element_type=F32)


def call(body, out, scratch=(), smem=(), near=(), held=(), pinned=(), count=0, work=(0, 0), limit=16):
    outs = list(out)
    n_out, n_scratch = len(outs), len(scratch)
    far = [i for i in range(count) if i not in smem and i not in held and i not in near]
    far_out = list(range(n_out)) if pinned is True else list(pinned)

    def kernel(*refs):
        ins, res = list(refs[:count]), list(refs[count : count + n_out])
        rest = refs[count + n_out :]
        own, rest = list(rest[:n_scratch]), list(rest[n_scratch:])
        copies, late = [], []
        for k, i in enumerate(far):
            copies.append(pltpu.make_async_copy(ins[i], rest[k], rest[-1].at[k]))
            ins[i] = rest[k]
        for k, i in enumerate(far_out, len(far)):
            late.append(pltpu.make_async_copy(rest[k], res[i], rest[-1].at[k]))
            res[i] = rest[k]
        for copy in copies:
            copy.start()
        if held:
            body(copies, *ins, *res, *own)
        else:
            for copy in copies:
                copy.wait()
            body(*ins, *res, *own)
        for copy in late:
            copy.start()
        for copy in late:
            copy.wait()

    def space(i):
        return pltpu.SMEM if i in smem else pltpu.VMEM if i in near else pltpu.HBM

    def run(*args):
        assert len(args) == count
        buffers = [pltpu.VMEM(args[i].shape, args[i].dtype) for i in far]
        buffers += [pltpu.VMEM(outs[i].shape, outs[i].dtype) for i in far_out]
        if buffers:
            buffers.append(pltpu.SemaphoreType.DMA((len(buffers),)))
        return pl.pallas_call(
            kernel,
            out_shape=[
                pltpu.HBM(v.shape, v.dtype) if i in far_out else v for i, v in enumerate(outs)
            ],
            in_specs=[pl.BlockSpec(memory_space=space(i)) for i in range(count)],
            out_specs=[
                pl.BlockSpec(memory_space=pltpu.HBM if i in far_out else pltpu.VMEM)
                for i in range(n_out)
            ],
            scratch_shapes=list(scratch) + buffers,
            cost_estimate=pl.CostEstimate(
                flops=work[0], bytes_accessed=work[1], transcendentals=0
            ),
            compiler_params=pltpu.CompilerParams(vmem_limit_bytes=limit * MIB),
        )(*args)

    return run


def spread(rows, width):
    head = lax.broadcasted_iota(jnp.int32, (rows, width), 0)
    lane = lax.broadcasted_iota(jnp.int32, (rows, width), 1)
    return jnp.where(lane // HEAD_DIM == head, 1.0, 0.0).astype(F32)


CUM, CUM_DOT, REM, REM_DOT, CUM_EXP = 0, 16, 32, 48, 64


def decay_body(dec, table, columns, vec, tail):
    s = lax.broadcasted_iota(jnp.int32, (SPAN, SPAN), 0)
    t = lax.broadcasted_iota(jnp.int32, (SPAN, SPAN), 1)
    upper = jnp.where(s <= t, 1.0, 0.0).astype(F32)
    lower = jnp.where(t <= s, 1.0, 0.0).astype(F32)
    ends = []
    for b in range(dec.shape[1] // SPAN):
        lanes = slice(b * SPAN, (b + 1) * SPAN)
        both = dec[:, lanes]
        c = mm(both, upper, NN, HIGHEST)
        c_t = mm(lower, both, NT, HIGHEST)
        p, d = c[:16], c[16:]
        table[CUM : CUM + 16, lanes] = p
        table[CUM_DOT : CUM_DOT + 16, lanes] = d
        table[CUM_EXP : CUM_EXP + 16, lanes] = jnp.exp(p)
        r = jnp.exp(p[:, SPAN - 1 :] - p)
        table[REM : REM + 16, lanes] = r
        table[REM_DOT : REM_DOT + 16, lanes] = r * (d[:, SPAN - 1 :] - d)
        columns[lanes, :] = c_t
        ends.append(c_t[SPAN - 1 :, :])
    rows = jnp.concatenate(
        [ends[0][:, :16], ends[0][:, 16:], ends[1][:, :16], ends[1][:, 16:]]
        + [jnp.zeros((4, 16), F32)],
        0,
    )
    wide = mm(rows, spread(16, vec.shape[1]), NN, HIGHEST)
    row = lax.broadcasted_iota(jnp.int32, wide.shape, 0)
    vec[...] = jnp.where((row == 0) | (row == 2), jnp.exp(wide), wide)
    rest = ends[0] + ends[1]
    tail[...] = jnp.zeros(tail.shape, F32)
    for i in range(3):
        term = rest.astype(BF16).astype(F32)
        tail[i : i + 1, 0:32] = term
        rest = rest - term


def group(place, distance, other):
    chip, core = place[0] // 2, place[0] % 2
    return (chip + distance) % CHIPS * 2 + (1 - core if other else core)


def gather(place, pieces, full, sems):
    rows = pieces[0].shape[0]
    arriving = []
    for i, piece in enumerate(pieces):
        at = group(place, AROUND[i % 4], i >= 4) * rows
        here = full.at[pl.ds(pl.multiple_of(at, rows), rows), :]
        arriving.append(pltpu.make_async_copy(piece, here, sems.at[i]))
    for copy in arriving:
        copy.start()
    return arriving


CHUNK = 64


def convolve(ext, taps, store):
    count = taps.shape[0]
    for c in range(taps.shape[1] // 128):
        lanes = slice(c * 128, (c + 1) * 128)
        kernel = [jnp.broadcast_to(taps[k : k + 1, lanes], (CHUNK, 128)) for k in range(count)]
        for r in range(0, SPAN, CHUNK):
            summed = None
            for k in range(count):
                at = r + 9 - count + k
                term = kernel[k] * ext[at : at + CHUNK, lanes]
                summed = term if summed is None else summed + term
            store(slice(r, r + CHUNK), lanes, summed)


def turn(rows):
    s = lax.broadcasted_iota(jnp.int32, (SPAN, SPAN), 0)
    t = lax.broadcasted_iota(jnp.int32, (SPAN, SPAN), 1)
    return mm(rows, jnp.where(s == t, 1.0, 0.0).astype(BF16), TN).astype(BF16)


def to_owners(values):
    n, width = values.shape
    halves = [values[:, : width // 2], values[:, width // 2 :]]
    stacked = jnp.stack([v.reshape(n // 8, 8, width // 2) for v in halves], 1)
    return stacked.reshape(2 * n, width // 2)


def from_owners(values):
    n, width = values.shape
    split = values.reshape(n // 16, 2, 8, width)
    return jnp.concatenate([split[:, i].reshape(n // 2, width) for i in range(2)], 1)


def project(place, pieces, weights, out, full, w_all, total, sems):
    arriving = gather(place, pieces, full, sems)
    half = w_all.shape[0] // 2
    coming = []
    for part in range(2):
        rows = slice(part * half, (part + 1) * half)
        at = 0
        for i, weight in enumerate(weights):
            columns = slice(at, at + weight.shape[1])
            at = columns.stop
            copy = pltpu.make_async_copy(
                weight.at[rows, :], w_all.at[rows, columns], sems.at[8 + 3 * part + i]
            )
            copy.start()
            coming.append(copy)
    for copy in [*arriving, *coming[:3]]:
        copy.wait()
    total[...] = mm(full[:half, :], w_all[:half, :], TN)
    for copy in coming[3:]:
        copy.wait()
    out[...] = (total[...] + mm(full[half:, :], w_all[half:, :], TN)).astype(BF16)


def primal_body(copies, place, *refs):
    project(place, refs[:8], refs[8:11], *refs[11:])


def tangent_body(copies, place, *refs):
    first, projected, edge, full, w_all, total, last, sems = refs[11:]
    length = full.shape[1]
    ending = pltpu.make_async_copy(first.at[length - 16 :, :], last, sems.at[14])
    ending.start()
    project(place, refs[:8], refs[8:11], projected, full, w_all, total, sems)
    ending.wait()
    ends = [last[...].astype(F32)[8:], projected[length - 16 :, :].astype(F32)[8:]]
    edge[...] = jnp.concatenate(ends, 0).astype(BF16)


def block_body(b, projected, projected_dot, before, taps, table, vec, tail, *refs):
    if b == 0:
        state1, state1_dot, mixed, mixed_dot, state, state_dot, message = refs[:7]
        refs = refs[7:]
    else:
        mixed, mixed_dot, state, state_dot = refs[:4]
        refs = refs[4:]
    ext, ext_dot, gate, rows, rows_dot, scaled = refs
    at = slice(b * SPAN, (b + 1) * SPAN)
    for i, (source, out) in enumerate(((projected, ext), (projected_dot, ext_dot))):
        ahead = before[...].astype(F32)[8 * i : 8 * i + 8]
        if b > 0:
            ahead = source[b * SPAN - 16 : b * SPAN, :].astype(F32)[8:]
        out[0:8, :] = ahead
        out[8:, :] = source[at, :].astype(F32)

    def store(where, lanes, v):
        sig = 1.0 / (1.0 + jnp.exp(-v))
        rows[where, lanes] = (v * sig).astype(BF16)
        gate[where, lanes] = sig * (1.0 + v * (1.0 - sig))

    def store_dot(where, lanes, v):
        rows_dot[where, lanes] = (gate[where, lanes] * v).astype(BF16)

    convolve(ext, taps, store)
    mixed[...] = turn(rows[...])
    convolve(ext_dot, taps, store_dot)
    mixed_dot[...] = turn(rows_dot[...])
    width = vec.shape[1]
    for h in range(width // HEAD_DIM):
        here = slice(h * HEAD_DIM, (h + 1) * HEAD_DIM)
        value = mixed[here, :].astype(F32)
        r = table[REM + h : REM + h + 1, at]
        scaled[here, SPAN:] = (value * r).astype(BF16)
        scaled[here, :SPAN] = (
            mixed_dot[here, :].astype(F32) * r + value * table[REM_DOT + h : REM_DOT + h + 1, at]
        ).astype(BF16)
    writer = mixed[width : width + 128, :]
    writer_dot = mixed_dot[width : width + 128, :]
    own = mm(writer, scaled[:, SPAN:], NT)
    own_dot = mm(writer, scaled[:, :SPAN], NT) + mm(writer_dot, scaled[:, SPAN:], NT)
    state[...] = own
    state_dot[...] = own_dot
    if b == 0:
        own_dot = vec[2:3, :] * (own_dot + vec[3:4, :] * own) + state1_dot[...]
        own = vec[2:3, :] * own + state1[...]
        message[:, : width // 2] = to_owners(own).astype(BF16)
        message[:, width // 2 : width] = to_owners(own_dot).astype(BF16)
        both = jnp.concatenate([tail[...], tail[...]], 0).astype(BF16)
        for j in range(message.shape[0] // 16):
            message[16 * j : 16 * j + 16, width:] = both


def within_body(first, second, first_dot, second_dot, table, columns, gain, within, within_dot, sc, scd):
    width = within.shape[0]
    state = (first.shape[0] - width) // 2
    s = lax.broadcasted_iota(jnp.int32, (SPAN, SPAN), 0)
    t = lax.broadcasted_iota(jnp.int32, (SPAN, SPAN), 1)
    causal = s <= t
    for b in range(2):
        lanes = slice(b * SPAN, (b + 1) * SPAN)
        mixed, mixed_dot = ((first, first_dot), (second, second_dot))[b]
        writer, reader = mixed[width : width + state, :], mixed[width + state :, :]
        writer_dot, reader_dot = mixed_dot[width : width + state, :], mixed_dot[width + state :, :]
        sc[...] = mm(writer, reader, TN)
        scd[...] = mm(writer_dot, reader, TN) + mm(writer, reader_dot, TN)
        for h in range(width // HEAD_DIM):
            rows = slice(h * HEAD_DIM, (h + 1) * HEAD_DIM)
            diff = table[CUM + h : CUM + h + 1, lanes] - columns[lanes, h : h + 1]
            diff_dot = (
                table[CUM_DOT + h : CUM_DOT + h + 1, lanes] - columns[lanes, 16 + h : 17 + h]
            )
            weight = jnp.exp(jnp.where(causal, diff, -jnp.inf))
            mix = (weight * sc[...]).astype(BF16)
            mix_dot = (weight * (scd[...] + diff_dot * sc[...])).astype(BF16)
            value, value_dot = mixed[rows, :], mixed_dot[rows, :]
            both = mm(jnp.concatenate([value, value_dot], 0), mix)
            other = mm(value, mix_dot)
            skip = gain[0:1, h : h + 1]
            within[rows, lanes] = both[:HEAD_DIM] + skip * value.astype(F32)
            within_dot[rows, lanes] = (both[HEAD_DIM:] + other) + skip * value_dot.astype(F32)


def unpack(half, width, which):
    lane = lax.broadcasted_iota(jnp.int32, (128, width), 0)
    head = lax.broadcasted_iota(jnp.int32, (128, width), 1) // HEAD_DIM + half * (width // HEAD_DIM)
    return jnp.where(lane == head + 16 * which, 1.0, 0.0).astype(BF16)


def scan_body(half, arrived, leaving, states, retain, slope):
    rows, whole = 8, leaving.shape[1]
    width = whole // 2
    steps = arrived.shape[0] // rows
    tails = arrived[:, whole:]
    for which, out in ((0, retain), (1, slope)):
        terms = mm(tails, unpack(half[0], width, which)).reshape(steps, rows, width)
        out[...] = (terms[:, 0] + terms[:, 1]) + terms[:, 2]
    retain[...] = jnp.exp(retain[...])
    states[...] = arrived[:, :whole].astype(F32)
    state = jnp.zeros((rows, width), F32)
    state_dot = jnp.zeros((rows, width), F32)
    for j in range(steps):
        own = slice(j * rows, (j + 1) * rows)
        arriving, arriving_dot = states[own, :width], states[own, width:]
        states[own, :width] = state
        states[own, width:] = state_dot
        r = retain[j : j + 1, :]
        state_dot = r * (state_dot + slope[j : j + 1, :] * state) + arriving_dot
        state = r * state + arriving
    leaving[...] = states[...].astype(BF16)


def arrange_body(place, w_t, keep, send):
    rows = w_t.shape[0] // (2 * CHIPS)
    for d in range(CHIPS):
        own = slice(d * rows, (d + 1) * rows)
        for other, out in ((False, keep), (True, send)):
            at = pl.multiple_of(group(place, d, other) * rows, rows)
            out[own, :] = w_t[pl.ds(at, rows), :]


def own_body(keep, own, out):
    for b in range(own.shape[1] // SPAN):
        lanes = slice(b * SPAN, (b + 1) * SPAN)
        out[:, lanes] = mm(keep[...], own[:, lanes])


def product_body(begun, received, other, *outs):
    rows = outs[0].shape[0]
    for b in range(other.shape[1] // SPAN):
        lanes = slice(b * SPAN, (b + 1) * SPAN)
        result = begun[:, lanes] + mm(received[...], other[:, lanes])
        for d, out in enumerate(outs):
            out[:, lanes] = result[d * rows : (d + 1) * rows].astype(BF16)


def read_body(
    copies, arrived, first, second, first_dot, second_dot, within, within_dot, table, vec, s0, s0_dot,
    inner, inner_dot, readers, readers_dot, sems,
):
    n = readers.shape[0]
    reading = []
    for i, (source, out) in enumerate(
        ((first, readers), (second, readers), (first_dot, readers_dot), (second_dot, readers_dot))
    ):
        lanes = slice((i % 2) * SPAN, (i % 2 + 1) * SPAN)
        reading.append(
            pltpu.make_async_copy(
                source.at[source.shape[0] - n :, :], out.at[:, lanes], sems.at[i]
            )
        )
    for copy in reading:
        copy.start()
    for copy in [*copies, *reading]:
        copy.wait()
    width = within.shape[0]
    entry = from_owners(arrived[:, : width // 2].astype(F32))
    entry_dot = from_owners(arrived[:, width // 2 :].astype(F32))
    for b in range(2):
        lanes = slice(b * SPAN, (b + 1) * SPAN)
        reader, reader_dot = readers[:, lanes], readers_dot[:, lanes]
        rounded = entry.astype(BF16)
        read = mm(rounded, reader, TN)
        read_dot = mm(rounded, reader_dot, TN) + mm(entry_dot.astype(BF16), reader, TN)
        for h in range(width // HEAD_DIM):
            rows = slice(h * HEAD_DIM, (h + 1) * HEAD_DIM)
            e = table[CUM_EXP + h : CUM_EXP + h + 1, lanes]
            d = table[CUM_DOT + h : CUM_DOT + h + 1, lanes]
            inner[rows, lanes] = (within[rows, lanes] + e * read[rows]).astype(BF16)
            inner_dot[rows, lanes] = (
                within_dot[rows, lanes] + e * (read_dot[rows] + d * read[rows])
            ).astype(BF16)
        if b == 0:
            retain, slope = vec[0:1, :], vec[1:2, :]
            entry_dot = retain * (entry_dot + slope * entry) + s0_dot[...]
            entry = retain * entry + s0[...]


def total_body(*refs):
    out = refs[-1]
    summed = refs[0][...].astype(F32)
    for ref in refs[1:-1]:
        summed = summed + ref[...].astype(F32)
    out[...] = summed.astype(BF16)


def on_device(
    tokens,
    tangent_tokens,
    log_decay,
    tangent_decay,
    w_inner,
    w_bmat,
    w_cmat,
    conv_inner,
    conv_bc,
    skip_gain,
    w_out,
):
    length, piece = tokens.shape
    model, width = w_inner.shape
    state_len = w_bmat.shape[1]
    channels = width + 2 * state_len
    heads = width // HEAD_DIM
    n_ctx, n_head = lax.axis_size("ctx"), lax.axis_size("head")
    chips = n_head // 2
    margin = conv_inner.shape[0] - 1
    shape = jax.ShapeDtypeStruct
    place = lax.axis_index("head")

    def along(values, distance):
        route = [
            (2 * i + j, 2 * ((i + distance) % chips) + j) for i in range(chips) for j in range(2)
        ]
        return lax.ppermute(values, "head", route)

    def swap(values):
        return lax.ppermute(values, "head", [(i, i ^ 1) for i in range(n_head)])

    def exchange(values):
        blocks = values.reshape(n_ctx, values.shape[0] // n_ctx, values.shape[1])
        return lax.all_to_all(blocks, "ctx", 0, 0).reshape(values.shape)

    first, second = tokens.T, tangent_tokens.T
    first_up, first_down = along(first, 1), along(first, -1)

    second_down = along(second, -1)
    pad = ((0, 16 - heads), (0, 0))
    dec = jnp.concatenate([jnp.pad(log_decay.T, pad), jnp.pad(tangent_decay.T, pad)], 0)
    table, columns, vec, tail = call(
        decay_body,
        [shape((80, length), F32), shape((length, 32), F32)]
        + [shape((8, width), F32), shape((8, 128), F32)],
        pinned=True,
        count=1,
        work=(10**8, 10**6),
    )(dec)
    first_up, table = lax.optimization_barrier((first_up, table))
    first_far = along(first_up, 1)
    later, first_far = lax.optimization_barrier((second, first_far))
    second_up = along(later, 1)
    second_far = along(second_down, -1)
    firsts = [first, first_up, first_down, first_far]
    firsts = firsts + [swap(v) for v in firsts]
    here = place[None]
    taps = jnp.concatenate([conv_inner, conv_bc], 1)

    full = [pltpu.VMEM((model, length), BF16), pltpu.VMEM((model, channels), BF16)]
    full += [pltpu.VMEM((length, channels), F32)]
    work = (2 * channels * model * length, 12 * MIB)
    tokens_by = shape((length, channels), BF16)
    (projected,) = call(
        primal_body,
        [tokens_by],
        [*full, pltpu.SemaphoreType.DMA((14,))],
        held=tuple(range(1, 12)),
        count=12,
        smem=(0,),
        work=work,
        limit=BIG,
    )(here, *firsts, w_inner, w_bmat, w_cmat)
    second_up, second_far, projected = lax.optimization_barrier(
        (second_up, second_far, projected)
    )
    seconds = [second, second_up, second_down, second_far]
    seconds = seconds + [swap(second), swap(second_up), swap(second_down), swap(second_far)]
    projected_dot, edge = call(
        tangent_body,
        [tokens_by, shape((16, channels), BF16)],
        [*full, pltpu.VMEM((16, channels), BF16), pltpu.SemaphoreType.DMA((15,))],
        held=tuple(range(1, 13)),
        count=13,
        smem=(0,),
        work=work,
        limit=BIG,
    )(here, *seconds, w_inner, w_bmat, w_cmat, projected)
    before = lax.ppermute(edge, "ctx", [(i, i + 1) for i in range(n_ctx - 1)])
    mix = shape((channels, SPAN), BF16)
    state = shape((state_len, width), F32)

    def block(b, out, before, *more):
        args = (projected, projected_dot, before, taps, table, vec, tail, *more)
        return call(
            functools.partial(block_body, b),
            [mix, mix, state, state, *out],
            [pltpu.VMEM((SPAN + 8, channels), F32)] * 2
            + [pltpu.VMEM((SPAN, channels), F32)]
            + [pltpu.VMEM((SPAN, channels), BF16)] * 2
            + [pltpu.VMEM((width, 2 * SPAN), BF16)],
            near=(0, 1, 2, 7, 8),
            pinned=(0, 1, 2, 3, 4) if out else (0, 1),
            count=len(args),
            work=(10**9, 8 * MIB),
            limit=20,
        )(*args)

    mixed1, mixed1_dot, state1, state1_dot = block(1, [], edge)
    mixed0, mixed0_dot, state0, state0_dot, message = block(
        0, [shape((2 * state_len, width + 128), BF16)], before, state1, state1_dot
    )

    arrived = exchange(message)
    gains = jnp.pad(skip_gain[None], ((0, 0), (0, 16 - heads)))
    wide = shape((width, length), F32)
    within, within_dot = call(
        within_body,
        [wide, wide],
        [pltpu.VMEM((SPAN, SPAN), F32)] * 2,
        pinned=True,
        count=7,
        work=(5 * 10**9, 8 * MIB),
        limit=BIG,
    )(mixed0, mixed1, mixed0_dot, mixed1_dot, table, columns, gains)
    half = (lax.axis_index("ctx") % 2).astype(jnp.int32)[None]
    line = pltpu.VMEM((n_ctx, width // 2), F32)
    (leaving,) = call(
        scan_body,
        [shape((2 * state_len, width), BF16)],
        [pltpu.VMEM((2 * state_len, width), F32), line, line],
        near=(1,),
        count=2,
        smem=(0,),
        work=(10**8, MIB),
    )(half, arrived)
    entry = exchange(leaving)

    side = shape((model // 2, width), BF16)
    keep, send = call(
        arrange_body, [side, side], near=(1,), count=2, smem=(0,), work=(10**6, 6 * MIB)
    )(here, w_out.T)
    received = swap(send)
    values = shape((width, length), BF16)
    reader = pltpu.VMEM((state_len, length), BF16)
    inner, inner_dot = call(
        read_body,
        [values, values],
        [reader, reader, pltpu.SemaphoreType.DMA((4,))],
        near=(0,),
        held=(1, 2, 3, 4),
        count=11,
        work=(10**9, 6 * MIB),
        limit=BIG,
    )(
        entry, mixed0, mixed1, mixed0_dot, mixed1_dot, within, within_dot, table, vec, state0,
        state0_dot,
    )
    term = shape((piece, length), BF16)
    work = (2 * chips * piece * width * length, 4 * MIB)
    begin = call(
        own_body, [shape((chips * piece, length), F32)], near=(0, 1), count=2, work=work
    )
    product = call(product_body, [term] * chips, near=(0, 1, 2), count=3, work=work)

    def total(*terms):
        count = len(terms)
        body = call(total_body, [term], near=range(count), count=count, work=(10**6, 2 * MIB))
        return body(*terms)[0]

    def finish(begun, other, way):
        terms = product(begun, received, other)
        far = along(terms[2], way)
        near, back = (terms[1], terms[3]) if way == 1 else (terms[3], terms[1])
        back = along(back, -way)
        near = along(total(near, far), way)
        return total(terms[0], near, back).T

    other, other_dot = swap(inner), swap(inner_dot)
    begun, begun_dot = begin(keep, inner)[0], begin(keep, inner_dot)[0]
    return finish(begun, other, 1), finish(begun_dot, other_dot, -1)


def solution(mesh):
    in_specs = (
        P("ctx", "head"),
        P("ctx", "head"),
        P("ctx", "head"),
        P("ctx", "head"),
        P(None, "head"),
        P(),
        P(),
        P(None, "head"),
        P(),
        P("head"),
        P("head", None),
    )
    out_specs = (P("ctx", "head"), P("ctx", "head"))
    return jax.shard_map(
        on_device, mesh=mesh, in_specs=in_specs, out_specs=out_specs, check_vma=False
    )
```

time: 154 us -> 143 us (0.929)
  local copies, waits for them, and re-layouts: 27.8 us -> 11.4 us
  waiting for transfers between devices: 40.5 us -> 44.7 us
    unnamed x54 -> x58, local copies, waits for them, and re-layouts: 23.2 us -> 10.8 us
    ppermute x12, starting transfers between devices: 15.1 us -> 19.6 us  [along(): return lax.ppermute(values, 'head', route)]
    ppermute x12, waiting for transfers between devices: 24 us -> 28.2 us  [along(): return lax.ppermute(values, 'head', route)]
    all_to_all x2, waiting for transfers between devices: 11 us -> 15 us  [exchange(): return lax.all_to_all(blocks, 'ctx', 0, 0).reshape(values.shape)]
    all_to_all x1 -> x0, waiting for transfers between devices: 3.69 us -> none  [on_device(): lax.all_to_all(jnp.broadcast_to(edge[None], (n_head, *edge.shape)), 'head...]
    all_to_all x1 -> x0, starting transfers between devices: 3.36 us -> none  [on_device(): lax.all_to_all(jnp.broadcast_to(edge[None], (n_head, *edge.shape)), 'head...]
    slice x2 -> x0, local copies, waits for them, and re-layouts: 3.13 us -> none  [the longest x1 1.57 us: on_device(): mixed_dot[bc:]]
    pallas_call x16 -> x17, Pallas kernels: 42.2 us -> 43.4 us  [run(): pl.pallas_call(kernel, out_shape=[pltpu.HBM(v.shape, v.dtype) if i in far...]
  transfers between devices with their start and end apart: 27 -> 26, of which waited for: 12 -> 12; matrix products, arithmetic and copies ran while one was open for 6% -> 4% of each run, Pallas kernels for 22% -> 22%
where the time goes in v3:
time: 143 us; the launch traced here: 142 us
  waiting for transfers between devices  44.7 us (31%)
  Pallas kernels  43.4 us (30%)
  starting transfers between devices  41 us (29%)
  local copies, waits for them, and re-layouts  11.4 us (8%)
    pallas_call x17, Pallas kernels, run(): pl.pallas_call(kernel, out_shape=[pltpu.HBM(v.shape, v.dtype) if i in far...  43.4 us
    ppermute x12, waiting for transfers between devices, along(): return lax.ppermute(values, 'head', route)  28.2 us
    ppermute x12, starting transfers between devices, along(): return lax.ppermute(values, 'head', route)  19.6 us
    all_to_all x2, starting transfers between devices, exchange(): return lax.all_to_all(blocks, 'ctx', 0, 0).reshape(values.shape)  15.3 us
    all_to_all x2, waiting for transfers between devices, exchange(): return lax.all_to_all(blocks, 'ctx', 0, 0).reshape(values.shape)  15 us
    unnamed x58, local copies, waits for them, and re-layouts  10.8 us
    ppermute x1, starting transfers between devices, on_device(): before = lax.ppermute(edge, 'ctx', [(i, i + 1) for i in range(n_ctx - 1)])  3.82 us
  transfers between devices with their start and end apart: 26, of which 12 were waited for; matrix products, arithmetic and copies ran while one was open for 4% of the time, Pallas kernels for 22%

profile of v3, /device:TPU:32, one launch (start us, length us, event | category | flops | bytes accessed | tf_op | source)
XLA Modules:
  0.0 142.4 jit_solution(13155236909358996618)
XLA Ops:
  0.6 1.6 %collective-permute-start = (bf16[320,512]{1,0:T(8,128)(2,1)}, bf16[320,512]{1,0:T(8,128)(2,1)S(1)}, u32[]{:S(2)}, u32[]{:S(2)}) collective-permute-start(bf16[320,512]{1,0:T(8,128)(2,1)} %bitcast.21), channel_id=1, source_target_pairs={{0,2},{1,3},{2,4},{3,5},{4,6},{5,7},{6,0},{7,1},{8,10},{9,11},{10,... | collective-permute-start | bytes 983048 | tf_op jit(solution)/shard_map/ppermute | solution.py:438
  2.2 1.7 %collective-permute-start.5 = (bf16[320,512]{1,0:T(8,128)(2,1)}, bf16[320,512]{1,0:T(8,128)(2,1)S(1)}, u32[]{:S(2)}, u32[]{:S(2)}) collective-permute-start(bf16[320,512]{1,0:T(8,128)(2,1)} %bitcast.22), channel_id=1, source_target_pairs={{0,6},{1,7},{2,0},{3,1},{4,2},{5,3},{6,4},{7,5},{8,14},{9,15},{10,... | collective-permute-start | bytes 983048 | tf_op jit(solution)/shard_map/ppermute | solution.py:438
  4.7 1.8 %shard_map.123 = (f32[80,512]{1,0:T(8,128)}, f32[512,32]{1,0:T(8,128)}, f32[8,640]{1,0:T(8,128)}, f32[8,128]{1,0:T(8,128)}) custom-call(f32[32,512]{1,0:T(8,128)S(1)} %select_maximum_fusion.refs_0_), custom_call_target="tpu_custom_call" | custom-call | flops 100000000 | bytes 1000000 | tf_op jit(solution)/shard_map/pallas_call | solution.py:68
  6.5 5.1 %collective-permute-done.refs_2_ = bf16[320,512]{1,0:T(8,128)(2,1)S(1)} collective-permute-done((bf16[320,512]{1,0:T(8,128)(2,1)}, bf16[320,512]{1,0:T(8,128)(2,1)S(1)}, u32[]{:S(2)}, u32[]{:S(2)}) %collective-permute-start) | collective-permute-done | bytes 327712 | tf_op jit(solution)/shard_map/ppermute | solution.py:438
  11.9 3.0 %collective-permute-start.3 = (bf16[320,512]{1,0:T(8,128)(2,1)}, bf16[320,512]{1,0:T(8,128)(2,1)S(1)}, u32[]{:S(2)}, u32[]{:S(2)}) collective-permute-start(bf16[320,512]{1,0:T(8,128)(2,1)} %bitcast.25), channel_id=1, source_target_pairs={{0,6},{1,7},{2,0},{3,1},{4,2},{5,3},{6,4},{7,5},{8,14},{9,15},{10,... | collective-permute-start | bytes 983048 | tf_op jit(solution)/shard_map/ppermute | solution.py:438
  15.4 5.9 %collective-permute-done.1.refs_4_ = bf16[320,512]{1,0:T(8,128)(2,1)S(1)} collective-permute-done((bf16[320,512]{1,0:T(8,128)(2,1)S(1)}, bf16[320,512]{1,0:T(8,128)(2,1)S(1)}, u32[]{:S(2)}, u32[]{:S(2)}) %collective-permute-start.1) | collective-permute-done | bytes 327712 | tf_op jit(solution)/shard_map/ppermute | solution.py:438
  21.4 3.1 %collective-permute-start.4 = (bf16[320,512]{1,0:T(8,128)(2,1)S(1)}, bf16[320,512]{1,0:T(8,128)(2,1)S(1)}, u32[]{:S(2)}, u32[]{:S(2)}) collective-permute-start(bf16[320,512]{1,0:T(8,128)(2,1)S(1)} %collective-permute-done.3.refs_3_), channel_id=1, source_target_pairs={{0,6},{1,7},{2,0},{3,1},{4,2},{5,3},{6,4},{7,5},{8,14},{9,15},{10,... | collective-permute-start | bytes 983048 | tf_op jit(solution)/shard_map/ppermute | solution.py:438
  25.9 6.4 %shard_map.124.refs_12_.refs_0_ = bf16[512,896]{1,0:T(8,128)(2,1)} custom-call(s32[1]{0:T(128)} %bitcast.refs_0_, bf16[320,512]{1,0:T(8,128)(2,1)} %bitcast.24, bf16[320,512]{1,0:T(8,128)(2,1)} %copy-done.14, bf16[320,512]{1,0:T(8,128)(2,1)} %copy-done.15, bf16[320,512]{1,0:T(8,128)(2,1)} %copy-done.17, bf16[320,512]{1,0:T(8,128)(2,1)} %copy-done.19, ...), custom_call_target="tpu_custom_call" | custom-call | flops 2348810240 | bytes 12582912 | tf_op jit(solution)/shard_map/pallas_call | solution.py:68
  36.2 6.5 %shard_map.125 = (bf16[512,896]{1,0:T(8,128)(2,1)}, bf16[16,896]{1,0:T(8,128)(2,1)}) custom-call(s32[1]{0:T(128)} %bitcast.refs_0_, bf16[320,512]{1,0:T(8,128)(2,1)} %bitcast.28, bf16[320,512]{1,0:T(8,128)(2,1)} %copy-done.18, bf16[320,512]{1,0:T(8,128)(2,1)} %copy-done.13, bf16[320,512]{1,0:T(8,128)(2,1)} %copy-done.16, bf16[320,512]{1,0:T(8,128)(2,1)} %copy-done.21, ...), custom_call_target="tpu_custom_call" | custom-call | flops 2348810240 | bytes 12582912 | tf_op jit(solution)/shard_map/pallas_call | solution.py:68
  42.6 3.8 %collective-permute-start.14 = (bf16[16,896]{1,0:T(8,128)(2,1)}, bf16[16,896]{1,0:T(8,128)(2,1)S(1)}, u32[]{:S(2)}, u32[]{:S(2)}) collective-permute-start(bf16[16,896]{1,0:T(8,128)(2,1)} %get-tuple-element.47.refs_2_), channel_id=1, source_target_pairs={{0,8},{8,16},{16,24},{24,32},{32,40},{40,48},{48,56},{56,64},{64,7... | collective-permute-start | bytes 86024 | tf_op jit(solution)/shard_map/ppermute | solution.py:500
  47.3 1.2 copy-done.8
  48.4 3.6 %shard_map.126 = (bf16[896,256]{1,0:T(8,128)(2,1)}, bf16[896,256]{1,0:T(8,128)(2,1)}, f32[128,640]{1,0:T(8,128)S(1)}, f32[128,640]{1,0:T(8,128)S(1)}) custom-call(bf16[512,896]{1,0:T(8,128)(2,1)S(1)} %copy-done.7, bf16[512,896]{1,0:T(8,128)(2,1)S(1)} %copy-done.8, bf16[16,896]{1,0:T(8,128)(2,1)S(1)} %copy-done.6, ...), custom_call_target="tpu_custom_call" | custom-call | flops 1000000000 | bytes 8388608 | tf_op jit(solution)/shard_map/pallas_call | solution.py:68
  52.1 4.2 %shard_map.127 = (bf16[896,256]{1,0:T(8,128)(2,1)}, bf16[896,256]{1,0:T(8,128)(2,1)}, f32[128,640]{1,0:T(8,128)}, f32[128,640]{1,0:T(8,128)}, bf16[256,768]{1,0:T(8,128)(2,1)}) custom-call(bf16[512,896]{1,0:T(8,128)(2,1)S(1)} %copy-done.7, bf16[512,896]{1,0:T(8,128)(2,1)S(1)} %copy-done.8, bf16[16,896]{1,0:T(8,128)(2,1)S(1)} %collective-permute-done.14.refs_2_, ...), custom_call_target="tpu_custom_call" | custom-call | flops 1000000000 | bytes 8388608 | tf_op jit(solution)/shard_map/pallas_call | solution.py:68
  56.2 10.5 %all-to-all-start = ((bf16[32,8,768]{2,1,0:T(8,128)(2,1)}), bf16[32,8,768]{2,1,0:T(8,128)(2,1)}, u32[]{:S(2)}, u32[]{:S(2)}) async-start(bf16[32,8,768]{2,1,0:T(8,128)(2,1)} %bitcast.16), calls=%async_computation | async-start | bytes 786432 | tf_op jit(solution)/shard_map/all_to_all | solution.py:445
  66.8 4.2 %copy.13 = bf16[640,2560]{0,1:T(8,128)(2,1)S(1)} copy(bf16[640,2560]{1,0:T(8,128)(2,1)} %param.21) | data formatting | bytes 6553600 | tf_op args[10]
  71.0 1.5 %shard_map.122 = (bf16[1280,640]{1,0:T(8,128)(2,1)S(1)}, bf16[1280,640]{1,0:T(8,128)(2,1)}) custom-call(s32[1]{0:T(128)} %bitcast.refs_0_, bf16[2560,640]{1,0:T(8,128)(2,1)S(1)} %bitcast.14), custom_call_target="tpu_custom_call" | custom-call | flops 1000000 | bytes 6291456 | tf_op jit(solution)/shard_map/pallas_call | solution.py:68
  73.6 8.1 %all-to-all-done = bf16[32,8,768]{2,1,0:T(8,128)(2,1)} async-done(((bf16[32,8,768]{2,1,0:T(8,128)(2,1)}), bf16[32,8,768]{2,1,0:T(8,128)(2,1)}, u32[]{:S(2)}, u32[]{:S(2)}) %all-to-all-start) | async-done | bytes 393248 | tf_op jit(solution)/shard_map/all_to_all | solution.py:445
  81.7 2.3 %shard_map.128 = bf16[256,640]{1,0:T(8,128)(2,1)} custom-call(s32[1]{0:T(128)} %bitcast.2.refs_0_, bf16[256,768]{1,0:T(8,128)(2,1)} %bitcast.8.refs_1_), custom_call_target="tpu_custom_call" | custom-call | flops 100000000 | bytes 1048576 | tf_op jit(solution)/shard_map/pallas_call | solution.py:68
  84.0 4.8 %all-to-all-start.1 = ((bf16[32,8,640]{2,1,0:T(8,128)(2,1)}), bf16[32,8,640]{2,1,0:T(8,128)(2,1)S(1)}, u32[]{:S(2)}, u32[]{:S(2)}) async-start(bf16[32,8,640]{2,1,0:T(8,128)(2,1)} %bitcast.9), calls=%async_computation.1 | async-start | bytes 655360 | tf_op jit(solution)/shard_map/all_to_all | solution.py:445
  89.3 5.7 %shard_map.129 = (f32[640,512]{1,0:T(8,128)}, f32[640,512]{1,0:T(8,128)}) custom-call(bf16[896,256]{1,0:T(8,128)(2,1)} %get-tuple-element.54.refs_0_.refs_1_, bf16[896,256]{1,0:T(8,128)(2,1)} %get-tuple-element.55.refs_1_.refs_2_, bf16[896,256]{1,0:T(8,128)(2,1)} %get-tuple-element.56.refs_2_.refs_3_, bf16[896,256]{1,0:T(8,128)(2,1)} %get-tuple-element.57.refs_3_.refs_4_, ...), custom_call_target="tpu_custom_call" | custom-call | flops 5000000000 | bytes 8388608 | tf_op jit(solution)/shard_map/pallas_call | solution.py:68
  95.1 6.9 %all-to-all-done.1 = bf16[32,8,640]{2,1,0:T(8,128)(2,1)S(1)} async-done(((bf16[32,8,640]{2,1,0:T(8,128)(2,1)}), bf16[32,8,640]{2,1,0:T(8,128)(2,1)S(1)}, u32[]{:S(2)}, u32[]{:S(2)}) %all-to-all-start.1) | async-done | bytes 327712 | tf_op jit(solution)/shard_map/all_to_all | solution.py:445
  102.7 5.0 %shard_map.130 = (bf16[640,512]{1,0:T(8,128)(2,1)}, bf16[640,512]{1,0:T(8,128)(2,1)}) custom-call(bf16[256,640]{1,0:T(8,128)(2,1)} %bitcast.15, bf16[896,256]{1,0:T(8,128)(2,1)} %get-tuple-element.54.refs_0_.refs_1_, bf16[896,256]{1,0:T(8,128)(2,1)} %get-tuple-element.55.refs_1_.refs_2_, bf16[896,256]{1,0:T(8,128)(2,1)} %get-tuple-element.56.refs_2_.refs_3_, ...), custom_call_target="tpu_custom_call" | custom-call | flops 1000000000 | bytes 6291456 | tf_op jit(solution)/shard_map/pallas_call | solution.py:68
  110.5 1.2 shard_map.131.refs_0_
  111.8 1.2 shard_map.136
  112.9 2.7 %collective-permute-start.21 = (bf16[320,512]{1,0:T(8,128)(2,1)S(1)}, bf16[320,512]{1,0:T(8,128)(2,1)S(1)}, u32[]{:S(2)}, u32[]{:S(2)}) collective-permute-start(bf16[320,512]{1,0:T(8,128)(2,1)S(1)} %get-tuple-element.72), channel_id=1, source_target_pairs={{0,6},{1,7},{2,0},{3,1},{4,2},{5,3},{6,4},{7,5},{8,14},{9,15},{10,... | collective-permute-start | bytes 983048 | tf_op jit(solution)/shard_map/ppermute | solution.py:438
  115.6 1.2 shard_map.132
  117.0 3.2 %collective-permute-start.19 = (bf16[320,512]{1,0:T(8,128)(2,1)S(1)}, bf16[320,512]{1,0:T(8,128)(2,1)S(1)}, u32[]{:S(2)}, u32[]{:S(2)}) collective-permute-start(bf16[320,512]{1,0:T(8,128)(2,1)S(1)} %get-tuple-element.68), channel_id=1, source_target_pairs={{0,6},{1,7},{2,0},{3,1},{4,2},{5,3},{6,4},{7,5},{8,14},{9,15},{10,... | collective-permute-start | bytes 983048 | tf_op jit(solution)/shard_map/ppermute | solution.py:438
  120.2 3.5 %collective-permute-done.21.refs_1_ = bf16[320,512]{1,0:T(8,128)(2,1)S(1)} collective-permute-done((bf16[320,512]{1,0:T(8,128)(2,1)S(1)}, bf16[320,512]{1,0:T(8,128)(2,1)S(1)}, u32[]{:S(2)}, u32[]{:S(2)}) %collective-permute-start.21) | collective-permute-done | bytes 327712 | tf_op jit(solution)/shard_map/ppermute | solution.py:438
  123.7 3.8 %collective-permute-start.22 = (bf16[320,512]{1,0:T(8,128)(2,1)S(1)}, bf16[320,512]{1,0:T(8,128)(2,1)S(1)}, u32[]{:S(2)}, u32[]{:S(2)}) collective-permute-start(bf16[320,512]{1,0:T(8,128)(2,1)S(1)} %shard_map.137), channel_id=1, source_target_pairs={{0,6},{1,7},{2,0},{3,1},{4,2},{5,3},{6,4},{7,5},{8,14},{9,15},{10,... | collective-permute-start | bytes 983048 | tf_op jit(solution)/shard_map/ppermute | solution.py:438
  128.8 6.9 %collective-permute-done.23.refs_2_ = bf16[320,512]{1,0:T(8,128)(2,1)S(1)} collective-permute-done((bf16[320,512]{1,0:T(8,128)(2,1)S(1)}, bf16[320,512]{1,0:T(8,128)(2,1)S(1)}, u32[]{:S(2)}, u32[]{:S(2)}) %collective-permute-start.23) | collective-permute-done | bytes 327712 | tf_op jit(solution)/shard_map/ppermute | solution.py:438
  135.7 1.2 collective-permute-done.22.refs_1_
  137.7 3.8 %collective-permute-done.18.refs_1_ = bf16[320,512]{1,0:T(8,128)(2,1)S(1)} collective-permute-done((bf16[320,512]{1,0:T(8,128)(2,1)S(1)}, bf16[320,512]{1,0:T(8,128)(2,1)S(1)}, u32[]{:S(2)}, u32[]{:S(2)}) %collective-permute-start.18) | collective-permute-done | bytes 327712 | tf_op jit(solution)/shard_map/ppermute | solution.py:438
  (98 shorter events, 16.0 us)
Async XLA Ops:
  0.6 10.9 %collective-permute-start = (bf16[320,512]{1,0:T(8,128)(2,1)}, bf16[320,512]{1,0:T(8,128)(2,1)S(1)}, u32[]{:S(2)}, u32[]{:S(2)}) collective-permute-start(bf16[320,512]{1,0:T(8,128)(2,1)} %bitcast.21), channel_id=1, source_target_pairs={{0,2},{1,3},{2,4},{3,5},{4,6},{5,7},{6,0},{7,1},{8,10},{9,11},{10,... | collective-permute-start | bytes 983048 | tf_op jit(solution)/shard_map/ppermute | solution.py:438
  2.2 13.1 %collective-permute-start.5 = (bf16[320,512]{1,0:T(8,128)(2,1)}, bf16[320,512]{1,0:T(8,128)(2,1)S(1)}, u32[]{:S(2)}, u32[]{:S(2)}) collective-permute-start(bf16[320,512]{1,0:T(8,128)(2,1)} %bitcast.22), channel_id=1, source_target_pairs={{0,6},{1,7},{2,0},{3,1},{4,2},{5,3},{6,4},{7,5},{8,14},{9,15},{10,... | collective-permute-start | bytes 983048 | tf_op jit(solution)/shard_map/ppermute | solution.py:438
  11.6 13.6 %copy-start.14 = (bf16[320,512]{1,0:T(8,128)(2,1)}, bf16[320,512]{1,0:T(8,128)(2,1)S(1)}, u32[]{:S(2)}) copy-start(bf16[320,512]{1,0:T(8,128)(2,1)S(1)} %collective-permute-done.refs_2_) | copy-start | bytes 983044
  11.6 9.8 %collective-permute-start.1 = (bf16[320,512]{1,0:T(8,128)(2,1)S(1)}, bf16[320,512]{1,0:T(8,128)(2,1)S(1)}, u32[]{:S(2)}, u32[]{:S(2)}) collective-permute-start(bf16[320,512]{1,0:T(8,128)(2,1)S(1)} %collective-permute-done.refs_2_), channel_id=1, source_target_pairs={{0,2},{1,3},{2,4},{3,5},{4,6},{5,7},{6,0},{7,1},{8,10},{9,11},{10,... | collective-permute-start | bytes 983048 | tf_op jit(solution)/shard_map/ppermute | solution.py:438
  11.9 9.5 %collective-permute-start.3 = (bf16[320,512]{1,0:T(8,128)(2,1)}, bf16[320,512]{1,0:T(8,128)(2,1)S(1)}, u32[]{:S(2)}, u32[]{:S(2)}) collective-permute-start(bf16[320,512]{1,0:T(8,128)(2,1)} %bitcast.25), channel_id=1, source_target_pairs={{0,6},{1,7},{2,0},{3,1},{4,2},{5,3},{6,4},{7,5},{8,14},{9,15},{10,... | collective-permute-start | bytes 983048 | tf_op jit(solution)/shard_map/ppermute | solution.py:438
  14.8 9.7 %collective-permute-start.6 = (bf16[320,512]{1,0:T(8,128)(2,1)}, bf16[320,512]{1,0:T(8,128)(2,1)S(1)}, u32[]{:S(2)}, u32[]{:S(2)}) collective-permute-start(bf16[320,512]{1,0:T(8,128)(2,1)} %bitcast.23), channel_id=1, source_target_pairs={{0,1},{1,0},{2,3},{3,2},{4,5},{5,4},{6,7},{7,6},{8,9},{9,8},{10,11... | collective-permute-start | bytes 983048 | tf_op jit(solution)/shard_map/ppermute | solution.py:441
  14.8 9.7 %collective-permute-start.7 = (bf16[320,512]{1,0:T(8,128)(2,1)S(1)}, bf16[320,512]{1,0:T(8,128)(2,1)S(1)}, u32[]{:S(2)}, u32[]{:S(2)}) collective-permute-start(bf16[320,512]{1,0:T(8,128)(2,1)S(1)} %collective-permute-done.refs_2_), channel_id=1, source_target_pairs={{0,1},{1,0},{2,3},{3,2},{4,5},{5,4},{6,7},{7,6},{8,9},{9,8},{10,11... | collective-permute-start | bytes 983048 | tf_op jit(solution)/shard_map/ppermute | solution.py:441
  15.3 9.3 %collective-permute-start.8 = (bf16[320,512]{1,0:T(8,128)(2,1)S(1)}, bf16[320,512]{1,0:T(8,128)(2,1)S(1)}, u32[]{:S(2)}, u32[]{:S(2)}) collective-permute-start(bf16[320,512]{1,0:T(8,128)(2,1)S(1)} %collective-permute-done.5.refs_3_), channel_id=1, source_target_pairs={{0,1},{1,0},{2,3},{3,2},{4,5},{5,4},{6,7},{7,6},{8,9},{9,8},{10,11... | collective-permute-start | bytes 983048 | tf_op jit(solution)/shard_map/ppermute | solution.py:441
  21.4 3.8 %collective-permute-start.9 = (bf16[320,512]{1,0:T(8,128)(2,1)S(1)}, bf16[320,512]{1,0:T(8,128)(2,1)S(1)}, u32[]{:S(2)}, u32[]{:S(2)}) collective-permute-start(bf16[320,512]{1,0:T(8,128)(2,1)S(1)} %collective-permute-done.1.refs_4_), channel_id=1, source_target_pairs={{0,1},{1,0},{2,3},{3,2},{4,5},{5,4},{6,7},{7,6},{8,9},{9,8},{10,11... | collective-permute-start | bytes 983048 | tf_op jit(solution)/shard_map/ppermute | solution.py:441
  21.4 11.0 %collective-permute-start.4 = (bf16[320,512]{1,0:T(8,128)(2,1)S(1)}, bf16[320,512]{1,0:T(8,128)(2,1)S(1)}, u32[]{:S(2)}, u32[]{:S(2)}) collective-permute-start(bf16[320,512]{1,0:T(8,128)(2,1)S(1)} %collective-permute-done.3.refs_3_), channel_id=1, source_target_pairs={{0,6},{1,7},{2,0},{3,1},{4,2},{5,3},{6,4},{7,5},{8,14},{9,15},{10,... | collective-permute-start | bytes 983048 | tf_op jit(solution)/shard_map/ppermute | solution.py:438
  24.5 8.5 %collective-permute-start.2 = (bf16[320,512]{1,0:T(8,128)(2,1)}, bf16[320,512]{1,0:T(8,128)(2,1)S(1)}, u32[]{:S(2)}, u32[]{:S(2)}) collective-permute-start(bf16[320,512]{1,0:T(8,128)(2,1)} %bitcast.26), channel_id=1, source_target_pairs={{0,2},{1,3},{2,4},{3,5},{4,6},{5,7},{6,0},{7,1},{8,10},{9,11},{10,... | collective-permute-start | bytes 983048 | tf_op jit(solution)/shard_map/ppermute | solution.py:438
  24.6 9.1 %collective-permute-start.10 = (bf16[320,512]{1,0:T(8,128)(2,1)}, bf16[320,512]{1,0:T(8,128)(2,1)S(1)}, u32[]{:S(2)}, u32[]{:S(2)}) collective-permute-start(bf16[320,512]{1,0:T(8,128)(2,1)} %bitcast.27), channel_id=1, source_target_pairs={{0,1},{1,0},{2,3},{3,2},{4,5},{5,4},{6,7},{7,6},{8,9},{9,8},{10,11... | collective-permute-start | bytes 983048 | tf_op jit(solution)/shard_map/ppermute | solution.py:441
  24.7 9.0 %collective-permute-start.12 = (bf16[320,512]{1,0:T(8,128)(2,1)S(1)}, bf16[320,512]{1,0:T(8,128)(2,1)S(1)}, u32[]{:S(2)}, u32[]{:S(2)}) collective-permute-start(bf16[320,512]{1,0:T(8,128)(2,1)S(1)} %collective-permute-done.3.refs_3_), channel_id=1, source_target_pairs={{0,1},{1,0},{2,3},{3,2},{4,5},{5,4},{6,7},{7,6},{8,9},{9,8},{10,11... | collective-permute-start | bytes 983048 | tf_op jit(solution)/shard_map/ppermute | solution.py:441
  33.1 1.6 %collective-permute-start.11 = (bf16[320,512]{1,0:T(8,128)(2,1)S(1)}, bf16[320,512]{1,0:T(8,128)(2,1)S(1)}, u32[]{:S(2)}, u32[]{:S(2)}) collective-permute-start(bf16[320,512]{1,0:T(8,128)(2,1)S(1)} %collective-permute-done.2.refs_2_), channel_id=1, source_target_pairs={{0,1},{1,0},{2,3},{3,2},{4,5},{5,4},{6,7},{7,6},{8,9},{9,8},{10,11... | collective-permute-start | bytes 983048 | tf_op jit(solution)/shard_map/ppermute | solution.py:441
  33.1 2.1 %collective-permute-start.13 = (bf16[320,512]{1,0:T(8,128)(2,1)S(1)}, bf16[320,512]{1,0:T(8,128)(2,1)S(1)}, u32[]{:S(2)}, u32[]{:S(2)}) collective-permute-start(bf16[320,512]{1,0:T(8,128)(2,1)S(1)} %collective-permute-done.4.refs_4_), channel_id=1, source_target_pairs={{0,1},{1,0},{2,3},{3,2},{4,5},{5,4},{6,7},{7,6},{8,9},{9,8},{10,11... | collective-permute-start | bytes 983048 | tf_op jit(solution)/shard_map/ppermute | solution.py:441
  33.6 12.9 %copy-start.4 = (f32[80,512]{1,0:T(8,128)S(1)}, f32[80,512]{1,0:T(8,128)}, u32[]{:S(2)}) copy-start(f32[80,512]{1,0:T(8,128)} %get-tuple-element.48.refs_4_.refs_7_) | copy-start | bytes 491524
  33.6 12.9 %copy-start.5 = (f32[8,640]{1,0:T(8,128)S(1)}, f32[8,640]{1,0:T(8,128)}, u32[]{:S(2)}) copy-start(f32[8,640]{1,0:T(8,128)} %get-tuple-element.49.refs_5_.refs_8_) | copy-start | bytes 61444
  33.6 12.9 %copy-start.7 = (bf16[512,896]{1,0:T(8,128)(2,1)S(1)}, bf16[512,896]{1,0:T(8,128)(2,1)}, u32[]{:S(2)}) copy-start(bf16[512,896]{1,0:T(8,128)(2,1)} %shard_map.124.refs_12_.refs_0_) | copy-start | bytes 2752516
  33.6 12.9 %copy-start.9 = (f32[8,128]{1,0:T(8,128)S(1)}, f32[8,128]{1,0:T(8,128)}, u32[]{:S(2)}) copy-start(f32[8,128]{1,0:T(8,128)} %get-tuple-element.50.refs_6_) | copy-start | bytes 12292
  42.6 9.4 %collective-permute-start.14 = (bf16[16,896]{1,0:T(8,128)(2,1)}, bf16[16,896]{1,0:T(8,128)(2,1)S(1)}, u32[]{:S(2)}, u32[]{:S(2)}) collective-permute-start(bf16[16,896]{1,0:T(8,128)(2,1)} %get-tuple-element.47.refs_2_), channel_id=1, source_target_pairs={{0,8},{8,16},{16,24},{24,32},{32,40},{40,48},{48,56},{56,64},{64,7... | collective-permute-start | bytes 86024 | tf_op jit(solution)/shard_map/ppermute | solution.py:500
  56.2 25.5 %all-to-all-start = ((bf16[32,8,768]{2,1,0:T(8,128)(2,1)}), bf16[32,8,768]{2,1,0:T(8,128)(2,1)}, u32[]{:S(2)}, u32[]{:S(2)}) async-start(bf16[32,8,768]{2,1,0:T(8,128)(2,1)} %bitcast.16), calls=%async_computation | async-start | bytes 786432 | tf_op jit(solution)/shard_map/all_to_all | solution.py:445
  70.9 17.8 %copy-start.27 = (f32[10]{0:T(128)S(1)}, f32[10]{0:T(128)}, u32[]{:S(2)}) copy-start(f32[10]{0:T(128)} %param.20) | copy-start | bytes 124
  73.6 38.1 %collective-permute-start.15 = (bf16[1280,640]{1,0:T(8,128)(2,1)}, bf16[1280,640]{1,0:T(8,128)(2,1)S(1)}, u32[]{:S(2)}, u32[]{:S(2)}) collective-permute-start(bf16[1280,640]{1,0:T(8,128)(2,1)} %get-tuple-element.64), channel_id=1, source_target_pairs={{0,1},{1,0},{2,3},{3,2},{4,5},{5,4},{6,7},{7,6},{8,9},{9,8},{10,11... | collective-permute-start | bytes 4915208 | tf_op jit(solution)/shard_map/ppermute | solution.py:441
  84.0 18.0 %all-to-all-start.1 = ((bf16[32,8,640]{2,1,0:T(8,128)(2,1)}), bf16[32,8,640]{2,1,0:T(8,128)(2,1)S(1)}, u32[]{:S(2)}, u32[]{:S(2)}) async-start(bf16[32,8,640]{2,1,0:T(8,128)(2,1)} %bitcast.9), calls=%async_computation.1 | async-start | bytes 655360 | tf_op jit(solution)/shard_map/all_to_all | solution.py:445
  107.7 4.1 %collective-permute-start.20 = (bf16[640,512]{1,0:T(8,128)(2,1)}, bf16[640,512]{1,0:T(8,128)(2,1)S(1)}, u32[]{:S(2)}, u32[]{:S(2)}) collective-permute-start(bf16[640,512]{1,0:T(8,128)(2,1)} %get-tuple-element.69.refs_1_), channel_id=1, source_target_pairs={{0,1},{1,0},{2,3},{3,2},{4,5},{5,4},{6,7},{7,6},{8,9},{9,8},{10,11... | collective-permute-start | bytes 1966088 | tf_op jit(solution)/shard_map/ppermute | solution.py:441
  107.8 7.8 %collective-permute-start.16 = (bf16[640,512]{1,0:T(8,128)(2,1)}, bf16[640,512]{1,0:T(8,128)(2,1)S(1)}, u32[]{:S(2)}, u32[]{:S(2)}) collective-permute-start(bf16[640,512]{1,0:T(8,128)(2,1)} %get-tuple-element.63.refs_1_), channel_id=1, source_target_pairs={{0,1},{1,0},{2,3},{3,2},{4,5},{5,4},{6,7},{7,6},{8,9},{9,8},{10,11... | collective-permute-start | bytes 1966088 | tf_op jit(solution)/shard_map/ppermute | solution.py:441
  112.9 10.7 %collective-permute-start.21 = (bf16[320,512]{1,0:T(8,128)(2,1)S(1)}, bf16[320,512]{1,0:T(8,128)(2,1)S(1)}, u32[]{:S(2)}, u32[]{:S(2)}) collective-permute-start(bf16[320,512]{1,0:T(8,128)(2,1)S(1)} %get-tuple-element.72), channel_id=1, source_target_pairs={{0,6},{1,7},{2,0},{3,1},{4,2},{5,3},{6,4},{7,5},{8,14},{9,15},{10,... | collective-permute-start | bytes 983048 | tf_op jit(solution)/shard_map/ppermute | solution.py:438
  116.8 11.9 %collective-permute-start.17 = (bf16[320,512]{1,0:T(8,128)(2,1)S(1)}, bf16[320,512]{1,0:T(8,128)(2,1)S(1)}, u32[]{:S(2)}, u32[]{:S(2)}) collective-permute-start(bf16[320,512]{1,0:T(8,128)(2,1)S(1)} %get-tuple-element.67), channel_id=1, source_target_pairs={{0,2},{1,3},{2,4},{3,5},{4,6},{5,7},{6,0},{7,1},{8,10},{9,11},{10,... | collective-permute-start | bytes 983048 | tf_op jit(solution)/shard_map/ppermute | solution.py:438
  116.9 18.8 %collective-permute-start.23 = (bf16[320,512]{1,0:T(8,128)(2,1)S(1)}, bf16[320,512]{1,0:T(8,128)(2,1)S(1)}, u32[]{:S(2)}, u32[]{:S(2)}) collective-permute-start(bf16[320,512]{1,0:T(8,128)(2,1)S(1)} %get-tuple-element.73), channel_id=1, source_target_pairs={{0,2},{1,3},{2,4},{3,5},{4,6},{5,7},{6,0},{7,1},{8,10},{9,11},{10,... | collective-permute-start | bytes 983048 | tf_op jit(solution)/shard_map/ppermute | solution.py:438
  117.0 20.8 %collective-permute-start.19 = (bf16[320,512]{1,0:T(8,128)(2,1)S(1)}, bf16[320,512]{1,0:T(8,128)(2,1)S(1)}, u32[]{:S(2)}, u32[]{:S(2)}) collective-permute-start(bf16[320,512]{1,0:T(8,128)(2,1)S(1)} %get-tuple-element.68), channel_id=1, source_target_pairs={{0,6},{1,7},{2,0},{3,1},{4,2},{5,3},{6,4},{7,5},{8,14},{9,15},{10,... | collective-permute-start | bytes 983048 | tf_op jit(solution)/shard_map/ppermute | solution.py:438
  123.7 13.1 %collective-permute-start.22 = (bf16[320,512]{1,0:T(8,128)(2,1)S(1)}, bf16[320,512]{1,0:T(8,128)(2,1)S(1)}, u32[]{:S(2)}, u32[]{:S(2)}) collective-permute-start(bf16[320,512]{1,0:T(8,128)(2,1)S(1)} %shard_map.137), channel_id=1, source_target_pairs={{0,6},{1,7},{2,0},{3,1},{4,2},{5,3},{6,4},{7,5},{8,14},{9,15},{10,... | collective-permute-start | bytes 983048 | tf_op jit(solution)/shard_map/ppermute | solution.py:438
  128.7 12.8 %collective-permute-start.18 = (bf16[320,512]{1,0:T(8,128)(2,1)S(1)}, bf16[320,512]{1,0:T(8,128)(2,1)S(1)}, u32[]{:S(2)}, u32[]{:S(2)}) collective-permute-start(bf16[320,512]{1,0:T(8,128)(2,1)S(1)} %shard_map.133), channel_id=1, source_target_pairs={{0,2},{1,3},{2,4},{3,5},{4,6},{5,7},{6,0},{7,1},{8,10},{9,11},{10,... | collective-permute-start | bytes 983048 | tf_op jit(solution)/shard_map/ppermute | solution.py:438
  (22 other events, 65.8 us)

commit v4 on v3

--- a/solution.py
+++ b/solution.py
@@ -10,7 +10,7 @@
 HEAD_DIM = 64
 SPAN = 256
 MIB = 1 << 20
-BIG = 56
+BIG = 24
 CHIPS = 4
 AROUND = (0, CHIPS - 1, 1, 2)
 BF16 = jnp.bfloat16
@@ -26,7 +26,7 @@
     return lax.dot_general(a, b, dims, precision=precision, preferred_element_type=F32)
 
 
-def call(body, out, scratch=(), smem=(), near=(), held=(), pinned=(), count=0, work=(0, 0), limit=16):
+def call(body, out, scratch=(), smem=(), near=(), held=(), loose=(), pinned=(), count=0, work=(0, 0), limit=16):
     outs = list(out)
     n_out, n_scratch = len(outs), len(scratch)
     far = [i for i in range(count) if i not in smem and i not in held and i not in near]
@@ -57,11 +57,17 @@
             copy.wait()
 
     def space(i):
-        return pltpu.SMEM if i in smem else pltpu.VMEM if i in near else pltpu.HBM
+        if i in smem:
+            return pltpu.SMEM
+        return pltpu.VMEM if i in near else pl.ANY if i in loose else pltpu.HBM
 
     def run(*args):
         assert len(args) == count
         buffers = [pltpu.VMEM(args[i].shape, args[i].dtype) for i in far]
+        args = [
+            pltpu.with_memory_space_constraint(v, pltpu.HBM) if space(i) is pltpu.HBM else v
+            for i, v in enumerate(args)
+        ]
         buffers += [pltpu.VMEM(outs[i].shape, outs[i].dtype) for i in far_out]
         if buffers:
             buffers.append(pltpu.SemaphoreType.DMA((len(buffers),)))
@@ -221,24 +227,25 @@
     edge[...] = jnp.concatenate(ends, 0).astype(BF16)
 
 
-def block_body(b, projected, projected_dot, before, taps, table, vec, tail, *refs):
+def block_body(b, projected, projected_dot, taps, table, vec, tail, *refs):
     if b == 0:
-        state1, state1_dot, mixed, mixed_dot, state, state_dot, message = refs[:7]
-        refs = refs[7:]
+        before, state1, state1_dot, mixed, mixed_dot, state, state_dot, message = refs[:8]
+        refs = refs[8:]
     else:
         mixed, mixed_dot, state, state_dot = refs[:4]
         refs = refs[4:]
     ext, ext_dot, gate, rows, rows_dot, scaled = refs
     at = slice(b * SPAN, (b + 1) * SPAN)
     for i, (source, out) in enumerate(((projected, ext), (projected_dot, ext_dot))):
-        ahead = before[...].astype(F32)[8 * i : 8 * i + 8]
         if b > 0:
             ahead = source[b * SPAN - 16 : b * SPAN, :].astype(F32)[8:]
+        else:
+            ahead = before[...].astype(F32)[8 * i : 8 * i + 8]
         out[0:8, :] = ahead
         out[8:, :] = source[at, :].astype(F32)
 
     def store(where, lanes, v):
-        sig = 1.0 / (1.0 + jnp.exp(-v))
+        sig = 0.5 + 0.5 * jnp.tanh(0.5 * v)
         rows[where, lanes] = (v * sig).astype(BF16)
         gate[where, lanes] = sig * (1.0 + v * (1.0 - sig))
 
@@ -261,7 +268,7 @@
     writer = mixed[width : width + 128, :]
     writer_dot = mixed_dot[width : width + 128, :]
     own = mm(writer, scaled[:, SPAN:], NT)
-    own_dot = mm(writer, scaled[:, :SPAN], NT) + mm(writer_dot, scaled[:, SPAN:], NT)
+    own_dot = mm(jnp.concatenate([writer, writer_dot], 1), scaled[...], NT)
     state[...] = own
     state_dot[...] = own_dot
     if b == 0:
@@ -286,7 +293,7 @@
         writer, reader = mixed[width : width + state, :], mixed[width + state :, :]
         writer_dot, reader_dot = mixed_dot[width : width + state, :], mixed_dot[width + state :, :]
         sc[...] = mm(writer, reader, TN)
-        scd[...] = mm(writer_dot, reader, TN) + mm(writer, reader_dot, TN)
+        scd[...] = mm(jnp.concatenate([writer_dot, writer], 0), jnp.concatenate([reader, reader_dot], 0), TN)
         for h in range(width // HEAD_DIM):
             rows = slice(h * HEAD_DIM, (h + 1) * HEAD_DIM)
             diff = table[CUM + h : CUM + h + 1, lanes] - columns[lanes, h : h + 1]
@@ -382,9 +389,9 @@
     for b in range(2):
         lanes = slice(b * SPAN, (b + 1) * SPAN)
         reader, reader_dot = readers[:, lanes], readers_dot[:, lanes]
-        rounded = entry.astype(BF16)
-        read = mm(rounded, reader, TN)
-        read_dot = mm(rounded, reader_dot, TN) + mm(entry_dot.astype(BF16), reader, TN)
+        rounded = jnp.concatenate([entry.astype(BF16), entry_dot.astype(BF16)], 0)
+        read = mm(rounded[: entry.shape[0]], reader, TN)
+        read_dot = mm(rounded, jnp.concatenate([reader_dot, reader], 0), TN)
         for h in range(width // HEAD_DIM):
             rows = slice(h * HEAD_DIM, (h + 1) * HEAD_DIM)
             e = table[CUM_EXP + h : CUM_EXP + h + 1, lanes]
@@ -477,6 +484,7 @@
         [tokens_by],
         [*full, pltpu.SemaphoreType.DMA((14,))],
         held=tuple(range(1, 12)),
+        loose=tuple(range(1, 9)),
         count=12,
         smem=(0,),
         work=work,
@@ -491,7 +499,9 @@
         tangent_body,
         [tokens_by, shape((16, channels), BF16)],
         [*full, pltpu.VMEM((16, channels), BF16), pltpu.SemaphoreType.DMA((15,))],
+        near=(12,),
         held=tuple(range(1, 13)),
+        loose=tuple(range(1, 9)),
         count=13,
         smem=(0,),
         work=work,
@@ -501,8 +511,8 @@
     mix = shape((channels, SPAN), BF16)
     state = shape((state_len, width), F32)
 
-    def block(b, out, before, *more):
-        args = (projected, projected_dot, before, taps, table, vec, tail, *more)
+    def block(b, out, *more):
+        args = (projected, projected_dot, taps, table, vec, tail, *more)
         return call(
             functools.partial(block_body, b),
             [mix, mix, state, state, *out],
@@ -517,7 +527,7 @@
             limit=20,
         )(*args)
 
-    mixed1, mixed1_dot, state1, state1_dot = block(1, [], edge)
+    mixed1, mixed1_dot, state1, state1_dot = block(1, [])
     mixed0, mixed0_dot, state0, state0_dot, message = block(
         0, [shape((2 * state_len, width + 128), BF16)], before, state1, state1_dot
     )

time: 143 us -> 136 us (0.951)
  local copies, waits for them, and re-layouts: 11.4 us -> 7.46 us
  Pallas kernels: 43.4 us -> 41.2 us
    unnamed x58 -> x18, local copies, waits for them, and re-layouts: 10.8 us -> 6.92 us
    pallas_call x17, Pallas kernels: 43.4 us -> 41.2 us  [run(): pl.pallas_call(kernel, out_shape=[pltpu.HBM(v.shape, v.dtype) if i in far...]
  transfers between devices with their start and end apart: 26 -> 26, of which waited for: 12 -> 12; matrix products, arithmetic and copies ran while one was open for 4% -> 5% of each run, Pallas kernels for 22% -> 22%
where the time goes in v4:
time: 136 us
  waiting for transfers between devices  44.9 us (33%)
  Pallas kernels  41.2 us (30%)
  starting transfers between devices  39.7 us (29%)
  local copies, waits for them, and re-layouts  7.46 us (5%)
  other arithmetic  1.41 us (1%)
    pallas_call x17, Pallas kernels, run(): pl.pallas_call(kernel, out_shape=[pltpu.HBM(v.shape, v.dtype) if i in far...  41.2 us
    ppermute x12, waiting for transfers between devices, along(): return lax.ppermute(values, 'head', route)  28.2 us
    ppermute x12, starting transfers between devices, along(): return lax.ppermute(values, 'head', route)  18.3 us
    all_to_all x2, starting transfers between devices, exchange(): return lax.all_to_all(blocks, 'ctx', 0, 0).reshape(values.shape)  15.3 us
    all_to_all x2, waiting for transfers between devices, exchange(): return lax.all_to_all(blocks, 'ctx', 0, 0).reshape(values.shape)  15.1 us
    unnamed x18, local copies, waits for them, and re-layouts  6.92 us
    ppermute x1, starting transfers between devices, on_device(): before = lax.ppermute(edge, 'ctx', [(i, i + 1) for i in range(n_ctx - 1)])  3.83 us
  transfers between devices with their start and end apart: 26, of which 12 were waited for; matrix products, arithmetic and copies ran while one was open for 5% of the time, Pallas kernels for 22%

profile of v4, /device:TPU:32, one launch (start us, length us, event | category | flops | bytes accessed | tf_op | source)
XLA Modules:
  0.0 135.5 jit_solution(13182075105316885631)
XLA Ops:
  0.6 1.6 %collective-permute-start = (bf16[320,512]{1,0:T(8,128)(2,1)}, bf16[320,512]{1,0:T(8,128)(2,1)S(1)}, u32[]{:S(2)}, u32[]{:S(2)}) collective-permute-start(bf16[320,512]{1,0:T(8,128)(2,1)} %bitcast.16), channel_id=1, source_target_pairs={{0,2},{1,3},{2,4},{3,5},{4,6},{5,7},{6,0},{7,1},{8,10},{9,11},{10,... | collective-permute-start | bytes 983048 | tf_op jit(solution)/shard_map/ppermute | solution.py:445
  2.2 1.7 %collective-permute-start.5 = (bf16[320,512]{1,0:T(8,128)(2,1)}, bf16[320,512]{1,0:T(8,128)(2,1)S(1)}, u32[]{:S(2)}, u32[]{:S(2)}) collective-permute-start(bf16[320,512]{1,0:T(8,128)(2,1)} %bitcast.17), channel_id=1, source_target_pairs={{0,6},{1,7},{2,0},{3,1},{4,2},{5,3},{6,4},{7,5},{8,14},{9,15},{10,... | collective-permute-start | bytes 983048 | tf_op jit(solution)/shard_map/ppermute | solution.py:445
  3.9 1.4 %select_maximum_fusion.refs_0_ = f32[32,512]{1,0:T(8,128)} fusion(f32[10,512]{1,0:T(8,128)} %bitcast.27, f32[10,512]{1,0:T(8,128)} %bitcast.28), kind=kLoop, calls=%fused_computation | loop fusion | flops 81920 | bytes 106496 | tf_op jit(solution)/shard_map/concatenate | solution.py:459
  5.4 2.5 %shard_map.123 = (f32[80,512]{1,0:T(8,128)}, f32[512,32]{1,0:T(8,128)}, f32[8,640]{1,0:T(8,128)}, f32[8,128]{1,0:T(8,128)}) custom-call(f32[32,512]{1,0:T(8,128)} %select_maximum_fusion.refs_0_), custom_call_target="tpu_custom_call" | custom-call | flops 100000000 | bytes 1000000 | tf_op jit(solution)/shard_map/pallas_call | solution.py:74
  7.9 3.7 %collective-permute-done.refs_2_ = bf16[320,512]{1,0:T(8,128)(2,1)S(1)} collective-permute-done((bf16[320,512]{1,0:T(8,128)(2,1)}, bf16[320,512]{1,0:T(8,128)(2,1)S(1)}, u32[]{:S(2)}, u32[]{:S(2)}) %collective-permute-start) | collective-permute-done | bytes 327712 | tf_op jit(solution)/shard_map/ppermute | solution.py:445
  11.9 3.0 %collective-permute-start.3 = (bf16[320,512]{1,0:T(8,128)(2,1)}, bf16[320,512]{1,0:T(8,128)(2,1)S(1)}, u32[]{:S(2)}, u32[]{:S(2)}) collective-permute-start(bf16[320,512]{1,0:T(8,128)(2,1)} %bitcast.20), channel_id=1, source_target_pairs={{0,6},{1,7},{2,0},{3,1},{4,2},{5,3},{6,4},{7,5},{8,14},{9,15},{10,... | collective-permute-start | bytes 983048 | tf_op jit(solution)/shard_map/ppermute | solution.py:445
  15.3 6.0 %collective-permute-done.1.refs_4_ = bf16[320,512]{1,0:T(8,128)(2,1)S(1)} collective-permute-done((bf16[320,512]{1,0:T(8,128)(2,1)S(1)}, bf16[320,512]{1,0:T(8,128)(2,1)S(1)}, u32[]{:S(2)}, u32[]{:S(2)}) %collective-permute-start.1) | collective-permute-done | bytes 327712 | tf_op jit(solution)/shard_map/ppermute | solution.py:445
  21.4 3.2 %collective-permute-start.4 = (bf16[320,512]{1,0:T(8,128)(2,1)S(1)}, bf16[320,512]{1,0:T(8,128)(2,1)S(1)}, u32[]{:S(2)}, u32[]{:S(2)}) collective-permute-start(bf16[320,512]{1,0:T(8,128)(2,1)S(1)} %collective-permute-done.3.refs_3_), channel_id=1, source_target_pairs={{0,6},{1,7},{2,0},{3,1},{4,2},{5,3},{6,4},{7,5},{8,14},{9,15},{10,... | collective-permute-start | bytes 983048 | tf_op jit(solution)/shard_map/ppermute | solution.py:445
  26.1 5.5 %shard_map.124.refs_12_.refs_0_ = bf16[512,896]{1,0:T(8,128)(2,1)S(1)} custom-call(s32[1]{0:T(128)} %bitcast.refs_0_, bf16[320,512]{1,0:T(8,128)(2,1)S(1)} %bitcast.19, bf16[320,512]{1,0:T(8,128)(2,1)S(1)} %collective-permute-done.refs_2_, bf16[320,512]{1,0:T(8,128)(2,1)S(1)} %collective-permute-done.5.refs_3_, ...), custom_call_target="tpu_custom_call" | custom-call | flops 2348810240 | bytes 12582912 | tf_op jit(solution)/shard_map/pallas_call | solution.py:74
  31.6 1.4 %collective-permute-done.2.refs_2_ = bf16[320,512]{1,0:T(8,128)(2,1)S(1)} collective-permute-done((bf16[320,512]{1,0:T(8,128)(2,1)}, bf16[320,512]{1,0:T(8,128)(2,1)S(1)}, u32[]{:S(2)}, u32[]{:S(2)}) %collective-permute-start.2) | collective-permute-done | bytes 327712 | tf_op jit(solution)/shard_map/ppermute | solution.py:445
  35.2 5.6 %shard_map.125 = (bf16[512,896]{1,0:T(8,128)(2,1)S(1)}, bf16[16,896]{1,0:T(8,128)(2,1)S(1)}) custom-call(s32[1]{0:T(128)} %bitcast.refs_0_, bf16[320,512]{1,0:T(8,128)(2,1)S(1)} %bitcast.23, bf16[320,512]{1,0:T(8,128)(2,1)S(1)} %collective-permute-done.2.refs_2_, bf16[320,512]{1,0:T(8,128)(2,1)S(1)} %collective-permute-done.3.refs_3_, ...), custom_call_target="tpu_custom_call" | custom-call | flops 2348810240 | bytes 12582912 | tf_op jit(solution)/shard_map/pallas_call | solution.py:74
  40.7 3.8 %collective-permute-start.14 = (bf16[16,896]{1,0:T(8,128)(2,1)S(1)}, bf16[16,896]{1,0:T(8,128)(2,1)S(1)}, u32[]{:S(2)}, u32[]{:S(2)}) collective-permute-start(bf16[16,896]{1,0:T(8,128)(2,1)S(1)} %get-tuple-element.50), channel_id=1, source_target_pairs={{0,8},{8,16},{16,24},{24,32},{32,40},{40,48},{48,56},{56,64},{64,7... | collective-permute-start | bytes 86024 | tf_op jit(solution)/shard_map/ppermute | solution.py:510
  44.6 4.1 %shard_map.126 = (bf16[896,256]{1,0:T(8,128)(2,1)}, bf16[896,256]{1,0:T(8,128)(2,1)}, f32[128,640]{1,0:T(8,128)S(1)}, f32[128,640]{1,0:T(8,128)S(1)}) custom-call(bf16[512,896]{1,0:T(8,128)(2,1)S(1)} %shard_map.124.refs_12_.refs_0_, bf16[512,896]{1,0:T(8,128)(2,1)S(1)} %get-tuple-element.46.refs_1_, f32[4,896]{1,0:T(4,128)S(1)} %constant_dynamic-update-slice_fusion.refs_2_, ...), custom_call_target="tpu_custom_call" | custom-call | flops 1000000000 | bytes 8388608 | tf_op jit(solution)/shard_map/pallas_call | solution.py:74
  49.3 4.7 %shard_map.127 = (bf16[896,256]{1,0:T(8,128)(2,1)}, bf16[896,256]{1,0:T(8,128)(2,1)}, f32[128,640]{1,0:T(8,128)}, f32[128,640]{1,0:T(8,128)}, bf16[256,768]{1,0:T(8,128)(2,1)}) custom-call(bf16[512,896]{1,0:T(8,128)(2,1)S(1)} %shard_map.124.refs_12_.refs_0_, bf16[512,896]{1,0:T(8,128)(2,1)S(1)} %get-tuple-element.46.refs_1_, ...), custom_call_target="tpu_custom_call" | custom-call | flops 1000000000 | bytes 8388608 | tf_op jit(solution)/shard_map/pallas_call | solution.py:74
  54.0 10.5 %all-to-all-start = ((bf16[32,8,768]{2,1,0:T(8,128)(2,1)}), bf16[32,8,768]{2,1,0:T(8,128)(2,1)}, u32[]{:S(2)}, u32[]{:S(2)}) async-start(bf16[32,8,768]{2,1,0:T(8,128)(2,1)} %bitcast.24), calls=%async_computation | async-start | bytes 786432 | tf_op jit(solution)/shard_map/all_to_all | solution.py:452
  64.5 4.2 %copy.13 = bf16[640,2560]{0,1:T(8,128)(2,1)S(1)} copy(bf16[640,2560]{1,0:T(8,128)(2,1)} %param.21) | data formatting | bytes 6553600 | tf_op args[10]
  68.7 1.5 %shard_map.122 = (bf16[1280,640]{1,0:T(8,128)(2,1)S(1)}, bf16[1280,640]{1,0:T(8,128)(2,1)}) custom-call(s32[1]{0:T(128)} %bitcast.refs_0_, bf16[2560,640]{1,0:T(8,128)(2,1)S(1)} %bitcast.14), custom_call_target="tpu_custom_call" | custom-call | flops 1000000 | bytes 6291456 | tf_op jit(solution)/shard_map/pallas_call | solution.py:74
  71.4 8.1 %all-to-all-done = bf16[32,8,768]{2,1,0:T(8,128)(2,1)} async-done(((bf16[32,8,768]{2,1,0:T(8,128)(2,1)}), bf16[32,8,768]{2,1,0:T(8,128)(2,1)}, u32[]{:S(2)}, u32[]{:S(2)}) %all-to-all-start) | async-done | bytes 393248 | tf_op jit(solution)/shard_map/all_to_all | solution.py:452
  79.5 2.3 %shard_map.128 = bf16[256,640]{1,0:T(8,128)(2,1)} custom-call(s32[1]{0:T(128)} %bitcast.2.refs_0_, bf16[256,768]{1,0:T(8,128)(2,1)} %bitcast.8.refs_1_), custom_call_target="tpu_custom_call" | custom-call | flops 100000000 | bytes 1048576 | tf_op jit(solution)/shard_map/pallas_call | solution.py:74
  81.8 4.8 %all-to-all-start.1 = ((bf16[32,8,640]{2,1,0:T(8,128)(2,1)}), bf16[32,8,640]{2,1,0:T(8,128)(2,1)S(1)}, u32[]{:S(2)}, u32[]{:S(2)}) async-start(bf16[32,8,640]{2,1,0:T(8,128)(2,1)} %bitcast.9), calls=%async_computation.1 | async-start | bytes 655360 | tf_op jit(solution)/shard_map/all_to_all | solution.py:452
  87.1 5.7 %shard_map.129 = (f32[640,512]{1,0:T(8,128)}, f32[640,512]{1,0:T(8,128)}) custom-call(bf16[896,256]{1,0:T(8,128)(2,1)} %get-tuple-element.54.refs_0_.refs_1_, bf16[896,256]{1,0:T(8,128)(2,1)} %get-tuple-element.55.refs_1_.refs_2_, bf16[896,256]{1,0:T(8,128)(2,1)} %get-tuple-element.56.refs_2_.refs_3_, bf16[896,256]{1,0:T(8,128)(2,1)} %get-tuple-element.57.refs_3_.refs_4_, ...), custom_call_target="tpu_custom_call" | custom-call | flops 5000000000 | bytes 8388608 | tf_op jit(solution)/shard_map/pallas_call | solution.py:74
  92.8 7.0 %all-to-all-done.1 = bf16[32,8,640]{2,1,0:T(8,128)(2,1)S(1)} async-done(((bf16[32,8,640]{2,1,0:T(8,128)(2,1)}), bf16[32,8,640]{2,1,0:T(8,128)(2,1)S(1)}, u32[]{:S(2)}, u32[]{:S(2)}) %all-to-all-start.1) | async-done | bytes 327712 | tf_op jit(solution)/shard_map/all_to_all | solution.py:452
  99.8 2.8 %shard_map.130 = (bf16[640,512]{1,0:T(8,128)(2,1)S(1)}, bf16[640,512]{1,0:T(8,128)(2,1)S(1)}) custom-call(bf16[256,640]{1,0:T(8,128)(2,1)S(1)} %bitcast.15, bf16[896,256]{1,0:T(8,128)(2,1)} %get-tuple-element.54.refs_0_.refs_1_, bf16[896,256]{1,0:T(8,128)(2,1)} %get-tuple-element.55.refs_1_.refs_2_, bf16[896,256]{1,0:T(8,128)(2,1)} %get-tuple-element.56.refs_2_.refs_3_, ...), custom_call_target="tpu_custom_call" | custom-call | flops 1000000000 | bytes 6291456 | tf_op jit(solution)/shard_map/pallas_call | solution.py:74
  104.4 1.2 shard_map.131.refs_0_
  105.6 1.2 shard_map.136
  106.8 1.9 %collective-permute-start.21 = (bf16[320,512]{1,0:T(8,128)(2,1)S(1)}, bf16[320,512]{1,0:T(8,128)(2,1)S(1)}, u32[]{:S(2)}, u32[]{:S(2)}) collective-permute-start(bf16[320,512]{1,0:T(8,128)(2,1)S(1)} %get-tuple-element.72), channel_id=1, source_target_pairs={{0,6},{1,7},{2,0},{3,1},{4,2},{5,3},{6,4},{7,5},{8,14},{9,15},{10,... | collective-permute-start | bytes 983048 | tf_op jit(solution)/shard_map/ppermute | solution.py:445
  110.6 2.8 %collective-permute-start.19 = (bf16[320,512]{1,0:T(8,128)(2,1)S(1)}, bf16[320,512]{1,0:T(8,128)(2,1)S(1)}, u32[]{:S(2)}, u32[]{:S(2)}) collective-permute-start(bf16[320,512]{1,0:T(8,128)(2,1)S(1)} %get-tuple-element.68), channel_id=1, source_target_pairs={{0,6},{1,7},{2,0},{3,1},{4,2},{5,3},{6,4},{7,5},{8,14},{9,15},{10,... | collective-permute-start | bytes 983048 | tf_op jit(solution)/shard_map/ppermute | solution.py:445
  113.4 4.0 %collective-permute-done.21.refs_1_ = bf16[320,512]{1,0:T(8,128)(2,1)S(1)} collective-permute-done((bf16[320,512]{1,0:T(8,128)(2,1)S(1)}, bf16[320,512]{1,0:T(8,128)(2,1)S(1)}, u32[]{:S(2)}, u32[]{:S(2)}) %collective-permute-start.21) | collective-permute-done | bytes 327712 | tf_op jit(solution)/shard_map/ppermute | solution.py:445
  117.5 3.1 %collective-permute-start.22 = (bf16[320,512]{1,0:T(8,128)(2,1)S(1)}, bf16[320,512]{1,0:T(8,128)(2,1)S(1)}, u32[]{:S(2)}, u32[]{:S(2)}) collective-permute-start(bf16[320,512]{1,0:T(8,128)(2,1)S(1)} %shard_map.137), channel_id=1, source_target_pairs={{0,6},{1,7},{2,0},{3,1},{4,2},{5,3},{6,4},{7,5},{8,14},{9,15},{10,... | collective-permute-start | bytes 983048 | tf_op jit(solution)/shard_map/ppermute | solution.py:445
  121.9 6.9 %collective-permute-done.23.refs_2_ = bf16[320,512]{1,0:T(8,128)(2,1)S(1)} collective-permute-done((bf16[320,512]{1,0:T(8,128)(2,1)S(1)}, bf16[320,512]{1,0:T(8,128)(2,1)S(1)}, u32[]{:S(2)}, u32[]{:S(2)}) %collective-permute-start.23) | collective-permute-done | bytes 327712 | tf_op jit(solution)/shard_map/ppermute | solution.py:445
  128.8 1.8 %collective-permute-done.22.refs_1_ = bf16[320,512]{1,0:T(8,128)(2,1)S(1)} collective-permute-done((bf16[320,512]{1,0:T(8,128)(2,1)S(1)}, bf16[320,512]{1,0:T(8,128)(2,1)S(1)}, u32[]{:S(2)}, u32[]{:S(2)}) %collective-permute-start.22) | collective-permute-done | bytes 327712 | tf_op jit(solution)/shard_map/ppermute | solution.py:445
  131.5 3.2 %collective-permute-done.18.refs_1_ = bf16[320,512]{1,0:T(8,128)(2,1)S(1)} collective-permute-done((bf16[320,512]{1,0:T(8,128)(2,1)S(1)}, bf16[320,512]{1,0:T(8,128)(2,1)S(1)}, u32[]{:S(2)}, u32[]{:S(2)}) %collective-permute-start.18) | collective-permute-done | bytes 327712 | tf_op jit(solution)/shard_map/ppermute | solution.py:445
  (58 shorter events, 13.4 us)
Async XLA Ops:
  0.6 10.9 %collective-permute-start = (bf16[320,512]{1,0:T(8,128)(2,1)}, bf16[320,512]{1,0:T(8,128)(2,1)S(1)}, u32[]{:S(2)}, u32[]{:S(2)}) collective-permute-start(bf16[320,512]{1,0:T(8,128)(2,1)} %bitcast.16), channel_id=1, source_target_pairs={{0,2},{1,3},{2,4},{3,5},{4,6},{5,7},{6,0},{7,1},{8,10},{9,11},{10,... | collective-permute-start | bytes 983048 | tf_op jit(solution)/shard_map/ppermute | solution.py:445
  2.2 13.1 %collective-permute-start.5 = (bf16[320,512]{1,0:T(8,128)(2,1)}, bf16[320,512]{1,0:T(8,128)(2,1)S(1)}, u32[]{:S(2)}, u32[]{:S(2)}) collective-permute-start(bf16[320,512]{1,0:T(8,128)(2,1)} %bitcast.17), channel_id=1, source_target_pairs={{0,6},{1,7},{2,0},{3,1},{4,2},{5,3},{6,4},{7,5},{8,14},{9,15},{10,... | collective-permute-start | bytes 983048 | tf_op jit(solution)/shard_map/ppermute | solution.py:445
  11.6 9.8 %collective-permute-start.1 = (bf16[320,512]{1,0:T(8,128)(2,1)S(1)}, bf16[320,512]{1,0:T(8,128)(2,1)S(1)}, u32[]{:S(2)}, u32[]{:S(2)}) collective-permute-start(bf16[320,512]{1,0:T(8,128)(2,1)S(1)} %collective-permute-done.refs_2_), channel_id=1, source_target_pairs={{0,2},{1,3},{2,4},{3,5},{4,6},{5,7},{6,0},{7,1},{8,10},{9,11},{10,... | collective-permute-start | bytes 983048 | tf_op jit(solution)/shard_map/ppermute | solution.py:445
  11.9 9.5 %collective-permute-start.3 = (bf16[320,512]{1,0:T(8,128)(2,1)}, bf16[320,512]{1,0:T(8,128)(2,1)S(1)}, u32[]{:S(2)}, u32[]{:S(2)}) collective-permute-start(bf16[320,512]{1,0:T(8,128)(2,1)} %bitcast.20), channel_id=1, source_target_pairs={{0,6},{1,7},{2,0},{3,1},{4,2},{5,3},{6,4},{7,5},{8,14},{9,15},{10,... | collective-permute-start | bytes 983048 | tf_op jit(solution)/shard_map/ppermute | solution.py:445
  14.8 9.7 %collective-permute-start.6 = (bf16[320,512]{1,0:T(8,128)(2,1)}, bf16[320,512]{1,0:T(8,128)(2,1)S(1)}, u32[]{:S(2)}, u32[]{:S(2)}) collective-permute-start(bf16[320,512]{1,0:T(8,128)(2,1)} %bitcast.18), channel_id=1, source_target_pairs={{0,1},{1,0},{2,3},{3,2},{4,5},{5,4},{6,7},{7,6},{8,9},{9,8},{10,11... | collective-permute-start | bytes 983048 | tf_op jit(solution)/shard_map/ppermute | solution.py:448
  14.8 9.7 %collective-permute-start.7 = (bf16[320,512]{1,0:T(8,128)(2,1)S(1)}, bf16[320,512]{1,0:T(8,128)(2,1)S(1)}, u32[]{:S(2)}, u32[]{:S(2)}) collective-permute-start(bf16[320,512]{1,0:T(8,128)(2,1)S(1)} %collective-permute-done.refs_2_), channel_id=1, source_target_pairs={{0,1},{1,0},{2,3},{3,2},{4,5},{5,4},{6,7},{7,6},{8,9},{9,8},{10,11... | collective-permute-start | bytes 983048 | tf_op jit(solution)/shard_map/ppermute | solution.py:448
  15.3 9.3 %collective-permute-start.8 = (bf16[320,512]{1,0:T(8,128)(2,1)S(1)}, bf16[320,512]{1,0:T(8,128)(2,1)S(1)}, u32[]{:S(2)}, u32[]{:S(2)}) collective-permute-start(bf16[320,512]{1,0:T(8,128)(2,1)S(1)} %collective-permute-done.5.refs_3_), channel_id=1, source_target_pairs={{0,1},{1,0},{2,3},{3,2},{4,5},{5,4},{6,7},{7,6},{8,9},{9,8},{10,11... | collective-permute-start | bytes 983048 | tf_op jit(solution)/shard_map/ppermute | solution.py:448
  21.4 3.8 %collective-permute-start.9 = (bf16[320,512]{1,0:T(8,128)(2,1)S(1)}, bf16[320,512]{1,0:T(8,128)(2,1)S(1)}, u32[]{:S(2)}, u32[]{:S(2)}) collective-permute-start(bf16[320,512]{1,0:T(8,128)(2,1)S(1)} %collective-permute-done.1.refs_4_), channel_id=1, source_target_pairs={{0,1},{1,0},{2,3},{3,2},{4,5},{5,4},{6,7},{7,6},{8,9},{9,8},{10,11... | collective-permute-start | bytes 983048 | tf_op jit(solution)/shard_map/ppermute | solution.py:448
  21.4 10.3 %collective-permute-start.4 = (bf16[320,512]{1,0:T(8,128)(2,1)S(1)}, bf16[320,512]{1,0:T(8,128)(2,1)S(1)}, u32[]{:S(2)}, u32[]{:S(2)}) collective-permute-start(bf16[320,512]{1,0:T(8,128)(2,1)S(1)} %collective-permute-done.3.refs_3_), channel_id=1, source_target_pairs={{0,6},{1,7},{2,0},{3,1},{4,2},{5,3},{6,4},{7,5},{8,14},{9,15},{10,... | collective-permute-start | bytes 983048 | tf_op jit(solution)/shard_map/ppermute | solution.py:445
  24.5 8.5 %collective-permute-start.2 = (bf16[320,512]{1,0:T(8,128)(2,1)}, bf16[320,512]{1,0:T(8,128)(2,1)S(1)}, u32[]{:S(2)}, u32[]{:S(2)}) collective-permute-start(bf16[320,512]{1,0:T(8,128)(2,1)} %bitcast.21), channel_id=1, source_target_pairs={{0,2},{1,3},{2,4},{3,5},{4,6},{5,7},{6,0},{7,1},{8,10},{9,11},{10,... | collective-permute-start | bytes 983048 | tf_op jit(solution)/shard_map/ppermute | solution.py:445
  24.5 9.0 %collective-permute-start.10 = (bf16[320,512]{1,0:T(8,128)(2,1)}, bf16[320,512]{1,0:T(8,128)(2,1)S(1)}, u32[]{:S(2)}, u32[]{:S(2)}) collective-permute-start(bf16[320,512]{1,0:T(8,128)(2,1)} %bitcast.22), channel_id=1, source_target_pairs={{0,1},{1,0},{2,3},{3,2},{4,5},{5,4},{6,7},{7,6},{8,9},{9,8},{10,11... | collective-permute-start | bytes 983048 | tf_op jit(solution)/shard_map/ppermute | solution.py:448
  24.7 8.9 %collective-permute-start.12 = (bf16[320,512]{1,0:T(8,128)(2,1)S(1)}, bf16[320,512]{1,0:T(8,128)(2,1)S(1)}, u32[]{:S(2)}, u32[]{:S(2)}) collective-permute-start(bf16[320,512]{1,0:T(8,128)(2,1)S(1)} %collective-permute-done.3.refs_3_), channel_id=1, source_target_pairs={{0,1},{1,0},{2,3},{3,2},{4,5},{5,4},{6,7},{7,6},{8,9},{9,8},{10,11... | collective-permute-start | bytes 983048 | tf_op jit(solution)/shard_map/ppermute | solution.py:448
  26.1 7.4 %copy-start.4 = (f32[4,640]{1,0:T(4,128)S(1)}, f32[4,640]{1,0:T(4,128)}, u32[]{:S(2)}) copy-start(f32[4,640]{1,0:T(4,128)} %param.18) | copy-start | bytes 30724
  26.1 7.4 %copy-start.5 = (f32[4,256]{1,0:T(4,128)S(1)}, f32[4,256]{1,0:T(4,128)}, u32[]{:S(2)}) copy-start(f32[4,256]{1,0:T(4,128)} %param.19) | copy-start | bytes 12292
  26.1 9.0 %copy-start.3 = (bf16[512,320]{0,1:T(8,128)(2,1)S(1)}, bf16[512,320]{0,1:T(8,128)(2,1)}, u32[]{:S(2)}) copy-start(bf16[512,320]{0,1:T(8,128)(2,1)} %param.12) | copy-start | bytes 983044
  33.1 1.6 %collective-permute-start.11 = (bf16[320,512]{1,0:T(8,128)(2,1)S(1)}, bf16[320,512]{1,0:T(8,128)(2,1)S(1)}, u32[]{:S(2)}, u32[]{:S(2)}) collective-permute-start(bf16[320,512]{1,0:T(8,128)(2,1)S(1)} %collective-permute-done.2.refs_2_), channel_id=1, source_target_pairs={{0,1},{1,0},{2,3},{3,2},{4,5},{5,4},{6,7},{7,6},{8,9},{9,8},{10,11... | collective-permute-start | bytes 983048 | tf_op jit(solution)/shard_map/ppermute | solution.py:448
  33.1 2.1 %collective-permute-start.13 = (bf16[320,512]{1,0:T(8,128)(2,1)S(1)}, bf16[320,512]{1,0:T(8,128)(2,1)S(1)}, u32[]{:S(2)}, u32[]{:S(2)}) collective-permute-start(bf16[320,512]{1,0:T(8,128)(2,1)S(1)} %collective-permute-done.4.refs_4_), channel_id=1, source_target_pairs={{0,1},{1,0},{2,3},{3,2},{4,5},{5,4},{6,7},{7,6},{8,9},{9,8},{10,11... | collective-permute-start | bytes 983048 | tf_op jit(solution)/shard_map/ppermute | solution.py:448
  40.7 8.0 %collective-permute-start.14 = (bf16[16,896]{1,0:T(8,128)(2,1)S(1)}, bf16[16,896]{1,0:T(8,128)(2,1)S(1)}, u32[]{:S(2)}, u32[]{:S(2)}) collective-permute-start(bf16[16,896]{1,0:T(8,128)(2,1)S(1)} %get-tuple-element.50), channel_id=1, source_target_pairs={{0,8},{8,16},{16,24},{24,32},{32,40},{40,48},{48,56},{56,64},{64,7... | collective-permute-start | bytes 86024 | tf_op jit(solution)/shard_map/ppermute | solution.py:510
  54.0 25.5 %all-to-all-start = ((bf16[32,8,768]{2,1,0:T(8,128)(2,1)}), bf16[32,8,768]{2,1,0:T(8,128)(2,1)}, u32[]{:S(2)}, u32[]{:S(2)}) async-start(bf16[32,8,768]{2,1,0:T(8,128)(2,1)} %bitcast.24), calls=%async_computation | async-start | bytes 786432 | tf_op jit(solution)/shard_map/all_to_all | solution.py:452
  68.7 17.9 %copy-start.7 = (f32[10]{0:T(128)S(1)}, f32[10]{0:T(128)}, u32[]{:S(2)}) copy-start(f32[10]{0:T(128)} %param.20) | copy-start | bytes 124
  70.2 1.2 copy-start
  71.4 34.2 %collective-permute-start.15 = (bf16[1280,640]{1,0:T(8,128)(2,1)}, bf16[1280,640]{1,0:T(8,128)(2,1)S(1)}, u32[]{:S(2)}, u32[]{:S(2)}) collective-permute-start(bf16[1280,640]{1,0:T(8,128)(2,1)} %get-tuple-element.64), channel_id=1, source_target_pairs={{0,1},{1,0},{2,3},{3,2},{4,5},{5,4},{6,7},{7,6},{8,9},{9,8},{10,11... | collective-permute-start | bytes 4915208 | tf_op jit(solution)/shard_map/ppermute | solution.py:448
  81.8 18.0 %all-to-all-start.1 = ((bf16[32,8,640]{2,1,0:T(8,128)(2,1)}), bf16[32,8,640]{2,1,0:T(8,128)(2,1)S(1)}, u32[]{:S(2)}, u32[]{:S(2)}) async-start(bf16[32,8,640]{2,1,0:T(8,128)(2,1)} %bitcast.9), calls=%async_computation.1 | async-start | bytes 655360 | tf_op jit(solution)/shard_map/all_to_all | solution.py:452
  99.8 3.4 %copy-start.1 = (bf16[1280,640]{1,0:T(8,128)(2,1)S(1)}, bf16[1280,640]{1,0:T(8,128)(2,1)}, u32[]{:S(2)}) copy-start(bf16[1280,640]{1,0:T(8,128)(2,1)} %copy-done) | copy-start | bytes 4915204
  102.6 3.0 %collective-permute-start.20 = (bf16[640,512]{1,0:T(8,128)(2,1)S(1)}, bf16[640,512]{1,0:T(8,128)(2,1)S(1)}, u32[]{:S(2)}, u32[]{:S(2)}) collective-permute-start(bf16[640,512]{1,0:T(8,128)(2,1)S(1)} %get-tuple-element.69.refs_1_), channel_id=1, source_target_pairs={{0,1},{1,0},{2,3},{3,2},{4,5},{5,4},{6,7},{7,6},{8,9},{9,8},{10,11... | collective-permute-start | bytes 1966088 | tf_op jit(solution)/shard_map/ppermute | solution.py:448
  102.7 6.0 %collective-permute-start.16 = (bf16[640,512]{1,0:T(8,128)(2,1)S(1)}, bf16[640,512]{1,0:T(8,128)(2,1)S(1)}, u32[]{:S(2)}, u32[]{:S(2)}) collective-permute-start(bf16[640,512]{1,0:T(8,128)(2,1)S(1)} %get-tuple-element.63.refs_1_), channel_id=1, source_target_pairs={{0,1},{1,0},{2,3},{3,2},{4,5},{5,4},{6,7},{7,6},{8,9},{9,8},{10,11... | collective-permute-start | bytes 1966088 | tf_op jit(solution)/shard_map/ppermute | solution.py:448
  106.8 10.6 %collective-permute-start.21 = (bf16[320,512]{1,0:T(8,128)(2,1)S(1)}, bf16[320,512]{1,0:T(8,128)(2,1)S(1)}, u32[]{:S(2)}, u32[]{:S(2)}) collective-permute-start(bf16[320,512]{1,0:T(8,128)(2,1)S(1)} %get-tuple-element.72), channel_id=1, source_target_pairs={{0,6},{1,7},{2,0},{3,1},{4,2},{5,3},{6,4},{7,5},{8,14},{9,15},{10,... | collective-permute-start | bytes 983048 | tf_op jit(solution)/shard_map/ppermute | solution.py:445
  109.9 11.9 %collective-permute-start.17 = (bf16[320,512]{1,0:T(8,128)(2,1)S(1)}, bf16[320,512]{1,0:T(8,128)(2,1)S(1)}, u32[]{:S(2)}, u32[]{:S(2)}) collective-permute-start(bf16[320,512]{1,0:T(8,128)(2,1)S(1)} %get-tuple-element.67), channel_id=1, source_target_pairs={{0,2},{1,3},{2,4},{3,5},{4,6},{5,7},{6,0},{7,1},{8,10},{9,11},{10,... | collective-permute-start | bytes 983048 | tf_op jit(solution)/shard_map/ppermute | solution.py:445
  110.2 18.6 %collective-permute-start.23 = (bf16[320,512]{1,0:T(8,128)(2,1)S(1)}, bf16[320,512]{1,0:T(8,128)(2,1)S(1)}, u32[]{:S(2)}, u32[]{:S(2)}) collective-permute-start(bf16[320,512]{1,0:T(8,128)(2,1)S(1)} %get-tuple-element.73), channel_id=1, source_target_pairs={{0,2},{1,3},{2,4},{3,5},{4,6},{5,7},{6,0},{7,1},{8,10},{9,11},{10,... | collective-permute-start | bytes 983048 | tf_op jit(solution)/shard_map/ppermute | solution.py:445
  110.6 20.9 %collective-permute-start.19 = (bf16[320,512]{1,0:T(8,128)(2,1)S(1)}, bf16[320,512]{1,0:T(8,128)(2,1)S(1)}, u32[]{:S(2)}, u32[]{:S(2)}) collective-permute-start(bf16[320,512]{1,0:T(8,128)(2,1)S(1)} %get-tuple-element.68), channel_id=1, source_target_pairs={{0,6},{1,7},{2,0},{3,1},{4,2},{5,3},{6,4},{7,5},{8,14},{9,15},{10,... | collective-permute-start | bytes 983048 | tf_op jit(solution)/shard_map/ppermute | solution.py:445
  117.5 13.1 %collective-permute-start.22 = (bf16[320,512]{1,0:T(8,128)(2,1)S(1)}, bf16[320,512]{1,0:T(8,128)(2,1)S(1)}, u32[]{:S(2)}, u32[]{:S(2)}) collective-permute-start(bf16[320,512]{1,0:T(8,128)(2,1)S(1)} %shard_map.137), channel_id=1, source_target_pairs={{0,6},{1,7},{2,0},{3,1},{4,2},{5,3},{6,4},{7,5},{8,14},{9,15},{10,... | collective-permute-start | bytes 983048 | tf_op jit(solution)/shard_map/ppermute | solution.py:445
  121.9 12.8 %collective-permute-start.18 = (bf16[320,512]{1,0:T(8,128)(2,1)S(1)}, bf16[320,512]{1,0:T(8,128)(2,1)S(1)}, u32[]{:S(2)}, u32[]{:S(2)}) collective-permute-start(bf16[320,512]{1,0:T(8,128)(2,1)S(1)} %shard_map.133), channel_id=1, source_target_pairs={{0,2},{1,3},{2,4},{3,5},{4,6},{5,7},{6,0},{7,1},{8,10},{9,11},{10,... | collective-permute-start | bytes 983048 | tf_op jit(solution)/shard_map/ppermute | solution.py:445
  (2 other events, 1.6 us)

commit v5 on v4

--- a/solution.py
+++ b/solution.py
@@ -484,7 +484,7 @@
         [tokens_by],
         [*full, pltpu.SemaphoreType.DMA((14,))],
         held=tuple(range(1, 12)),
-        loose=tuple(range(1, 9)),
+        loose=tuple(range(2, 9)),
         count=12,
         smem=(0,),
         work=work,
@@ -501,7 +501,7 @@
         [*full, pltpu.VMEM((16, channels), BF16), pltpu.SemaphoreType.DMA((15,))],
         near=(12,),
         held=tuple(range(1, 13)),
-        loose=tuple(range(1, 9)),
+        loose=tuple(range(2, 9)),
         count=13,
         smem=(0,),
         work=work,
@@ -520,7 +520,7 @@
             + [pltpu.VMEM((SPAN, channels), F32)]
             + [pltpu.VMEM((SPAN, channels), BF16)] * 2
             + [pltpu.VMEM((width, 2 * SPAN), BF16)],
-            near=(0, 1, 2, 7, 8),
+            near=(0, 1, 2, 6, 7, 8),
             pinned=(0, 1, 2, 3, 4) if out else (0, 1),
             count=len(args),
             work=(10**9, 8 * MIB),

time: 136 us -> 134 us (0.985)
  local copies, waits for them, and re-layouts: 7.46 us -> 5.97 us
    unnamed x18 -> x12, local copies, waits for them, and re-layouts: 6.92 us -> 5.37 us
  transfers between devices with their start and end apart: 26 -> 26, of which waited for: 12 -> 13; matrix products, arithmetic and copies ran while one was open for 5% -> 5% of each run, Pallas kernels for 22% -> 22%
where the time goes in v5:
time: 134 us
  waiting for transfers between devices  45.7 us (34%)
  Pallas kernels  41.1 us (31%)
  starting transfers between devices  38.8 us (29%)
  local copies, waits for them, and re-layouts  5.97 us (4%)
  other arithmetic  1.41 us (1%)
    pallas_call x17, Pallas kernels, run(): pl.pallas_call(kernel, out_shape=[pltpu.HBM(v.shape, v.dtype) if i in far...  41.1 us
    ppermute x12, waiting for transfers between devices, along(): return lax.ppermute(values, 'head', route)  29.3 us
    ppermute x12, starting transfers between devices, along(): return lax.ppermute(values, 'head', route)  17.4 us
    all_to_all x2, starting transfers between devices, exchange(): return lax.all_to_all(blocks, 'ctx', 0, 0).reshape(values.shape)  15.3 us
    all_to_all x2, waiting for transfers between devices, exchange(): return lax.all_to_all(blocks, 'ctx', 0, 0).reshape(values.shape)  14.9 us
    unnamed x12, local copies, waits for them, and re-layouts  5.37 us
    ppermute x1, starting transfers between devices, on_device(): before = lax.ppermute(edge, 'ctx', [(i, i + 1) for i in range(n_ctx - 1)])  3.82 us
  transfers between devices with their start and end apart: 26, of which 13 were waited for; matrix products, arithmetic and copies ran while one was open for 5% of the time, Pallas kernels for 22%

profile of v5, /device:TPU:32, one launch (start us, length us, event | category | flops | bytes accessed | tf_op | source)
XLA Modules:
  0.0 133.8 jit_solution(16731969868715150099)
XLA Ops:
  0.6 1.6 %collective-permute-start = (bf16[320,512]{1,0:T(8,128)(2,1)}, bf16[320,512]{1,0:T(8,128)(2,1)S(1)}, u32[]{:S(2)}, u32[]{:S(2)}) collective-permute-start(bf16[320,512]{1,0:T(8,128)(2,1)} %bitcast.21), channel_id=1, source_target_pairs={{0,2},{1,3},{2,4},{3,5},{4,6},{5,7},{6,0},{7,1},{8,10},{9,11},{10,... | collective-permute-start | bytes 983048 | tf_op jit(solution)/shard_map/ppermute | solution.py:445
  2.2 1.7 %collective-permute-start.5 = (bf16[320,512]{1,0:T(8,128)(2,1)}, bf16[320,512]{1,0:T(8,128)(2,1)S(1)}, u32[]{:S(2)}, u32[]{:S(2)}) collective-permute-start(bf16[320,512]{1,0:T(8,128)(2,1)} %bitcast.22), channel_id=1, source_target_pairs={{0,6},{1,7},{2,0},{3,1},{4,2},{5,3},{6,4},{7,5},{8,14},{9,15},{10,... | collective-permute-start | bytes 983048 | tf_op jit(solution)/shard_map/ppermute | solution.py:445
  3.9 1.4 %select_maximum_fusion.refs_0_ = f32[32,512]{1,0:T(8,128)} fusion(f32[10,512]{1,0:T(8,128)} %bitcast.19, f32[10,512]{1,0:T(8,128)} %bitcast.20), kind=kLoop, calls=%fused_computation | loop fusion | flops 81920 | bytes 106496 | tf_op jit(solution)/shard_map/concatenate | solution.py:459
  5.4 2.5 %shard_map.123 = (f32[80,512]{1,0:T(8,128)}, f32[512,32]{1,0:T(8,128)}, f32[8,640]{1,0:T(8,128)}, f32[8,128]{1,0:T(8,128)}) custom-call(f32[32,512]{1,0:T(8,128)} %select_maximum_fusion.refs_0_), custom_call_target="tpu_custom_call" | custom-call | flops 100000000 | bytes 1000000 | tf_op jit(solution)/shard_map/pallas_call | solution.py:74
  7.9 3.7 %collective-permute-done.refs_2_ = bf16[320,512]{1,0:T(8,128)(2,1)S(1)} collective-permute-done((bf16[320,512]{1,0:T(8,128)(2,1)}, bf16[320,512]{1,0:T(8,128)(2,1)S(1)}, u32[]{:S(2)}, u32[]{:S(2)}) %collective-permute-start) | collective-permute-done | bytes 327712 | tf_op jit(solution)/shard_map/ppermute | solution.py:445
  11.9 3.0 %collective-permute-start.3 = (bf16[320,512]{1,0:T(8,128)(2,1)}, bf16[320,512]{1,0:T(8,128)(2,1)S(1)}, u32[]{:S(2)}, u32[]{:S(2)}) collective-permute-start(bf16[320,512]{1,0:T(8,128)(2,1)} %bitcast.25), channel_id=1, source_target_pairs={{0,6},{1,7},{2,0},{3,1},{4,2},{5,3},{6,4},{7,5},{8,14},{9,15},{10,... | collective-permute-start | bytes 983048 | tf_op jit(solution)/shard_map/ppermute | solution.py:445
  15.3 6.0 %collective-permute-done.1.refs_4_ = bf16[320,512]{1,0:T(8,128)(2,1)S(1)} collective-permute-done((bf16[320,512]{1,0:T(8,128)(2,1)S(1)}, bf16[320,512]{1,0:T(8,128)(2,1)S(1)}, u32[]{:S(2)}, u32[]{:S(2)}) %collective-permute-start.1) | collective-permute-done | bytes 327712 | tf_op jit(solution)/shard_map/ppermute | solution.py:445
  21.4 3.2 %collective-permute-start.4 = (bf16[320,512]{1,0:T(8,128)(2,1)S(1)}, bf16[320,512]{1,0:T(8,128)(2,1)S(1)}, u32[]{:S(2)}, u32[]{:S(2)}) collective-permute-start(bf16[320,512]{1,0:T(8,128)(2,1)S(1)} %collective-permute-done.3.refs_3_), channel_id=1, source_target_pairs={{0,6},{1,7},{2,0},{3,1},{4,2},{5,3},{6,4},{7,5},{8,14},{9,15},{10,... | collective-permute-start | bytes 983048 | tf_op jit(solution)/shard_map/ppermute | solution.py:445
  25.2 5.4 %shard_map.124.refs_12_.refs_0_ = bf16[512,896]{1,0:T(8,128)(2,1)S(1)} custom-call(s32[1]{0:T(128)} %bitcast.refs_0_, bf16[320,512]{1,0:T(8,128)(2,1)} %bitcast.24, bf16[320,512]{1,0:T(8,128)(2,1)S(1)} %collective-permute-done.refs_2_, bf16[320,512]{1,0:T(8,128)(2,1)S(1)} %collective-permute-done.5.refs_3_, ...), custom_call_target="tpu_custom_call" | custom-call | flops 2348810240 | bytes 12582912 | tf_op jit(solution)/shard_map/pallas_call | solution.py:74
  31.5 1.6 %collective-permute-done.2.refs_2_ = bf16[320,512]{1,0:T(8,128)(2,1)S(1)} collective-permute-done((bf16[320,512]{1,0:T(8,128)(2,1)}, bf16[320,512]{1,0:T(8,128)(2,1)S(1)}, u32[]{:S(2)}, u32[]{:S(2)}) %collective-permute-start.2) | collective-permute-done | bytes 327712 | tf_op jit(solution)/shard_map/ppermute | solution.py:445
  35.2 5.5 %shard_map.125 = (bf16[512,896]{1,0:T(8,128)(2,1)S(1)}, bf16[16,896]{1,0:T(8,128)(2,1)S(1)}) custom-call(s32[1]{0:T(128)} %bitcast.refs_0_, bf16[320,512]{1,0:T(8,128)(2,1)} %bitcast.28, bf16[320,512]{1,0:T(8,128)(2,1)S(1)} %collective-permute-done.2.refs_2_, bf16[320,512]{1,0:T(8,128)(2,1)S(1)} %collective-permute-done.3.refs_3_, ...), custom_call_target="tpu_custom_call" | custom-call | flops 2348810240 | bytes 12582912 | tf_op jit(solution)/shard_map/pallas_call | solution.py:74
  40.6 3.8 %collective-permute-start.14 = (bf16[16,896]{1,0:T(8,128)(2,1)S(1)}, bf16[16,896]{1,0:T(8,128)(2,1)S(1)}, u32[]{:S(2)}, u32[]{:S(2)}) collective-permute-start(bf16[16,896]{1,0:T(8,128)(2,1)S(1)} %get-tuple-element.50), channel_id=1, source_target_pairs={{0,8},{8,16},{16,24},{24,32},{32,40},{40,48},{48,56},{56,64},{64,7... | collective-permute-start | bytes 86024 | tf_op jit(solution)/shard_map/ppermute | solution.py:510
  44.5 4.1 %shard_map.126 = (bf16[896,256]{1,0:T(8,128)(2,1)}, bf16[896,256]{1,0:T(8,128)(2,1)}, f32[128,640]{1,0:T(8,128)S(1)}, f32[128,640]{1,0:T(8,128)S(1)}) custom-call(bf16[512,896]{1,0:T(8,128)(2,1)S(1)} %shard_map.124.refs_12_.refs_0_, bf16[512,896]{1,0:T(8,128)(2,1)S(1)} %get-tuple-element.46.refs_1_, f32[4,896]{1,0:T(4,128)S(1)} %constant_dynamic-update-slice_fusion.refs_2_, ...), custom_call_target="tpu_custom_call" | custom-call | flops 1000000000 | bytes 8388608 | tf_op jit(solution)/shard_map/pallas_call | solution.py:74
  48.6 4.7 %shard_map.127 = (bf16[896,256]{1,0:T(8,128)(2,1)}, bf16[896,256]{1,0:T(8,128)(2,1)}, f32[128,640]{1,0:T(8,128)}, f32[128,640]{1,0:T(8,128)}, bf16[256,768]{1,0:T(8,128)(2,1)}) custom-call(bf16[512,896]{1,0:T(8,128)(2,1)S(1)} %shard_map.124.refs_12_.refs_0_, bf16[512,896]{1,0:T(8,128)(2,1)S(1)} %get-tuple-element.46.refs_1_, ...), custom_call_target="tpu_custom_call" | custom-call | flops 1000000000 | bytes 8388608 | tf_op jit(solution)/shard_map/pallas_call | solution.py:74
  53.3 10.5 %all-to-all-start = ((bf16[32,8,768]{2,1,0:T(8,128)(2,1)}), bf16[32,8,768]{2,1,0:T(8,128)(2,1)}, u32[]{:S(2)}, u32[]{:S(2)}) async-start(bf16[32,8,768]{2,1,0:T(8,128)(2,1)} %bitcast.16), calls=%async_computation | async-start | bytes 786432 | tf_op jit(solution)/shard_map/all_to_all | solution.py:452
  63.9 4.2 %copy.13 = bf16[640,2560]{0,1:T(8,128)(2,1)S(1)} copy(bf16[640,2560]{1,0:T(8,128)(2,1)} %param.21) | data formatting | bytes 6553600 | tf_op args[10]
  68.1 1.5 %shard_map.122 = (bf16[1280,640]{1,0:T(8,128)(2,1)S(1)}, bf16[1280,640]{1,0:T(8,128)(2,1)}) custom-call(s32[1]{0:T(128)} %bitcast.refs_0_, bf16[2560,640]{1,0:T(8,128)(2,1)S(1)} %bitcast.14), custom_call_target="tpu_custom_call" | custom-call | flops 1000000 | bytes 6291456 | tf_op jit(solution)/shard_map/pallas_call | solution.py:74
  70.7 8.1 %all-to-all-done = bf16[32,8,768]{2,1,0:T(8,128)(2,1)} async-done(((bf16[32,8,768]{2,1,0:T(8,128)(2,1)}), bf16[32,8,768]{2,1,0:T(8,128)(2,1)}, u32[]{:S(2)}, u32[]{:S(2)}) %all-to-all-start) | async-done | bytes 393248 | tf_op jit(solution)/shard_map/all_to_all | solution.py:452
  78.8 2.3 %shard_map.128 = bf16[256,640]{1,0:T(8,128)(2,1)} custom-call(s32[1]{0:T(128)} %bitcast.2.refs_0_, bf16[256,768]{1,0:T(8,128)(2,1)} %bitcast.8.refs_1_), custom_call_target="tpu_custom_call" | custom-call | flops 100000000 | bytes 1048576 | tf_op jit(solution)/shard_map/pallas_call | solution.py:74
  81.1 4.8 %all-to-all-start.1 = ((bf16[32,8,640]{2,1,0:T(8,128)(2,1)}), bf16[32,8,640]{2,1,0:T(8,128)(2,1)S(1)}, u32[]{:S(2)}, u32[]{:S(2)}) async-start(bf16[32,8,640]{2,1,0:T(8,128)(2,1)} %bitcast.9), calls=%async_computation.1 | async-start | bytes 655360 | tf_op jit(solution)/shard_map/all_to_all | solution.py:452
  86.5 5.7 %shard_map.129 = (f32[640,512]{1,0:T(8,128)}, f32[640,512]{1,0:T(8,128)}) custom-call(bf16[896,256]{1,0:T(8,128)(2,1)} %get-tuple-element.54.refs_0_.refs_1_, bf16[896,256]{1,0:T(8,128)(2,1)} %get-tuple-element.55.refs_1_.refs_2_, bf16[896,256]{1,0:T(8,128)(2,1)} %get-tuple-element.56.refs_2_.refs_3_, bf16[896,256]{1,0:T(8,128)(2,1)} %get-tuple-element.57.refs_3_.refs_4_, ...), custom_call_target="tpu_custom_call" | custom-call | flops 5000000000 | bytes 8388608 | tf_op jit(solution)/shard_map/pallas_call | solution.py:74
  92.2 6.8 %all-to-all-done.1 = bf16[32,8,640]{2,1,0:T(8,128)(2,1)S(1)} async-done(((bf16[32,8,640]{2,1,0:T(8,128)(2,1)}), bf16[32,8,640]{2,1,0:T(8,128)(2,1)S(1)}, u32[]{:S(2)}, u32[]{:S(2)}) %all-to-all-start.1) | async-done | bytes 327712 | tf_op jit(solution)/shard_map/all_to_all | solution.py:452
  98.9 2.8 %shard_map.130 = (bf16[640,512]{1,0:T(8,128)(2,1)S(1)}, bf16[640,512]{1,0:T(8,128)(2,1)S(1)}) custom-call(bf16[256,640]{1,0:T(8,128)(2,1)S(1)} %bitcast.15, bf16[896,256]{1,0:T(8,128)(2,1)} %get-tuple-element.54.refs_0_.refs_1_, bf16[896,256]{1,0:T(8,128)(2,1)} %get-tuple-element.55.refs_1_.refs_2_, bf16[896,256]{1,0:T(8,128)(2,1)} %get-tuple-element.56.refs_2_.refs_3_, ...), custom_call_target="tpu_custom_call" | custom-call | flops 1000000000 | bytes 6291456 | tf_op jit(solution)/shard_map/pallas_call | solution.py:74
  103.6 1.2 shard_map.131.refs_0_
  104.8 1.2 shard_map.136
  107.0 1.2 shard_map.132
  109.7 2.8 %collective-permute-start.19 = (bf16[320,512]{1,0:T(8,128)(2,1)S(1)}, bf16[320,512]{1,0:T(8,128)(2,1)S(1)}, u32[]{:S(2)}, u32[]{:S(2)}) collective-permute-start(bf16[320,512]{1,0:T(8,128)(2,1)S(1)} %get-tuple-element.68), channel_id=1, source_target_pairs={{0,6},{1,7},{2,0},{3,1},{4,2},{5,3},{6,4},{7,5},{8,14},{9,15},{10,... | collective-permute-start | bytes 983048 | tf_op jit(solution)/shard_map/ppermute | solution.py:445
  112.6 4.0 %collective-permute-done.21.refs_1_ = bf16[320,512]{1,0:T(8,128)(2,1)S(1)} collective-permute-done((bf16[320,512]{1,0:T(8,128)(2,1)S(1)}, bf16[320,512]{1,0:T(8,128)(2,1)S(1)}, u32[]{:S(2)}, u32[]{:S(2)}) %collective-permute-start.21) | collective-permute-done | bytes 327712 | tf_op jit(solution)/shard_map/ppermute | solution.py:445
  116.7 2.2 %collective-permute-start.22 = (bf16[320,512]{1,0:T(8,128)(2,1)S(1)}, bf16[320,512]{1,0:T(8,128)(2,1)S(1)}, u32[]{:S(2)}, u32[]{:S(2)}) collective-permute-start(bf16[320,512]{1,0:T(8,128)(2,1)S(1)} %shard_map.137), channel_id=1, source_target_pairs={{0,6},{1,7},{2,0},{3,1},{4,2},{5,3},{6,4},{7,5},{8,14},{9,15},{10,... | collective-permute-start | bytes 983048 | tf_op jit(solution)/shard_map/ppermute | solution.py:445
  120.2 6.9 %collective-permute-done.23.refs_2_ = bf16[320,512]{1,0:T(8,128)(2,1)S(1)} collective-permute-done((bf16[320,512]{1,0:T(8,128)(2,1)S(1)}, bf16[320,512]{1,0:T(8,128)(2,1)S(1)}, u32[]{:S(2)}, u32[]{:S(2)}) %collective-permute-start.23) | collective-permute-done | bytes 327712 | tf_op jit(solution)/shard_map/ppermute | solution.py:445
  127.1 2.7 %collective-permute-done.22.refs_1_ = bf16[320,512]{1,0:T(8,128)(2,1)S(1)} collective-permute-done((bf16[320,512]{1,0:T(8,128)(2,1)S(1)}, bf16[320,512]{1,0:T(8,128)(2,1)S(1)}, u32[]{:S(2)}, u32[]{:S(2)}) %collective-permute-start.22) | collective-permute-done | bytes 327712 | tf_op jit(solution)/shard_map/ppermute | solution.py:445
  130.6 2.3 %collective-permute-done.18.refs_1_ = bf16[320,512]{1,0:T(8,128)(2,1)S(1)} collective-permute-done((bf16[320,512]{1,0:T(8,128)(2,1)S(1)}, bf16[320,512]{1,0:T(8,128)(2,1)S(1)}, u32[]{:S(2)}, u32[]{:S(2)}) %collective-permute-start.18) | collective-permute-done | bytes 327712 | tf_op jit(solution)/shard_map/ppermute | solution.py:445
  (52 shorter events, 13.6 us)
Async XLA Ops:
  0.6 10.9 %collective-permute-start = (bf16[320,512]{1,0:T(8,128)(2,1)}, bf16[320,512]{1,0:T(8,128)(2,1)S(1)}, u32[]{:S(2)}, u32[]{:S(2)}) collective-permute-start(bf16[320,512]{1,0:T(8,128)(2,1)} %bitcast.21), channel_id=1, source_target_pairs={{0,2},{1,3},{2,4},{3,5},{4,6},{5,7},{6,0},{7,1},{8,10},{9,11},{10,... | collective-permute-start | bytes 983048 | tf_op jit(solution)/shard_map/ppermute | solution.py:445
  2.2 13.1 %collective-permute-start.5 = (bf16[320,512]{1,0:T(8,128)(2,1)}, bf16[320,512]{1,0:T(8,128)(2,1)S(1)}, u32[]{:S(2)}, u32[]{:S(2)}) collective-permute-start(bf16[320,512]{1,0:T(8,128)(2,1)} %bitcast.22), channel_id=1, source_target_pairs={{0,6},{1,7},{2,0},{3,1},{4,2},{5,3},{6,4},{7,5},{8,14},{9,15},{10,... | collective-permute-start | bytes 983048 | tf_op jit(solution)/shard_map/ppermute | solution.py:445
  11.6 9.8 %collective-permute-start.1 = (bf16[320,512]{1,0:T(8,128)(2,1)S(1)}, bf16[320,512]{1,0:T(8,128)(2,1)S(1)}, u32[]{:S(2)}, u32[]{:S(2)}) collective-permute-start(bf16[320,512]{1,0:T(8,128)(2,1)S(1)} %collective-permute-done.refs_2_), channel_id=1, source_target_pairs={{0,2},{1,3},{2,4},{3,5},{4,6},{5,7},{6,0},{7,1},{8,10},{9,11},{10,... | collective-permute-start | bytes 983048 | tf_op jit(solution)/shard_map/ppermute | solution.py:445
  11.9 9.5 %collective-permute-start.3 = (bf16[320,512]{1,0:T(8,128)(2,1)}, bf16[320,512]{1,0:T(8,128)(2,1)S(1)}, u32[]{:S(2)}, u32[]{:S(2)}) collective-permute-start(bf16[320,512]{1,0:T(8,128)(2,1)} %bitcast.25), channel_id=1, source_target_pairs={{0,6},{1,7},{2,0},{3,1},{4,2},{5,3},{6,4},{7,5},{8,14},{9,15},{10,... | collective-permute-start | bytes 983048 | tf_op jit(solution)/shard_map/ppermute | solution.py:445
  14.8 9.7 %collective-permute-start.6 = (bf16[320,512]{1,0:T(8,128)(2,1)}, bf16[320,512]{1,0:T(8,128)(2,1)S(1)}, u32[]{:S(2)}, u32[]{:S(2)}) collective-permute-start(bf16[320,512]{1,0:T(8,128)(2,1)} %bitcast.23), channel_id=1, source_target_pairs={{0,1},{1,0},{2,3},{3,2},{4,5},{5,4},{6,7},{7,6},{8,9},{9,8},{10,11... | collective-permute-start | bytes 983048 | tf_op jit(solution)/shard_map/ppermute | solution.py:448
  14.8 9.7 %collective-permute-start.7 = (bf16[320,512]{1,0:T(8,128)(2,1)S(1)}, bf16[320,512]{1,0:T(8,128)(2,1)S(1)}, u32[]{:S(2)}, u32[]{:S(2)}) collective-permute-start(bf16[320,512]{1,0:T(8,128)(2,1)S(1)} %collective-permute-done.refs_2_), channel_id=1, source_target_pairs={{0,1},{1,0},{2,3},{3,2},{4,5},{5,4},{6,7},{7,6},{8,9},{9,8},{10,11... | collective-permute-start | bytes 983048 | tf_op jit(solution)/shard_map/ppermute | solution.py:448
  15.3 9.3 %collective-permute-start.8 = (bf16[320,512]{1,0:T(8,128)(2,1)S(1)}, bf16[320,512]{1,0:T(8,128)(2,1)S(1)}, u32[]{:S(2)}, u32[]{:S(2)}) collective-permute-start(bf16[320,512]{1,0:T(8,128)(2,1)S(1)} %collective-permute-done.5.refs_3_), channel_id=1, source_target_pairs={{0,1},{1,0},{2,3},{3,2},{4,5},{5,4},{6,7},{7,6},{8,9},{9,8},{10,11... | collective-permute-start | bytes 983048 | tf_op jit(solution)/shard_map/ppermute | solution.py:448
  21.4 3.8 %collective-permute-start.9 = (bf16[320,512]{1,0:T(8,128)(2,1)S(1)}, bf16[320,512]{1,0:T(8,128)(2,1)S(1)}, u32[]{:S(2)}, u32[]{:S(2)}) collective-permute-start(bf16[320,512]{1,0:T(8,128)(2,1)S(1)} %collective-permute-done.1.refs_4_), channel_id=1, source_target_pairs={{0,1},{1,0},{2,3},{3,2},{4,5},{5,4},{6,7},{7,6},{8,9},{9,8},{10,11... | collective-permute-start | bytes 983048 | tf_op jit(solution)/shard_map/ppermute | solution.py:448
  21.4 10.1 %collective-permute-start.4 = (bf16[320,512]{1,0:T(8,128)(2,1)S(1)}, bf16[320,512]{1,0:T(8,128)(2,1)S(1)}, u32[]{:S(2)}, u32[]{:S(2)}) collective-permute-start(bf16[320,512]{1,0:T(8,128)(2,1)S(1)} %collective-permute-done.3.refs_3_), channel_id=1, source_target_pairs={{0,6},{1,7},{2,0},{3,1},{4,2},{5,3},{6,4},{7,5},{8,14},{9,15},{10,... | collective-permute-start | bytes 983048 | tf_op jit(solution)/shard_map/ppermute | solution.py:445
  24.5 8.5 %collective-permute-start.2 = (bf16[320,512]{1,0:T(8,128)(2,1)}, bf16[320,512]{1,0:T(8,128)(2,1)S(1)}, u32[]{:S(2)}, u32[]{:S(2)}) collective-permute-start(bf16[320,512]{1,0:T(8,128)(2,1)} %bitcast.26), channel_id=1, source_target_pairs={{0,2},{1,3},{2,4},{3,5},{4,6},{5,7},{6,0},{7,1},{8,10},{9,11},{10,... | collective-permute-start | bytes 983048 | tf_op jit(solution)/shard_map/ppermute | solution.py:445
  24.5 9.0 %collective-permute-start.10 = (bf16[320,512]{1,0:T(8,128)(2,1)}, bf16[320,512]{1,0:T(8,128)(2,1)S(1)}, u32[]{:S(2)}, u32[]{:S(2)}) collective-permute-start(bf16[320,512]{1,0:T(8,128)(2,1)} %bitcast.27), channel_id=1, source_target_pairs={{0,1},{1,0},{2,3},{3,2},{4,5},{5,4},{6,7},{7,6},{8,9},{9,8},{10,11... | collective-permute-start | bytes 983048 | tf_op jit(solution)/shard_map/ppermute | solution.py:448
  24.7 8.9 %collective-permute-start.12 = (bf16[320,512]{1,0:T(8,128)(2,1)S(1)}, bf16[320,512]{1,0:T(8,128)(2,1)S(1)}, u32[]{:S(2)}, u32[]{:S(2)}) collective-permute-start(bf16[320,512]{1,0:T(8,128)(2,1)S(1)} %collective-permute-done.3.refs_3_), channel_id=1, source_target_pairs={{0,1},{1,0},{2,3},{3,2},{4,5},{5,4},{6,7},{7,6},{8,9},{9,8},{10,11... | collective-permute-start | bytes 983048 | tf_op jit(solution)/shard_map/ppermute | solution.py:448
  25.2 8.4 %copy-start.2 = (f32[4,640]{1,0:T(4,128)S(1)}, f32[4,640]{1,0:T(4,128)}, u32[]{:S(2)}) copy-start(f32[4,640]{1,0:T(4,128)} %param.18) | copy-start | bytes 30724
  25.2 8.4 %copy-start.3 = (f32[4,256]{1,0:T(4,128)S(1)}, f32[4,256]{1,0:T(4,128)}, u32[]{:S(2)}) copy-start(f32[4,256]{1,0:T(4,128)} %param.19) | copy-start | bytes 12292
  33.1 1.6 %collective-permute-start.11 = (bf16[320,512]{1,0:T(8,128)(2,1)S(1)}, bf16[320,512]{1,0:T(8,128)(2,1)S(1)}, u32[]{:S(2)}, u32[]{:S(2)}) collective-permute-start(bf16[320,512]{1,0:T(8,128)(2,1)S(1)} %collective-permute-done.2.refs_2_), channel_id=1, source_target_pairs={{0,1},{1,0},{2,3},{3,2},{4,5},{5,4},{6,7},{7,6},{8,9},{9,8},{10,11... | collective-permute-start | bytes 983048 | tf_op jit(solution)/shard_map/ppermute | solution.py:448
  33.1 2.1 %collective-permute-start.13 = (bf16[320,512]{1,0:T(8,128)(2,1)S(1)}, bf16[320,512]{1,0:T(8,128)(2,1)S(1)}, u32[]{:S(2)}, u32[]{:S(2)}) collective-permute-start(bf16[320,512]{1,0:T(8,128)(2,1)S(1)} %collective-permute-done.4.refs_4_), channel_id=1, source_target_pairs={{0,1},{1,0},{2,3},{3,2},{4,5},{5,4},{6,7},{7,6},{8,9},{9,8},{10,11... | collective-permute-start | bytes 983048 | tf_op jit(solution)/shard_map/ppermute | solution.py:448
  40.6 8.0 %collective-permute-start.14 = (bf16[16,896]{1,0:T(8,128)(2,1)S(1)}, bf16[16,896]{1,0:T(8,128)(2,1)S(1)}, u32[]{:S(2)}, u32[]{:S(2)}) collective-permute-start(bf16[16,896]{1,0:T(8,128)(2,1)S(1)} %get-tuple-element.50), channel_id=1, source_target_pairs={{0,8},{8,16},{16,24},{24,32},{32,40},{40,48},{48,56},{56,64},{64,7... | collective-permute-start | bytes 86024 | tf_op jit(solution)/shard_map/ppermute | solution.py:510
  53.3 25.5 %all-to-all-start = ((bf16[32,8,768]{2,1,0:T(8,128)(2,1)}), bf16[32,8,768]{2,1,0:T(8,128)(2,1)}, u32[]{:S(2)}, u32[]{:S(2)}) async-start(bf16[32,8,768]{2,1,0:T(8,128)(2,1)} %bitcast.16), calls=%async_computation | async-start | bytes 786432 | tf_op jit(solution)/shard_map/all_to_all | solution.py:452
  68.1 17.8 %copy-start.4 = (f32[10]{0:T(128)S(1)}, f32[10]{0:T(128)}, u32[]{:S(2)}) copy-start(f32[10]{0:T(128)} %param.20) | copy-start | bytes 124
  69.5 1.2 copy-start
  70.7 34.1 %collective-permute-start.15 = (bf16[1280,640]{1,0:T(8,128)(2,1)}, bf16[1280,640]{1,0:T(8,128)(2,1)S(1)}, u32[]{:S(2)}, u32[]{:S(2)}) collective-permute-start(bf16[1280,640]{1,0:T(8,128)(2,1)} %get-tuple-element.64), channel_id=1, source_target_pairs={{0,1},{1,0},{2,3},{3,2},{4,5},{5,4},{6,7},{7,6},{8,9},{9,8},{10,11... | collective-permute-start | bytes 4915208 | tf_op jit(solution)/shard_map/ppermute | solution.py:448
  81.1 17.8 %all-to-all-start.1 = ((bf16[32,8,640]{2,1,0:T(8,128)(2,1)}), bf16[32,8,640]{2,1,0:T(8,128)(2,1)S(1)}, u32[]{:S(2)}, u32[]{:S(2)}) async-start(bf16[32,8,640]{2,1,0:T(8,128)(2,1)} %bitcast.9), calls=%async_computation.1 | async-start | bytes 655360 | tf_op jit(solution)/shard_map/all_to_all | solution.py:452
  98.9 3.4 %copy-start.1 = (bf16[1280,640]{1,0:T(8,128)(2,1)S(1)}, bf16[1280,640]{1,0:T(8,128)(2,1)}, u32[]{:S(2)}) copy-start(bf16[1280,640]{1,0:T(8,128)(2,1)} %copy-done) | copy-start | bytes 4915204
  101.8 3.0 %collective-permute-start.20 = (bf16[640,512]{1,0:T(8,128)(2,1)S(1)}, bf16[640,512]{1,0:T(8,128)(2,1)S(1)}, u32[]{:S(2)}, u32[]{:S(2)}) collective-permute-start(bf16[640,512]{1,0:T(8,128)(2,1)S(1)} %get-tuple-element.69.refs_1_), channel_id=1, source_target_pairs={{0,1},{1,0},{2,3},{3,2},{4,5},{5,4},{6,7},{7,6},{8,9},{9,8},{10,11... | collective-permute-start | bytes 1966088 | tf_op jit(solution)/shard_map/ppermute | solution.py:448
  101.9 5.1 %collective-permute-start.16 = (bf16[640,512]{1,0:T(8,128)(2,1)S(1)}, bf16[640,512]{1,0:T(8,128)(2,1)S(1)}, u32[]{:S(2)}, u32[]{:S(2)}) collective-permute-start(bf16[640,512]{1,0:T(8,128)(2,1)S(1)} %get-tuple-element.63.refs_1_), channel_id=1, source_target_pairs={{0,1},{1,0},{2,3},{3,2},{4,5},{5,4},{6,7},{7,6},{8,9},{9,8},{10,11... | collective-permute-start | bytes 1966088 | tf_op jit(solution)/shard_map/ppermute | solution.py:448
  106.0 10.6 %collective-permute-start.21 = (bf16[320,512]{1,0:T(8,128)(2,1)S(1)}, bf16[320,512]{1,0:T(8,128)(2,1)S(1)}, u32[]{:S(2)}, u32[]{:S(2)}) collective-permute-start(bf16[320,512]{1,0:T(8,128)(2,1)S(1)} %get-tuple-element.72), channel_id=1, source_target_pairs={{0,6},{1,7},{2,0},{3,1},{4,2},{5,3},{6,4},{7,5},{8,14},{9,15},{10,... | collective-permute-start | bytes 983048 | tf_op jit(solution)/shard_map/ppermute | solution.py:445
  108.2 11.9 %collective-permute-start.17 = (bf16[320,512]{1,0:T(8,128)(2,1)S(1)}, bf16[320,512]{1,0:T(8,128)(2,1)S(1)}, u32[]{:S(2)}, u32[]{:S(2)}) collective-permute-start(bf16[320,512]{1,0:T(8,128)(2,1)S(1)} %get-tuple-element.67), channel_id=1, source_target_pairs={{0,2},{1,3},{2,4},{3,5},{4,6},{5,7},{6,0},{7,1},{8,10},{9,11},{10,... | collective-permute-start | bytes 983048 | tf_op jit(solution)/shard_map/ppermute | solution.py:445
  109.3 17.7 %collective-permute-start.23 = (bf16[320,512]{1,0:T(8,128)(2,1)S(1)}, bf16[320,512]{1,0:T(8,128)(2,1)S(1)}, u32[]{:S(2)}, u32[]{:S(2)}) collective-permute-start(bf16[320,512]{1,0:T(8,128)(2,1)S(1)} %get-tuple-element.73), channel_id=1, source_target_pairs={{0,2},{1,3},{2,4},{3,5},{4,6},{5,7},{6,0},{7,1},{8,10},{9,11},{10,... | collective-permute-start | bytes 983048 | tf_op jit(solution)/shard_map/ppermute | solution.py:445
  109.7 20.9 %collective-permute-start.19 = (bf16[320,512]{1,0:T(8,128)(2,1)S(1)}, bf16[320,512]{1,0:T(8,128)(2,1)S(1)}, u32[]{:S(2)}, u32[]{:S(2)}) collective-permute-start(bf16[320,512]{1,0:T(8,128)(2,1)S(1)} %get-tuple-element.68), channel_id=1, source_target_pairs={{0,6},{1,7},{2,0},{3,1},{4,2},{5,3},{6,4},{7,5},{8,14},{9,15},{10,... | collective-permute-start | bytes 983048 | tf_op jit(solution)/shard_map/ppermute | solution.py:445
  116.7 13.1 %collective-permute-start.22 = (bf16[320,512]{1,0:T(8,128)(2,1)S(1)}, bf16[320,512]{1,0:T(8,128)(2,1)S(1)}, u32[]{:S(2)}, u32[]{:S(2)}) collective-permute-start(bf16[320,512]{1,0:T(8,128)(2,1)S(1)} %shard_map.137), channel_id=1, source_target_pairs={{0,6},{1,7},{2,0},{3,1},{4,2},{5,3},{6,4},{7,5},{8,14},{9,15},{10,... | collective-permute-start | bytes 983048 | tf_op jit(solution)/shard_map/ppermute | solution.py:445
  120.1 12.8 %collective-permute-start.18 = (bf16[320,512]{1,0:T(8,128)(2,1)S(1)}, bf16[320,512]{1,0:T(8,128)(2,1)S(1)}, u32[]{:S(2)}, u32[]{:S(2)}) collective-permute-start(bf16[320,512]{1,0:T(8,128)(2,1)S(1)} %shard_map.133), channel_id=1, source_target_pairs={{0,2},{1,3},{2,4},{3,5},{4,6},{5,7},{6,0},{7,1},{8,10},{9,11},{10,... | collective-permute-start | bytes 983048 | tf_op jit(solution)/shard_map/ppermute | solution.py:445

commit v6 on v5

--- a/solution.py
+++ b/solution.py
@@ -461,7 +461,6 @@
         decay_body,
         [shape((80, length), F32), shape((length, 32), F32)]
         + [shape((8, width), F32), shape((8, 128), F32)],
-        pinned=True,
         count=1,
         work=(10**8, 10**6),
     )(dec)
@@ -520,7 +519,7 @@
             + [pltpu.VMEM((SPAN, channels), F32)]
             + [pltpu.VMEM((SPAN, channels), BF16)] * 2
             + [pltpu.VMEM((width, 2 * SPAN), BF16)],
-            near=(0, 1, 2, 6, 7, 8),
+            near=tuple(range(9)),
             pinned=(0, 1, 2, 3, 4) if out else (0, 1),
             count=len(args),
             work=(10**9, 8 * MIB),

time: 134 us -> 131 us (0.978)
  Pallas kernels: 41.1 us -> 38.5 us
  waiting for transfers between devices: 45.7 us -> 44.1 us
    pallas_call x17, Pallas kernels: 41.1 us -> 38.5 us  [run(): pl.pallas_call(kernel, out_shape=[pltpu.HBM(v.shape, v.dtype) if i in far...]
    all_to_all x2, waiting for transfers between devices: 14.9 us -> 13.4 us  [exchange(): return lax.all_to_all(blocks, 'ctx', 0, 0).reshape(values.shape)]
    unnamed x12 -> x18, local copies, waits for them, and re-layouts: 5.37 us -> 6.06 us
where the time goes in v6:
time: 131 us
  waiting for transfers between devices  44.1 us (34%)
  starting transfers between devices  39.3 us (30%)
  Pallas kernels  38.5 us (29%)
  local copies, waits for them, and re-layouts  6.6 us (5%)
  other arithmetic  1.41 us (1%)
    pallas_call x17, Pallas kernels, run(): pl.pallas_call(kernel, out_shape=[pltpu.HBM(v.shape, v.dtype) if i in far...  38.5 us
    ppermute x12, waiting for transfers between devices, along(): return lax.ppermute(values, 'head', route)  29.2 us
    ppermute x12, starting transfers between devices, along(): return lax.ppermute(values, 'head', route)  17.3 us
    all_to_all x2, starting transfers between devices, exchange(): return lax.all_to_all(blocks, 'ctx', 0, 0).reshape(values.shape)  16 us
    all_to_all x2, waiting for transfers between devices, exchange(): return lax.all_to_all(blocks, 'ctx', 0, 0).reshape(values.shape)  13.4 us
    unnamed x18, local copies, waits for them, and re-layouts  6.06 us
    ppermute x1, starting transfers between devices, on_device(): before = lax.ppermute(edge, 'ctx', [(i, i + 1) for i in range(n_ctx - 1)])  3.82 us
  transfers between devices with their start and end apart: 26, of which 13 were waited for; matrix products, arithmetic and copies ran while one was open for 5% of the time, Pallas kernels for 22%

profile of v6, /device:TPU:32, one launch (start us, length us, event | category | flops | bytes accessed | tf_op | source)
XLA Modules:
  0.0 130.8 jit_solution(15395936131344462)
XLA Ops:
  0.6 1.6 %collective-permute-start = (bf16[320,512]{1,0:T(8,128)(2,1)}, bf16[320,512]{1,0:T(8,128)(2,1)S(1)}, u32[]{:S(2)}, u32[]{:S(2)}) collective-permute-start(bf16[320,512]{1,0:T(8,128)(2,1)} %bitcast.21), channel_id=1, source_target_pairs={{0,2},{1,3},{2,4},{3,5},{4,6},{5,7},{6,0},{7,1},{8,10},{9,11},{10,... | collective-permute-start | bytes 983048 | tf_op jit(solution)/shard_map/ppermute | solution.py:445
  2.2 1.7 %collective-permute-start.5 = (bf16[320,512]{1,0:T(8,128)(2,1)}, bf16[320,512]{1,0:T(8,128)(2,1)S(1)}, u32[]{:S(2)}, u32[]{:S(2)}) collective-permute-start(bf16[320,512]{1,0:T(8,128)(2,1)} %bitcast.22), channel_id=1, source_target_pairs={{0,6},{1,7},{2,0},{3,1},{4,2},{5,3},{6,4},{7,5},{8,14},{9,15},{10,... | collective-permute-start | bytes 983048 | tf_op jit(solution)/shard_map/ppermute | solution.py:445
  3.9 1.4 %select_maximum_fusion.refs_0_ = f32[32,512]{1,0:T(8,128)} fusion(f32[10,512]{1,0:T(8,128)} %bitcast.19, f32[10,512]{1,0:T(8,128)} %bitcast.20), kind=kLoop, calls=%fused_computation | loop fusion | flops 81920 | bytes 106496 | tf_op jit(solution)/shard_map/concatenate | solution.py:459
  5.4 1.9 %shard_map.123 = (f32[80,512]{1,0:T(8,128)S(1)}, f32[512,32]{1,0:T(8,128)S(1)}, f32[8,640]{1,0:T(8,128)S(1)}, f32[8,128]{1,0:T(8,128)S(1)}) custom-call(f32[32,512]{1,0:T(8,128)} %select_maximum_fusion.refs_0_), custom_call_target="tpu_custom_call" | custom-call | flops 100000000 | bytes 1000000 | tf_op jit(solution)/shard_map/pallas_call | solution.py:74
  8.0 3.6 %collective-permute-done.refs_2_ = bf16[320,512]{1,0:T(8,128)(2,1)S(1)} collective-permute-done((bf16[320,512]{1,0:T(8,128)(2,1)}, bf16[320,512]{1,0:T(8,128)(2,1)S(1)}, u32[]{:S(2)}, u32[]{:S(2)}) %collective-permute-start) | collective-permute-done | bytes 327712 | tf_op jit(solution)/shard_map/ppermute | solution.py:445
  11.9 3.0 %collective-permute-start.3 = (bf16[320,512]{1,0:T(8,128)(2,1)}, bf16[320,512]{1,0:T(8,128)(2,1)S(1)}, u32[]{:S(2)}, u32[]{:S(2)}) collective-permute-start(bf16[320,512]{1,0:T(8,128)(2,1)} %bitcast.25), channel_id=1, source_target_pairs={{0,6},{1,7},{2,0},{3,1},{4,2},{5,3},{6,4},{7,5},{8,14},{9,15},{10,... | collective-permute-start | bytes 983048 | tf_op jit(solution)/shard_map/ppermute | solution.py:445
  15.3 6.0 %collective-permute-done.1.refs_4_ = bf16[320,512]{1,0:T(8,128)(2,1)S(1)} collective-permute-done((bf16[320,512]{1,0:T(8,128)(2,1)S(1)}, bf16[320,512]{1,0:T(8,128)(2,1)S(1)}, u32[]{:S(2)}, u32[]{:S(2)}) %collective-permute-start.1) | collective-permute-done | bytes 327712 | tf_op jit(solution)/shard_map/ppermute | solution.py:445
  21.4 3.2 %collective-permute-start.4 = (bf16[320,512]{1,0:T(8,128)(2,1)S(1)}, bf16[320,512]{1,0:T(8,128)(2,1)S(1)}, u32[]{:S(2)}, u32[]{:S(2)}) collective-permute-start(bf16[320,512]{1,0:T(8,128)(2,1)S(1)} %collective-permute-done.3.refs_3_), channel_id=1, source_target_pairs={{0,6},{1,7},{2,0},{3,1},{4,2},{5,3},{6,4},{7,5},{8,14},{9,15},{10,... | collective-permute-start | bytes 983048 | tf_op jit(solution)/shard_map/ppermute | solution.py:445
  25.2 5.4 %shard_map.124.refs_12_.refs_0_ = bf16[512,896]{1,0:T(8,128)(2,1)S(1)} custom-call(s32[1]{0:T(128)} %bitcast.refs_0_, bf16[320,512]{1,0:T(8,128)(2,1)} %bitcast.24, bf16[320,512]{1,0:T(8,128)(2,1)S(1)} %collective-permute-done.refs_2_, bf16[320,512]{1,0:T(8,128)(2,1)S(1)} %collective-permute-done.5.refs_3_, ...), custom_call_target="tpu_custom_call" | custom-call | flops 2348810240 | bytes 12582912 | tf_op jit(solution)/shard_map/pallas_call | solution.py:74
  31.5 1.6 %collective-permute-done.2.refs_2_ = bf16[320,512]{1,0:T(8,128)(2,1)S(1)} collective-permute-done((bf16[320,512]{1,0:T(8,128)(2,1)}, bf16[320,512]{1,0:T(8,128)(2,1)S(1)}, u32[]{:S(2)}, u32[]{:S(2)}) %collective-permute-start.2) | collective-permute-done | bytes 327712 | tf_op jit(solution)/shard_map/ppermute | solution.py:445
  35.2 5.5 %shard_map.125 = (bf16[512,896]{1,0:T(8,128)(2,1)S(1)}, bf16[16,896]{1,0:T(8,128)(2,1)S(1)}) custom-call(s32[1]{0:T(128)} %bitcast.refs_0_, bf16[320,512]{1,0:T(8,128)(2,1)} %bitcast.28, bf16[320,512]{1,0:T(8,128)(2,1)S(1)} %collective-permute-done.2.refs_2_, bf16[320,512]{1,0:T(8,128)(2,1)S(1)} %collective-permute-done.3.refs_3_, ...), custom_call_target="tpu_custom_call" | custom-call | flops 2348810240 | bytes 12582912 | tf_op jit(solution)/shard_map/pallas_call | solution.py:74
  40.6 3.8 %collective-permute-start.14 = (bf16[16,896]{1,0:T(8,128)(2,1)S(1)}, bf16[16,896]{1,0:T(8,128)(2,1)S(1)}, u32[]{:S(2)}, u32[]{:S(2)}) collective-permute-start(bf16[16,896]{1,0:T(8,128)(2,1)S(1)} %get-tuple-element.50), channel_id=1, source_target_pairs={{0,8},{8,16},{16,24},{24,32},{32,40},{40,48},{48,56},{56,64},{64,7... | collective-permute-start | bytes 86024 | tf_op jit(solution)/shard_map/ppermute | solution.py:509
  44.5 3.2 %shard_map.126 = (bf16[896,256]{1,0:T(8,128)(2,1)}, bf16[896,256]{1,0:T(8,128)(2,1)}, f32[128,640]{1,0:T(8,128)S(1)}, f32[128,640]{1,0:T(8,128)S(1)}) custom-call(bf16[512,896]{1,0:T(8,128)(2,1)S(1)} %shard_map.124.refs_12_.refs_0_, bf16[512,896]{1,0:T(8,128)(2,1)S(1)} %get-tuple-element.46.refs_1_, f32[4,896]{1,0:T(4,128)S(1)} %constant_dynamic-update-slice_fusion.refs_2_, ...), custom_call_target="tpu_custom_call" | custom-call | flops 1000000000 | bytes 8388608 | tf_op jit(solution)/shard_map/pallas_call | solution.py:74
  47.7 3.7 %shard_map.127 = (bf16[896,256]{1,0:T(8,128)(2,1)}, bf16[896,256]{1,0:T(8,128)(2,1)}, f32[128,640]{1,0:T(8,128)}, f32[128,640]{1,0:T(8,128)}, bf16[256,768]{1,0:T(8,128)(2,1)}) custom-call(bf16[512,896]{1,0:T(8,128)(2,1)S(1)} %shard_map.124.refs_12_.refs_0_, bf16[512,896]{1,0:T(8,128)(2,1)S(1)} %get-tuple-element.46.refs_1_, ...), custom_call_target="tpu_custom_call" | custom-call | flops 1000000000 | bytes 8388608 | tf_op jit(solution)/shard_map/pallas_call | solution.py:74
  51.4 11.4 %all-to-all-start = ((bf16[32,8,768]{2,1,0:T(8,128)(2,1)}), bf16[32,8,768]{2,1,0:T(8,128)(2,1)}, u32[]{:S(2)}, u32[]{:S(2)}) async-start(bf16[32,8,768]{2,1,0:T(8,128)(2,1)} %bitcast.16), calls=%async_computation | async-start | bytes 786432 | tf_op jit(solution)/shard_map/all_to_all | solution.py:452
  62.8 4.2 %copy.13 = bf16[640,2560]{0,1:T(8,128)(2,1)S(1)} copy(bf16[640,2560]{1,0:T(8,128)(2,1)} %param.21) | data formatting | bytes 6553600 | tf_op args[10]
  67.0 1.5 %shard_map.122 = (bf16[1280,640]{1,0:T(8,128)(2,1)S(1)}, bf16[1280,640]{1,0:T(8,128)(2,1)}) custom-call(s32[1]{0:T(128)} %bitcast.refs_0_, bf16[2560,640]{1,0:T(8,128)(2,1)S(1)} %bitcast.14), custom_call_target="tpu_custom_call" | custom-call | flops 1000000 | bytes 6291456 | tf_op jit(solution)/shard_map/pallas_call | solution.py:74
  69.6 7.4 %all-to-all-done = bf16[32,8,768]{2,1,0:T(8,128)(2,1)} async-done(((bf16[32,8,768]{2,1,0:T(8,128)(2,1)}), bf16[32,8,768]{2,1,0:T(8,128)(2,1)}, u32[]{:S(2)}, u32[]{:S(2)}) %all-to-all-start) | async-done | bytes 393248 | tf_op jit(solution)/shard_map/all_to_all | solution.py:452
  77.0 2.3 %shard_map.128 = bf16[256,640]{1,0:T(8,128)(2,1)} custom-call(s32[1]{0:T(128)} %bitcast.2.refs_0_, bf16[256,768]{1,0:T(8,128)(2,1)} %bitcast.8.refs_1_), custom_call_target="tpu_custom_call" | custom-call | flops 100000000 | bytes 1048576 | tf_op jit(solution)/shard_map/pallas_call | solution.py:74
  79.3 4.6 %all-to-all-start.1 = ((bf16[32,8,640]{2,1,0:T(8,128)(2,1)}), bf16[32,8,640]{2,1,0:T(8,128)(2,1)S(1)}, u32[]{:S(2)}, u32[]{:S(2)}) async-start(bf16[32,8,640]{2,1,0:T(8,128)(2,1)} %bitcast.9), calls=%async_computation.1 | async-start | bytes 655360 | tf_op jit(solution)/shard_map/all_to_all | solution.py:452
  84.5 5.7 %shard_map.129 = (f32[640,512]{1,0:T(8,128)}, f32[640,512]{1,0:T(8,128)}) custom-call(bf16[896,256]{1,0:T(8,128)(2,1)} %get-tuple-element.54.refs_0_.refs_1_, bf16[896,256]{1,0:T(8,128)(2,1)} %get-tuple-element.55.refs_1_.refs_2_, bf16[896,256]{1,0:T(8,128)(2,1)} %get-tuple-element.56.refs_2_.refs_3_, bf16[896,256]{1,0:T(8,128)(2,1)} %get-tuple-element.57.refs_3_.refs_4_, ...), custom_call_target="tpu_custom_call" | custom-call | flops 5000000000 | bytes 8388608 | tf_op jit(solution)/shard_map/pallas_call | solution.py:74
  90.2 6.0 %all-to-all-done.1 = bf16[32,8,640]{2,1,0:T(8,128)(2,1)S(1)} async-done(((bf16[32,8,640]{2,1,0:T(8,128)(2,1)}), bf16[32,8,640]{2,1,0:T(8,128)(2,1)S(1)}, u32[]{:S(2)}, u32[]{:S(2)}) %all-to-all-start.1) | async-done | bytes 327712 | tf_op jit(solution)/shard_map/all_to_all | solution.py:452
  96.2 2.8 %shard_map.130 = (bf16[640,512]{1,0:T(8,128)(2,1)S(1)}, bf16[640,512]{1,0:T(8,128)(2,1)S(1)}) custom-call(bf16[256,640]{1,0:T(8,128)(2,1)S(1)} %bitcast.15, bf16[896,256]{1,0:T(8,128)(2,1)} %get-tuple-element.54.refs_0_.refs_1_, bf16[896,256]{1,0:T(8,128)(2,1)} %get-tuple-element.55.refs_1_.refs_2_, bf16[896,256]{1,0:T(8,128)(2,1)} %get-tuple-element.56.refs_2_.refs_3_, ...), custom_call_target="tpu_custom_call" | custom-call | flops 1000000000 | bytes 6291456 | tf_op jit(solution)/shard_map/pallas_call | solution.py:74
  100.8 1.2 shard_map.131.refs_0_
  102.0 1.2 shard_map.136
  105.2 1.3 %collective-permute-start.17 = (bf16[320,512]{1,0:T(8,128)(2,1)S(1)}, bf16[320,512]{1,0:T(8,128)(2,1)S(1)}, u32[]{:S(2)}, u32[]{:S(2)}) collective-permute-start(bf16[320,512]{1,0:T(8,128)(2,1)S(1)} %get-tuple-element.67), channel_id=1, source_target_pairs={{0,2},{1,3},{2,4},{3,5},{4,6},{5,7},{6,0},{7,1},{8,10},{9,11},{10,... | collective-permute-start | bytes 983048 | tf_op jit(solution)/shard_map/ppermute | solution.py:445
  107.0 2.8 %collective-permute-start.19 = (bf16[320,512]{1,0:T(8,128)(2,1)S(1)}, bf16[320,512]{1,0:T(8,128)(2,1)S(1)}, u32[]{:S(2)}, u32[]{:S(2)}) collective-permute-start(bf16[320,512]{1,0:T(8,128)(2,1)S(1)} %get-tuple-element.68), channel_id=1, source_target_pairs={{0,6},{1,7},{2,0},{3,1},{4,2},{5,3},{6,4},{7,5},{8,14},{9,15},{10,... | collective-permute-start | bytes 983048 | tf_op jit(solution)/shard_map/ppermute | solution.py:445
  109.8 4.0 %collective-permute-done.21.refs_1_ = bf16[320,512]{1,0:T(8,128)(2,1)S(1)} collective-permute-done((bf16[320,512]{1,0:T(8,128)(2,1)S(1)}, bf16[320,512]{1,0:T(8,128)(2,1)S(1)}, u32[]{:S(2)}, u32[]{:S(2)}) %collective-permute-start.21) | collective-permute-done | bytes 327712 | tf_op jit(solution)/shard_map/ppermute | solution.py:445
  113.9 2.1 %collective-permute-start.22 = (bf16[320,512]{1,0:T(8,128)(2,1)S(1)}, bf16[320,512]{1,0:T(8,128)(2,1)S(1)}, u32[]{:S(2)}, u32[]{:S(2)}) collective-permute-start(bf16[320,512]{1,0:T(8,128)(2,1)S(1)} %shard_map.137), channel_id=1, source_target_pairs={{0,6},{1,7},{2,0},{3,1},{4,2},{5,3},{6,4},{7,5},{8,14},{9,15},{10,... | collective-permute-start | bytes 983048 | tf_op jit(solution)/shard_map/ppermute | solution.py:445
  117.3 6.8 %collective-permute-done.23.refs_2_ = bf16[320,512]{1,0:T(8,128)(2,1)S(1)} collective-permute-done((bf16[320,512]{1,0:T(8,128)(2,1)S(1)}, bf16[320,512]{1,0:T(8,128)(2,1)S(1)}, u32[]{:S(2)}, u32[]{:S(2)}) %collective-permute-start.23) | collective-permute-done | bytes 327712 | tf_op jit(solution)/shard_map/ppermute | solution.py:445
  124.1 2.9 %collective-permute-done.22.refs_1_ = bf16[320,512]{1,0:T(8,128)(2,1)S(1)} collective-permute-done((bf16[320,512]{1,0:T(8,128)(2,1)S(1)}, bf16[320,512]{1,0:T(8,128)(2,1)S(1)}, u32[]{:S(2)}, u32[]{:S(2)}) %collective-permute-start.22) | collective-permute-done | bytes 327712 | tf_op jit(solution)/shard_map/ppermute | solution.py:445
  127.9 2.1 %collective-permute-done.18.refs_1_ = bf16[320,512]{1,0:T(8,128)(2,1)S(1)} collective-permute-done((bf16[320,512]{1,0:T(8,128)(2,1)S(1)}, bf16[320,512]{1,0:T(8,128)(2,1)S(1)}, u32[]{:S(2)}, u32[]{:S(2)}) %collective-permute-start.18) | collective-permute-done | bytes 327712 | tf_op jit(solution)/shard_map/ppermute | solution.py:445
  (58 shorter events, 14.1 us)
Async XLA Ops:
  0.6 10.9 %collective-permute-start = (bf16[320,512]{1,0:T(8,128)(2,1)}, bf16[320,512]{1,0:T(8,128)(2,1)S(1)}, u32[]{:S(2)}, u32[]{:S(2)}) collective-permute-start(bf16[320,512]{1,0:T(8,128)(2,1)} %bitcast.21), channel_id=1, source_target_pairs={{0,2},{1,3},{2,4},{3,5},{4,6},{5,7},{6,0},{7,1},{8,10},{9,11},{10,... | collective-permute-start | bytes 983048 | tf_op jit(solution)/shard_map/ppermute | solution.py:445
  2.2 13.1 %collective-permute-start.5 = (bf16[320,512]{1,0:T(8,128)(2,1)}, bf16[320,512]{1,0:T(8,128)(2,1)S(1)}, u32[]{:S(2)}, u32[]{:S(2)}) collective-permute-start(bf16[320,512]{1,0:T(8,128)(2,1)} %bitcast.22), channel_id=1, source_target_pairs={{0,6},{1,7},{2,0},{3,1},{4,2},{5,3},{6,4},{7,5},{8,14},{9,15},{10,... | collective-permute-start | bytes 983048 | tf_op jit(solution)/shard_map/ppermute | solution.py:445
  8.0 39.7 %copy-start.2 = (f32[80,512]{1,0:T(8,128)}, f32[80,512]{1,0:T(8,128)S(1)}, u32[]{:S(2)}) copy-start(f32[80,512]{1,0:T(8,128)S(1)} %get-tuple-element.47.refs_3_.refs_4_.refs_7_) | copy-start | bytes 491524
  8.0 39.7 %copy-start.3 = (f32[8,640]{1,0:T(8,128)}, f32[8,640]{1,0:T(8,128)S(1)}, u32[]{:S(2)}) copy-start(f32[8,640]{1,0:T(8,128)S(1)} %get-tuple-element.48.refs_4_.refs_8_) | copy-start | bytes 61444
  11.6 9.8 %collective-permute-start.1 = (bf16[320,512]{1,0:T(8,128)(2,1)S(1)}, bf16[320,512]{1,0:T(8,128)(2,1)S(1)}, u32[]{:S(2)}, u32[]{:S(2)}) collective-permute-start(bf16[320,512]{1,0:T(8,128)(2,1)S(1)} %collective-permute-done.refs_2_), channel_id=1, source_target_pairs={{0,2},{1,3},{2,4},{3,5},{4,6},{5,7},{6,0},{7,1},{8,10},{9,11},{10,... | collective-permute-start | bytes 983048 | tf_op jit(solution)/shard_map/ppermute | solution.py:445
  11.9 9.5 %collective-permute-start.3 = (bf16[320,512]{1,0:T(8,128)(2,1)}, bf16[320,512]{1,0:T(8,128)(2,1)S(1)}, u32[]{:S(2)}, u32[]{:S(2)}) collective-permute-start(bf16[320,512]{1,0:T(8,128)(2,1)} %bitcast.25), channel_id=1, source_target_pairs={{0,6},{1,7},{2,0},{3,1},{4,2},{5,3},{6,4},{7,5},{8,14},{9,15},{10,... | collective-permute-start | bytes 983048 | tf_op jit(solution)/shard_map/ppermute | solution.py:445
  14.8 9.7 %collective-permute-start.6 = (bf16[320,512]{1,0:T(8,128)(2,1)}, bf16[320,512]{1,0:T(8,128)(2,1)S(1)}, u32[]{:S(2)}, u32[]{:S(2)}) collective-permute-start(bf16[320,512]{1,0:T(8,128)(2,1)} %bitcast.23), channel_id=1, source_target_pairs={{0,1},{1,0},{2,3},{3,2},{4,5},{5,4},{6,7},{7,6},{8,9},{9,8},{10,11... | collective-permute-start | bytes 983048 | tf_op jit(solution)/shard_map/ppermute | solution.py:448
  14.8 9.7 %collective-permute-start.7 = (bf16[320,512]{1,0:T(8,128)(2,1)S(1)}, bf16[320,512]{1,0:T(8,128)(2,1)S(1)}, u32[]{:S(2)}, u32[]{:S(2)}) collective-permute-start(bf16[320,512]{1,0:T(8,128)(2,1)S(1)} %collective-permute-done.refs_2_), channel_id=1, source_target_pairs={{0,1},{1,0},{2,3},{3,2},{4,5},{5,4},{6,7},{7,6},{8,9},{9,8},{10,11... | collective-permute-start | bytes 983048 | tf_op jit(solution)/shard_map/ppermute | solution.py:448
  15.3 9.3 %collective-permute-start.8 = (bf16[320,512]{1,0:T(8,128)(2,1)S(1)}, bf16[320,512]{1,0:T(8,128)(2,1)S(1)}, u32[]{:S(2)}, u32[]{:S(2)}) collective-permute-start(bf16[320,512]{1,0:T(8,128)(2,1)S(1)} %collective-permute-done.5.refs_3_), channel_id=1, source_target_pairs={{0,1},{1,0},{2,3},{3,2},{4,5},{5,4},{6,7},{7,6},{8,9},{9,8},{10,11... | collective-permute-start | bytes 983048 | tf_op jit(solution)/shard_map/ppermute | solution.py:448
  21.4 3.8 %collective-permute-start.9 = (bf16[320,512]{1,0:T(8,128)(2,1)S(1)}, bf16[320,512]{1,0:T(8,128)(2,1)}, u32[]{:S(2)}, u32[]{:S(2)}) collective-permute-start(bf16[320,512]{1,0:T(8,128)(2,1)S(1)} %collective-permute-done.1.refs_4_), channel_id=1, source_target_pairs={{0,1},{1,0},{2,3},{3,2},{4,5},{5,4},{6,7},{7,6},{8,9},{9,8},{10,11... | collective-permute-start | bytes 983048 | tf_op jit(solution)/shard_map/ppermute | solution.py:448
  21.4 10.1 %collective-permute-start.4 = (bf16[320,512]{1,0:T(8,128)(2,1)S(1)}, bf16[320,512]{1,0:T(8,128)(2,1)S(1)}, u32[]{:S(2)}, u32[]{:S(2)}) collective-permute-start(bf16[320,512]{1,0:T(8,128)(2,1)S(1)} %collective-permute-done.3.refs_3_), channel_id=1, source_target_pairs={{0,6},{1,7},{2,0},{3,1},{4,2},{5,3},{6,4},{7,5},{8,14},{9,15},{10,... | collective-permute-start | bytes 983048 | tf_op jit(solution)/shard_map/ppermute | solution.py:445
  24.5 8.5 %collective-permute-start.2 = (bf16[320,512]{1,0:T(8,128)(2,1)}, bf16[320,512]{1,0:T(8,128)(2,1)S(1)}, u32[]{:S(2)}, u32[]{:S(2)}) collective-permute-start(bf16[320,512]{1,0:T(8,128)(2,1)} %bitcast.26), channel_id=1, source_target_pairs={{0,2},{1,3},{2,4},{3,5},{4,6},{5,7},{6,0},{7,1},{8,10},{9,11},{10,... | collective-permute-start | bytes 983048 | tf_op jit(solution)/shard_map/ppermute | solution.py:445
  24.5 9.0 %collective-permute-start.10 = (bf16[320,512]{1,0:T(8,128)(2,1)}, bf16[320,512]{1,0:T(8,128)(2,1)S(1)}, u32[]{:S(2)}, u32[]{:S(2)}) collective-permute-start(bf16[320,512]{1,0:T(8,128)(2,1)} %bitcast.27), channel_id=1, source_target_pairs={{0,1},{1,0},{2,3},{3,2},{4,5},{5,4},{6,7},{7,6},{8,9},{9,8},{10,11... | collective-permute-start | bytes 983048 | tf_op jit(solution)/shard_map/ppermute | solution.py:448
  24.7 8.9 %collective-permute-start.12 = (bf16[320,512]{1,0:T(8,128)(2,1)S(1)}, bf16[320,512]{1,0:T(8,128)(2,1)S(1)}, u32[]{:S(2)}, u32[]{:S(2)}) collective-permute-start(bf16[320,512]{1,0:T(8,128)(2,1)S(1)} %collective-permute-done.3.refs_3_), channel_id=1, source_target_pairs={{0,1},{1,0},{2,3},{3,2},{4,5},{5,4},{6,7},{7,6},{8,9},{9,8},{10,11... | collective-permute-start | bytes 983048 | tf_op jit(solution)/shard_map/ppermute | solution.py:448
  25.2 8.4 %copy-start.5 = (f32[4,640]{1,0:T(4,128)S(1)}, f32[4,640]{1,0:T(4,128)}, u32[]{:S(2)}) copy-start(f32[4,640]{1,0:T(4,128)} %param.18) | copy-start | bytes 30724
  25.2 8.4 %copy-start.6 = (f32[4,256]{1,0:T(4,128)S(1)}, f32[4,256]{1,0:T(4,128)}, u32[]{:S(2)}) copy-start(f32[4,256]{1,0:T(4,128)} %param.19) | copy-start | bytes 12292
  33.1 1.6 %collective-permute-start.11 = (bf16[320,512]{1,0:T(8,128)(2,1)S(1)}, bf16[320,512]{1,0:T(8,128)(2,1)S(1)}, u32[]{:S(2)}, u32[]{:S(2)}) collective-permute-start(bf16[320,512]{1,0:T(8,128)(2,1)S(1)} %collective-permute-done.2.refs_2_), channel_id=1, source_target_pairs={{0,1},{1,0},{2,3},{3,2},{4,5},{5,4},{6,7},{7,6},{8,9},{9,8},{10,11... | collective-permute-start | bytes 983048 | tf_op jit(solution)/shard_map/ppermute | solution.py:448
  33.1 2.1 %collective-permute-start.13 = (bf16[320,512]{1,0:T(8,128)(2,1)S(1)}, bf16[320,512]{1,0:T(8,128)(2,1)S(1)}, u32[]{:S(2)}, u32[]{:S(2)}) collective-permute-start(bf16[320,512]{1,0:T(8,128)(2,1)S(1)} %collective-permute-done.4.refs_4_), channel_id=1, source_target_pairs={{0,1},{1,0},{2,3},{3,2},{4,5},{5,4},{6,7},{7,6},{8,9},{9,8},{10,11... | collective-permute-start | bytes 983048 | tf_op jit(solution)/shard_map/ppermute | solution.py:448
  40.6 7.0 %collective-permute-start.14 = (bf16[16,896]{1,0:T(8,128)(2,1)S(1)}, bf16[16,896]{1,0:T(8,128)(2,1)S(1)}, u32[]{:S(2)}, u32[]{:S(2)}) collective-permute-start(bf16[16,896]{1,0:T(8,128)(2,1)S(1)} %get-tuple-element.50), channel_id=1, source_target_pairs={{0,8},{8,16},{16,24},{24,32},{32,40},{40,48},{48,56},{56,64},{64,7... | collective-permute-start | bytes 86024 | tf_op jit(solution)/shard_map/ppermute | solution.py:509
  51.4 25.6 %all-to-all-start = ((bf16[32,8,768]{2,1,0:T(8,128)(2,1)}), bf16[32,8,768]{2,1,0:T(8,128)(2,1)}, u32[]{:S(2)}, u32[]{:S(2)}) async-start(bf16[32,8,768]{2,1,0:T(8,128)(2,1)} %bitcast.16), calls=%async_computation | async-start | bytes 786432 | tf_op jit(solution)/shard_map/all_to_all | solution.py:452
  67.0 17.0 %copy-start.7 = (f32[10]{0:T(128)S(1)}, f32[10]{0:T(128)}, u32[]{:S(2)}) copy-start(f32[10]{0:T(128)} %param.20) | copy-start | bytes 124
  69.6 32.4 %collective-permute-start.15 = (bf16[1280,640]{1,0:T(8,128)(2,1)}, bf16[1280,640]{1,0:T(8,128)(2,1)S(1)}, u32[]{:S(2)}, u32[]{:S(2)}) collective-permute-start(bf16[1280,640]{1,0:T(8,128)(2,1)} %get-tuple-element.64), channel_id=1, source_target_pairs={{0,1},{1,0},{2,3},{3,2},{4,5},{5,4},{6,7},{7,6},{8,9},{9,8},{10,11... | collective-permute-start | bytes 4915208 | tf_op jit(solution)/shard_map/ppermute | solution.py:448
  79.3 16.8 %all-to-all-start.1 = ((bf16[32,8,640]{2,1,0:T(8,128)(2,1)}), bf16[32,8,640]{2,1,0:T(8,128)(2,1)S(1)}, u32[]{:S(2)}, u32[]{:S(2)}) async-start(bf16[32,8,640]{2,1,0:T(8,128)(2,1)} %bitcast.9), calls=%async_computation.1 | async-start | bytes 655360 | tf_op jit(solution)/shard_map/all_to_all | solution.py:452
  96.2 3.4 %copy-start.1 = (bf16[1280,640]{1,0:T(8,128)(2,1)S(1)}, bf16[1280,640]{1,0:T(8,128)(2,1)}, u32[]{:S(2)}) copy-start(bf16[1280,640]{1,0:T(8,128)(2,1)} %copy-done) | copy-start | bytes 4915204
  99.0 3.0 %collective-permute-start.20 = (bf16[640,512]{1,0:T(8,128)(2,1)S(1)}, bf16[640,512]{1,0:T(8,128)(2,1)S(1)}, u32[]{:S(2)}, u32[]{:S(2)}) collective-permute-start(bf16[640,512]{1,0:T(8,128)(2,1)S(1)} %get-tuple-element.69.refs_1_), channel_id=1, source_target_pairs={{0,1},{1,0},{2,3},{3,2},{4,5},{5,4},{6,7},{7,6},{8,9},{9,8},{10,11... | collective-permute-start | bytes 1966088 | tf_op jit(solution)/shard_map/ppermute | solution.py:448
  99.1 4.9 %collective-permute-start.16 = (bf16[640,512]{1,0:T(8,128)(2,1)S(1)}, bf16[640,512]{1,0:T(8,128)(2,1)S(1)}, u32[]{:S(2)}, u32[]{:S(2)}) collective-permute-start(bf16[640,512]{1,0:T(8,128)(2,1)S(1)} %get-tuple-element.63.refs_1_), channel_id=1, source_target_pairs={{0,1},{1,0},{2,3},{3,2},{4,5},{5,4},{6,7},{7,6},{8,9},{9,8},{10,11... | collective-permute-start | bytes 1966088 | tf_op jit(solution)/shard_map/ppermute | solution.py:448
  103.2 10.6 %collective-permute-start.21 = (bf16[320,512]{1,0:T(8,128)(2,1)S(1)}, bf16[320,512]{1,0:T(8,128)(2,1)S(1)}, u32[]{:S(2)}, u32[]{:S(2)}) collective-permute-start(bf16[320,512]{1,0:T(8,128)(2,1)S(1)} %get-tuple-element.72), channel_id=1, source_target_pairs={{0,6},{1,7},{2,0},{3,1},{4,2},{5,3},{6,4},{7,5},{8,14},{9,15},{10,... | collective-permute-start | bytes 983048 | tf_op jit(solution)/shard_map/ppermute | solution.py:445
  105.2 11.9 %collective-permute-start.17 = (bf16[320,512]{1,0:T(8,128)(2,1)S(1)}, bf16[320,512]{1,0:T(8,128)(2,1)S(1)}, u32[]{:S(2)}, u32[]{:S(2)}) collective-permute-start(bf16[320,512]{1,0:T(8,128)(2,1)S(1)} %get-tuple-element.67), channel_id=1, source_target_pairs={{0,2},{1,3},{2,4},{3,5},{4,6},{5,7},{6,0},{7,1},{8,10},{9,11},{10,... | collective-permute-start | bytes 983048 | tf_op jit(solution)/shard_map/ppermute | solution.py:445
  106.6 17.6 %collective-permute-start.23 = (bf16[320,512]{1,0:T(8,128)(2,1)S(1)}, bf16[320,512]{1,0:T(8,128)(2,1)S(1)}, u32[]{:S(2)}, u32[]{:S(2)}) collective-permute-start(bf16[320,512]{1,0:T(8,128)(2,1)S(1)} %get-tuple-element.73), channel_id=1, source_target_pairs={{0,2},{1,3},{2,4},{3,5},{4,6},{5,7},{6,0},{7,1},{8,10},{9,11},{10,... | collective-permute-start | bytes 983048 | tf_op jit(solution)/shard_map/ppermute | solution.py:445
  107.0 20.9 %collective-permute-start.19 = (bf16[320,512]{1,0:T(8,128)(2,1)S(1)}, bf16[320,512]{1,0:T(8,128)(2,1)S(1)}, u32[]{:S(2)}, u32[]{:S(2)}) collective-permute-start(bf16[320,512]{1,0:T(8,128)(2,1)S(1)} %get-tuple-element.68), channel_id=1, source_target_pairs={{0,6},{1,7},{2,0},{3,1},{4,2},{5,3},{6,4},{7,5},{8,14},{9,15},{10,... | collective-permute-start | bytes 983048 | tf_op jit(solution)/shard_map/ppermute | solution.py:445
  113.9 13.1 %collective-permute-start.22 = (bf16[320,512]{1,0:T(8,128)(2,1)S(1)}, bf16[320,512]{1,0:T(8,128)(2,1)S(1)}, u32[]{:S(2)}, u32[]{:S(2)}) collective-permute-start(bf16[320,512]{1,0:T(8,128)(2,1)S(1)} %shard_map.137), channel_id=1, source_target_pairs={{0,6},{1,7},{2,0},{3,1},{4,2},{5,3},{6,4},{7,5},{8,14},{9,15},{10,... | collective-permute-start | bytes 983048 | tf_op jit(solution)/shard_map/ppermute | solution.py:445
  117.2 12.8 %collective-permute-start.18 = (bf16[320,512]{1,0:T(8,128)(2,1)S(1)}, bf16[320,512]{1,0:T(8,128)(2,1)S(1)}, u32[]{:S(2)}, u32[]{:S(2)}) collective-permute-start(bf16[320,512]{1,0:T(8,128)(2,1)S(1)} %shard_map.133), channel_id=1, source_target_pairs={{0,2},{1,3},{2,4},{3,5},{4,6},{5,7},{6,0},{7,1},{8,10},{9,11},{10,... | collective-permute-start | bytes 983048 | tf_op jit(solution)/shard_map/ppermute | solution.py:445
  (2 other events, 1.9 us)

commit v7 on v6

--- a/solution.py
+++ b/solution.py
@@ -468,9 +468,10 @@
     first_far = along(first_up, 1)
     later, first_far = lax.optimization_barrier((second, first_far))
     second_up = along(later, 1)
-    second_far = along(second_down, -1)
     firsts = [first, first_up, first_down, first_far]
     firsts = firsts + [swap(v) for v in firsts]
+    second_down, firsts[-1] = lax.optimization_barrier((second_down, firsts[-1]))
+    second_far = along(second_down, -1)
     here = place[None]
     taps = jnp.concatenate([conv_inner, conv_bc], 1)
 

time: 131 us -> 138 us (1.053)
  waiting for transfers between devices: 44.1 us -> 49.1 us
  starting transfers between devices: 39.3 us -> 40.7 us
    ppermute x12, waiting for transfers between devices: 29.2 us -> 34.2 us  [along(): return lax.ppermute(values, 'head', route)]
  transfers between devices with their start and end apart: 26 -> 26, of which waited for: 13 -> 13; matrix products, arithmetic and copies ran while one was open for 5% -> 4% of each run, Pallas kernels for 22% -> 21%
where the time goes in v7:
time: 138 us; the launch traced here: 137 us
  waiting for transfers between devices  49.1 us (36%)
  starting transfers between devices  40.7 us (29%)
  Pallas kernels  38.4 us (28%)
  local copies, waits for them, and re-layouts  6.6 us (5%)
  other arithmetic  1.41 us (1%)
    pallas_call x17, Pallas kernels, run(): pl.pallas_call(kernel, out_shape=[pltpu.HBM(v.shape, v.dtype) if i in far...  38.4 us
    ppermute x12, waiting for transfers between devices, along(): return lax.ppermute(values, 'head', route)  34.2 us
    ppermute x12, starting transfers between devices, along(): return lax.ppermute(values, 'head', route)  18.7 us
    all_to_all x2, starting transfers between devices, exchange(): return lax.all_to_all(blocks, 'ctx', 0, 0).reshape(values.shape)  16 us
    all_to_all x2, waiting for transfers between devices, exchange(): return lax.all_to_all(blocks, 'ctx', 0, 0).reshape(values.shape)  13.4 us
    unnamed x18, local copies, waits for them, and re-layouts  6.06 us
    ppermute x1, starting transfers between devices, on_device(): before = lax.ppermute(edge, 'ctx', [(i, i + 1) for i in range(n_ctx - 1)])  3.84 us
  transfers between devices with their start and end apart: 26, of which 13 were waited for; matrix products, arithmetic and copies ran while one was open for 4% of the time, Pallas kernels for 21%

profile of v7, /device:TPU:32, one launch (start us, length us, event | category | flops | bytes accessed | tf_op | source)
XLA Modules:
  0.0 137.2 jit_solution(11426780077467630189)
XLA Ops:
  0.6 1.6 %collective-permute-start = (bf16[320,512]{1,0:T(8,128)(2,1)}, bf16[320,512]{1,0:T(8,128)(2,1)S(1)}, u32[]{:S(2)}, u32[]{:S(2)}) collective-permute-start(bf16[320,512]{1,0:T(8,128)(2,1)} %bitcast.21), channel_id=1, source_target_pairs={{0,2},{1,3},{2,4},{3,5},{4,6},{5,7},{6,0},{7,1},{8,10},{9,11},{10,... | collective-permute-start | bytes 983048 | tf_op jit(solution)/shard_map/ppermute | solution.py:445
  2.2 1.4 %select_maximum_fusion.refs_0_ = f32[32,512]{1,0:T(8,128)} fusion(f32[10,512]{1,0:T(8,128)} %bitcast.19, f32[10,512]{1,0:T(8,128)} %bitcast.20), kind=kLoop, calls=%fused_computation | loop fusion | flops 81920 | bytes 106496 | tf_op jit(solution)/shard_map/concatenate | solution.py:459
  3.6 1.9 %shard_map.123 = (f32[80,512]{1,0:T(8,128)S(1)}, f32[512,32]{1,0:T(8,128)S(1)}, f32[8,640]{1,0:T(8,128)S(1)}, f32[8,128]{1,0:T(8,128)S(1)}) custom-call(f32[32,512]{1,0:T(8,128)} %select_maximum_fusion.refs_0_), custom_call_target="tpu_custom_call" | custom-call | flops 100000000 | bytes 1000000 | tf_op jit(solution)/shard_map/pallas_call | solution.py:74
  6.2 5.4 %collective-permute-done.refs_2_ = bf16[320,512]{1,0:T(8,128)(2,1)S(1)} collective-permute-done((bf16[320,512]{1,0:T(8,128)(2,1)}, bf16[320,512]{1,0:T(8,128)(2,1)S(1)}, u32[]{:S(2)}, u32[]{:S(2)}) %collective-permute-start) | collective-permute-done | bytes 327712 | tf_op jit(solution)/shard_map/ppermute | solution.py:445
  11.9 3.0 %collective-permute-start.6 = (bf16[320,512]{1,0:T(8,128)(2,1)}, bf16[320,512]{1,0:T(8,128)(2,1)S(1)}, u32[]{:S(2)}, u32[]{:S(2)}) collective-permute-start(bf16[320,512]{1,0:T(8,128)(2,1)} %bitcast.22), channel_id=1, source_target_pairs={{0,6},{1,7},{2,0},{3,1},{4,2},{5,3},{6,4},{7,5},{8,14},{9,15},{10,... | collective-permute-start | bytes 983048 | tf_op jit(solution)/shard_map/ppermute | solution.py:445
  15.2 6.2 %collective-permute-done.1.refs_4_ = bf16[320,512]{1,0:T(8,128)(2,1)S(1)} collective-permute-done((bf16[320,512]{1,0:T(8,128)(2,1)S(1)}, bf16[320,512]{1,0:T(8,128)(2,1)S(1)}, u32[]{:S(2)}, u32[]{:S(2)}) %collective-permute-start.1) | collective-permute-done | bytes 327712 | tf_op jit(solution)/shard_map/ppermute | solution.py:445
  21.9 1.4 %collective-permute-done.6.refs_3_ = bf16[320,512]{1,0:T(8,128)(2,1)S(1)} collective-permute-done((bf16[320,512]{1,0:T(8,128)(2,1)}, bf16[320,512]{1,0:T(8,128)(2,1)S(1)}, u32[]{:S(2)}, u32[]{:S(2)}) %collective-permute-start.6) | collective-permute-done | bytes 327712 | tf_op jit(solution)/shard_map/ppermute | solution.py:445
  23.3 4.7 %collective-permute-done.3.refs_3_ = bf16[320,512]{1,0:T(8,128)(2,1)S(1)} collective-permute-done((bf16[320,512]{1,0:T(8,128)(2,1)}, bf16[320,512]{1,0:T(8,128)(2,1)S(1)}, u32[]{:S(2)}, u32[]{:S(2)}) %collective-permute-start.3) | collective-permute-done | bytes 327712 | tf_op jit(solution)/shard_map/ppermute | solution.py:445
  28.9 2.7 %collective-permute-start.5 = (bf16[320,512]{1,0:T(8,128)(2,1)S(1)}, bf16[320,512]{1,0:T(8,128)(2,1)S(1)}, u32[]{:S(2)}, u32[]{:S(2)}) collective-permute-start(bf16[320,512]{1,0:T(8,128)(2,1)S(1)} %collective-permute-done.3.refs_3_), channel_id=1, source_target_pairs={{0,6},{1,7},{2,0},{3,1},{4,2},{5,3},{6,4},{7,5},{8,14},{9,15},{10,... | collective-permute-start | bytes 983048 | tf_op jit(solution)/shard_map/ppermute | solution.py:445
  32.1 5.3 %shard_map.124.refs_12_.refs_0_ = bf16[512,896]{1,0:T(8,128)(2,1)S(1)} custom-call(s32[1]{0:T(128)} %bitcast.refs_0_, bf16[320,512]{1,0:T(8,128)(2,1)} %bitcast.24, bf16[320,512]{1,0:T(8,128)(2,1)S(1)} %collective-permute-done.refs_2_, bf16[320,512]{1,0:T(8,128)(2,1)S(1)} %collective-permute-done.6.refs_3_, ...), custom_call_target="tpu_custom_call" | custom-call | flops 2348810240 | bytes 12582912 | tf_op jit(solution)/shard_map/pallas_call | solution.py:74
  39.6 5.5 %shard_map.125 = (bf16[512,896]{1,0:T(8,128)(2,1)S(1)}, bf16[16,896]{1,0:T(8,128)(2,1)S(1)}) custom-call(s32[1]{0:T(128)} %bitcast.refs_0_, bf16[320,512]{1,0:T(8,128)(2,1)} %bitcast.28, bf16[320,512]{1,0:T(8,128)(2,1)S(1)} %collective-permute-done.2.refs_2_, bf16[320,512]{1,0:T(8,128)(2,1)S(1)} %collective-permute-done.3.refs_3_, ...), custom_call_target="tpu_custom_call" | custom-call | flops 2348810240 | bytes 12582912 | tf_op jit(solution)/shard_map/pallas_call | solution.py:74
  45.1 3.8 %collective-permute-start.14 = (bf16[16,896]{1,0:T(8,128)(2,1)S(1)}, bf16[16,896]{1,0:T(8,128)(2,1)S(1)}, u32[]{:S(2)}, u32[]{:S(2)}) collective-permute-start(bf16[16,896]{1,0:T(8,128)(2,1)S(1)} %get-tuple-element.54), channel_id=1, source_target_pairs={{0,8},{8,16},{16,24},{24,32},{32,40},{40,48},{48,56},{56,64},{64,7... | collective-permute-start | bytes 86024 | tf_op jit(solution)/shard_map/ppermute | solution.py:510
  49.0 3.2 %shard_map.126 = (bf16[896,256]{1,0:T(8,128)(2,1)}, bf16[896,256]{1,0:T(8,128)(2,1)}, f32[128,640]{1,0:T(8,128)S(1)}, f32[128,640]{1,0:T(8,128)S(1)}) custom-call(bf16[512,896]{1,0:T(8,128)(2,1)S(1)} %shard_map.124.refs_12_.refs_0_, bf16[512,896]{1,0:T(8,128)(2,1)S(1)} %get-tuple-element.50.refs_1_, f32[4,896]{1,0:T(4,128)S(1)} %constant_dynamic-update-slice_fusion.refs_2_, ...), custom_call_target="tpu_custom_call" | custom-call | flops 1000000000 | bytes 8388608 | tf_op jit(solution)/shard_map/pallas_call | solution.py:74
  52.2 3.7 %shard_map.127 = (bf16[896,256]{1,0:T(8,128)(2,1)}, bf16[896,256]{1,0:T(8,128)(2,1)}, f32[128,640]{1,0:T(8,128)}, f32[128,640]{1,0:T(8,128)}, bf16[256,768]{1,0:T(8,128)(2,1)}) custom-call(bf16[512,896]{1,0:T(8,128)(2,1)S(1)} %shard_map.124.refs_12_.refs_0_, bf16[512,896]{1,0:T(8,128)(2,1)S(1)} %get-tuple-element.50.refs_1_, ...), custom_call_target="tpu_custom_call" | custom-call | flops 1000000000 | bytes 8388608 | tf_op jit(solution)/shard_map/pallas_call | solution.py:74
  55.9 11.3 %all-to-all-start = ((bf16[32,8,768]{2,1,0:T(8,128)(2,1)}), bf16[32,8,768]{2,1,0:T(8,128)(2,1)}, u32[]{:S(2)}, u32[]{:S(2)}) async-start(bf16[32,8,768]{2,1,0:T(8,128)(2,1)} %bitcast.16), calls=%async_computation | async-start | bytes 786432 | tf_op jit(solution)/shard_map/all_to_all | solution.py:452
  67.3 4.2 %copy.13 = bf16[640,2560]{0,1:T(8,128)(2,1)S(1)} copy(bf16[640,2560]{1,0:T(8,128)(2,1)} %param.21) | data formatting | bytes 6553600 | tf_op args[10]
  71.5 1.5 %shard_map.122 = (bf16[1280,640]{1,0:T(8,128)(2,1)S(1)}, bf16[1280,640]{1,0:T(8,128)(2,1)}) custom-call(s32[1]{0:T(128)} %bitcast.refs_0_, bf16[2560,640]{1,0:T(8,128)(2,1)S(1)} %bitcast.14), custom_call_target="tpu_custom_call" | custom-call | flops 1000000 | bytes 6291456 | tf_op jit(solution)/shard_map/pallas_call | solution.py:74
  74.1 7.4 %all-to-all-done = bf16[32,8,768]{2,1,0:T(8,128)(2,1)} async-done(((bf16[32,8,768]{2,1,0:T(8,128)(2,1)}), bf16[32,8,768]{2,1,0:T(8,128)(2,1)}, u32[]{:S(2)}, u32[]{:S(2)}) %all-to-all-start) | async-done | bytes 393248 | tf_op jit(solution)/shard_map/all_to_all | solution.py:452
  81.5 2.3 %shard_map.128 = bf16[256,640]{1,0:T(8,128)(2,1)} custom-call(s32[1]{0:T(128)} %bitcast.2.refs_0_, bf16[256,768]{1,0:T(8,128)(2,1)} %bitcast.8.refs_1_), custom_call_target="tpu_custom_call" | custom-call | flops 100000000 | bytes 1048576 | tf_op jit(solution)/shard_map/pallas_call | solution.py:74
  83.8 4.6 %all-to-all-start.1 = ((bf16[32,8,640]{2,1,0:T(8,128)(2,1)}), bf16[32,8,640]{2,1,0:T(8,128)(2,1)S(1)}, u32[]{:S(2)}, u32[]{:S(2)}) async-start(bf16[32,8,640]{2,1,0:T(8,128)(2,1)} %bitcast.9), calls=%async_computation.1 | async-start | bytes 655360 | tf_op jit(solution)/shard_map/all_to_all | solution.py:452
  89.0 5.7 %shard_map.129 = (f32[640,512]{1,0:T(8,128)}, f32[640,512]{1,0:T(8,128)}) custom-call(bf16[896,256]{1,0:T(8,128)(2,1)} %get-tuple-element.58.refs_0_.refs_1_, bf16[896,256]{1,0:T(8,128)(2,1)} %get-tuple-element.59.refs_1_.refs_2_, bf16[896,256]{1,0:T(8,128)(2,1)} %get-tuple-element.60.refs_2_.refs_3_, bf16[896,256]{1,0:T(8,128)(2,1)} %get-tuple-element.61.refs_3_.refs_4_, ...), custom_call_target="tpu_custom_call" | custom-call | flops 5000000000 | bytes 8388608 | tf_op jit(solution)/shard_map/pallas_call | solution.py:74
  94.7 6.0 %all-to-all-done.1 = bf16[32,8,640]{2,1,0:T(8,128)(2,1)S(1)} async-done(((bf16[32,8,640]{2,1,0:T(8,128)(2,1)}), bf16[32,8,640]{2,1,0:T(8,128)(2,1)S(1)}, u32[]{:S(2)}, u32[]{:S(2)}) %all-to-all-start.1) | async-done | bytes 327712 | tf_op jit(solution)/shard_map/all_to_all | solution.py:452
  100.6 2.8 %shard_map.130 = (bf16[640,512]{1,0:T(8,128)(2,1)S(1)}, bf16[640,512]{1,0:T(8,128)(2,1)S(1)}) custom-call(bf16[256,640]{1,0:T(8,128)(2,1)S(1)} %bitcast.15, bf16[896,256]{1,0:T(8,128)(2,1)} %get-tuple-element.58.refs_0_.refs_1_, bf16[896,256]{1,0:T(8,128)(2,1)} %get-tuple-element.59.refs_1_.refs_2_, bf16[896,256]{1,0:T(8,128)(2,1)} %get-tuple-element.60.refs_2_.refs_3_, ...), custom_call_target="tpu_custom_call" | custom-call | flops 1000000000 | bytes 6291456 | tf_op jit(solution)/shard_map/pallas_call | solution.py:74
  104.1 1.2 shard_map.135.refs_0_
  106.5 1.2 shard_map.136
  107.7 2.7 %collective-permute-start.21 = (bf16[320,512]{1,0:T(8,128)(2,1)S(1)}, bf16[320,512]{1,0:T(8,128)(2,1)S(1)}, u32[]{:S(2)}, u32[]{:S(2)}) collective-permute-start(bf16[320,512]{1,0:T(8,128)(2,1)S(1)} %get-tuple-element.76), channel_id=1, source_target_pairs={{0,6},{1,7},{2,0},{3,1},{4,2},{5,3},{6,4},{7,5},{8,14},{9,15},{10,... | collective-permute-start | bytes 983048 | tf_op jit(solution)/shard_map/ppermute | solution.py:445
  110.4 1.2 shard_map.132
  111.8 3.1 %collective-permute-start.19 = (bf16[320,512]{1,0:T(8,128)(2,1)S(1)}, bf16[320,512]{1,0:T(8,128)(2,1)S(1)}, u32[]{:S(2)}, u32[]{:S(2)}) collective-permute-start(bf16[320,512]{1,0:T(8,128)(2,1)S(1)} %get-tuple-element.72), channel_id=1, source_target_pairs={{0,6},{1,7},{2,0},{3,1},{4,2},{5,3},{6,4},{7,5},{8,14},{9,15},{10,... | collective-permute-start | bytes 983048 | tf_op jit(solution)/shard_map/ppermute | solution.py:445
  115.0 3.5 %collective-permute-done.21.refs_1_ = bf16[320,512]{1,0:T(8,128)(2,1)S(1)} collective-permute-done((bf16[320,512]{1,0:T(8,128)(2,1)S(1)}, bf16[320,512]{1,0:T(8,128)(2,1)S(1)}, u32[]{:S(2)}, u32[]{:S(2)}) %collective-permute-start.21) | collective-permute-done | bytes 327712 | tf_op jit(solution)/shard_map/ppermute | solution.py:445
  118.5 3.8 %collective-permute-start.22 = (bf16[320,512]{1,0:T(8,128)(2,1)S(1)}, bf16[320,512]{1,0:T(8,128)(2,1)S(1)}, u32[]{:S(2)}, u32[]{:S(2)}) collective-permute-start(bf16[320,512]{1,0:T(8,128)(2,1)S(1)} %shard_map.137), channel_id=1, source_target_pairs={{0,6},{1,7},{2,0},{3,1},{4,2},{5,3},{6,4},{7,5},{8,14},{9,15},{10,... | collective-permute-start | bytes 983048 | tf_op jit(solution)/shard_map/ppermute | solution.py:445
  123.6 6.9 %collective-permute-done.23.refs_2_ = bf16[320,512]{1,0:T(8,128)(2,1)S(1)} collective-permute-done((bf16[320,512]{1,0:T(8,128)(2,1)S(1)}, bf16[320,512]{1,0:T(8,128)(2,1)S(1)}, u32[]{:S(2)}, u32[]{:S(2)}) %collective-permute-start.23) | collective-permute-done | bytes 327712 | tf_op jit(solution)/shard_map/ppermute | solution.py:445
  132.5 3.8 %collective-permute-done.18.refs_1_ = bf16[320,512]{1,0:T(8,128)(2,1)S(1)} collective-permute-done((bf16[320,512]{1,0:T(8,128)(2,1)S(1)}, bf16[320,512]{1,0:T(8,128)(2,1)S(1)}, u32[]{:S(2)}, u32[]{:S(2)}) %collective-permute-start.18) | collective-permute-done | bytes 327712 | tf_op jit(solution)/shard_map/ppermute | solution.py:445
  (58 shorter events, 13.4 us)
Async XLA Ops:
  0.6 10.9 %collective-permute-start = (bf16[320,512]{1,0:T(8,128)(2,1)}, bf16[320,512]{1,0:T(8,128)(2,1)S(1)}, u32[]{:S(2)}, u32[]{:S(2)}) collective-permute-start(bf16[320,512]{1,0:T(8,128)(2,1)} %bitcast.21), channel_id=1, source_target_pairs={{0,2},{1,3},{2,4},{3,5},{4,6},{5,7},{6,0},{7,1},{8,10},{9,11},{10,... | collective-permute-start | bytes 983048 | tf_op jit(solution)/shard_map/ppermute | solution.py:445
  6.2 45.9 %copy-start.2 = (f32[80,512]{1,0:T(8,128)}, f32[80,512]{1,0:T(8,128)S(1)}, u32[]{:S(2)}) copy-start(f32[80,512]{1,0:T(8,128)S(1)} %get-tuple-element.51.refs_3_.refs_4_.refs_7_) | copy-start | bytes 491524
  6.2 45.9 %copy-start.3 = (f32[8,640]{1,0:T(8,128)}, f32[8,640]{1,0:T(8,128)S(1)}, u32[]{:S(2)}) copy-start(f32[8,640]{1,0:T(8,128)S(1)} %get-tuple-element.52.refs_4_.refs_8_) | copy-start | bytes 61444
  11.6 9.8 %collective-permute-start.1 = (bf16[320,512]{1,0:T(8,128)(2,1)S(1)}, bf16[320,512]{1,0:T(8,128)(2,1)S(1)}, u32[]{:S(2)}, u32[]{:S(2)}) collective-permute-start(bf16[320,512]{1,0:T(8,128)(2,1)S(1)} %collective-permute-done.refs_2_), channel_id=1, source_target_pairs={{0,2},{1,3},{2,4},{3,5},{4,6},{5,7},{6,0},{7,1},{8,10},{9,11},{10,... | collective-permute-start | bytes 983048 | tf_op jit(solution)/shard_map/ppermute | solution.py:445
  11.9 11.4 %collective-permute-start.6 = (bf16[320,512]{1,0:T(8,128)(2,1)}, bf16[320,512]{1,0:T(8,128)(2,1)S(1)}, u32[]{:S(2)}, u32[]{:S(2)}) collective-permute-start(bf16[320,512]{1,0:T(8,128)(2,1)} %bitcast.22), channel_id=1, source_target_pairs={{0,6},{1,7},{2,0},{3,1},{4,2},{5,3},{6,4},{7,5},{8,14},{9,15},{10,... | collective-permute-start | bytes 983048 | tf_op jit(solution)/shard_map/ppermute | solution.py:445
  14.8 13.2 %collective-permute-start.3 = (bf16[320,512]{1,0:T(8,128)(2,1)}, bf16[320,512]{1,0:T(8,128)(2,1)S(1)}, u32[]{:S(2)}, u32[]{:S(2)}) collective-permute-start(bf16[320,512]{1,0:T(8,128)(2,1)} %bitcast.25), channel_id=1, source_target_pairs={{0,6},{1,7},{2,0},{3,1},{4,2},{5,3},{6,4},{7,5},{8,14},{9,15},{10,... | collective-permute-start | bytes 983048 | tf_op jit(solution)/shard_map/ppermute | solution.py:445
  21.4 7.5 %collective-permute-start.4 = (bf16[320,512]{1,0:T(8,128)(2,1)S(1)}, bf16[320,512]{1,0:T(8,128)(2,1)S(1)}, u32[]{:S(2)}, u32[]{:S(2)}) collective-permute-start(bf16[320,512]{1,0:T(8,128)(2,1)S(1)} %collective-permute-done.1.refs_4_), channel_id=1, source_target_pairs={{0,1},{1,0},{2,3},{3,2},{4,5},{5,4},{6,7},{7,6},{8,9},{9,8},{10,11... | collective-permute-start | bytes 983048 | tf_op jit(solution)/shard_map/ppermute | solution.py:448
  21.4 10.2 %collective-permute-start.7 = (bf16[320,512]{1,0:T(8,128)(2,1)}, bf16[320,512]{1,0:T(8,128)(2,1)S(1)}, u32[]{:S(2)}, u32[]{:S(2)}) collective-permute-start(bf16[320,512]{1,0:T(8,128)(2,1)} %bitcast.23), channel_id=1, source_target_pairs={{0,1},{1,0},{2,3},{3,2},{4,5},{5,4},{6,7},{7,6},{8,9},{9,8},{10,11... | collective-permute-start | bytes 983048 | tf_op jit(solution)/shard_map/ppermute | solution.py:448
  21.9 9.7 %collective-permute-start.8 = (bf16[320,512]{1,0:T(8,128)(2,1)S(1)}, bf16[320,512]{1,0:T(8,128)(2,1)S(1)}, u32[]{:S(2)}, u32[]{:S(2)}) collective-permute-start(bf16[320,512]{1,0:T(8,128)(2,1)S(1)} %collective-permute-done.refs_2_), channel_id=1, source_target_pairs={{0,1},{1,0},{2,3},{3,2},{4,5},{5,4},{6,7},{7,6},{8,9},{9,8},{10,11... | collective-permute-start | bytes 983048 | tf_op jit(solution)/shard_map/ppermute | solution.py:448
  23.3 8.8 %collective-permute-start.9 = (bf16[320,512]{1,0:T(8,128)(2,1)S(1)}, bf16[320,512]{1,0:T(8,128)(2,1)}, u32[]{:S(2)}, u32[]{:S(2)}) collective-permute-start(bf16[320,512]{1,0:T(8,128)(2,1)S(1)} %collective-permute-done.6.refs_3_), channel_id=1, source_target_pairs={{0,1},{1,0},{2,3},{3,2},{4,5},{5,4},{6,7},{7,6},{8,9},{9,8},{10,11... | collective-permute-start | bytes 983048 | tf_op jit(solution)/shard_map/ppermute | solution.py:448
  28.0 9.5 %collective-permute-start.2 = (bf16[320,512]{1,0:T(8,128)(2,1)}, bf16[320,512]{1,0:T(8,128)(2,1)S(1)}, u32[]{:S(2)}, u32[]{:S(2)}) collective-permute-start(bf16[320,512]{1,0:T(8,128)(2,1)} %bitcast.26), channel_id=1, source_target_pairs={{0,2},{1,3},{2,4},{3,5},{4,6},{5,7},{6,0},{7,1},{8,10},{9,11},{10,... | collective-permute-start | bytes 983048 | tf_op jit(solution)/shard_map/ppermute | solution.py:445
  28.9 8.6 %collective-permute-start.5 = (bf16[320,512]{1,0:T(8,128)(2,1)S(1)}, bf16[320,512]{1,0:T(8,128)(2,1)S(1)}, u32[]{:S(2)}, u32[]{:S(2)}) collective-permute-start(bf16[320,512]{1,0:T(8,128)(2,1)S(1)} %collective-permute-done.3.refs_3_), channel_id=1, source_target_pairs={{0,6},{1,7},{2,0},{3,1},{4,2},{5,3},{6,4},{7,5},{8,14},{9,15},{10,... | collective-permute-start | bytes 983048 | tf_op jit(solution)/shard_map/ppermute | solution.py:445
  31.6 6.5 %collective-permute-start.10 = (bf16[320,512]{1,0:T(8,128)(2,1)}, bf16[320,512]{1,0:T(8,128)(2,1)S(1)}, u32[]{:S(2)}, u32[]{:S(2)}) collective-permute-start(bf16[320,512]{1,0:T(8,128)(2,1)} %bitcast.27), channel_id=1, source_target_pairs={{0,1},{1,0},{2,3},{3,2},{4,5},{5,4},{6,7},{7,6},{8,9},{9,8},{10,11... | collective-permute-start | bytes 983048 | tf_op jit(solution)/shard_map/ppermute | solution.py:448
  31.6 6.5 %collective-permute-start.12 = (bf16[320,512]{1,0:T(8,128)(2,1)S(1)}, bf16[320,512]{1,0:T(8,128)(2,1)S(1)}, u32[]{:S(2)}, u32[]{:S(2)}) collective-permute-start(bf16[320,512]{1,0:T(8,128)(2,1)S(1)} %collective-permute-done.3.refs_3_), channel_id=1, source_target_pairs={{0,1},{1,0},{2,3},{3,2},{4,5},{5,4},{6,7},{7,6},{8,9},{9,8},{10,11... | collective-permute-start | bytes 983048 | tf_op jit(solution)/shard_map/ppermute | solution.py:448
  32.1 6.0 %copy-start.5 = (f32[4,640]{1,0:T(4,128)S(1)}, f32[4,640]{1,0:T(4,128)}, u32[]{:S(2)}) copy-start(f32[4,640]{1,0:T(4,128)} %param.18) | copy-start | bytes 30724
  32.1 6.0 %copy-start.6 = (f32[4,256]{1,0:T(4,128)S(1)}, f32[4,256]{1,0:T(4,128)}, u32[]{:S(2)}) copy-start(f32[4,256]{1,0:T(4,128)} %param.19) | copy-start | bytes 12292
  37.5 1.7 %collective-permute-start.11 = (bf16[320,512]{1,0:T(8,128)(2,1)S(1)}, bf16[320,512]{1,0:T(8,128)(2,1)S(1)}, u32[]{:S(2)}, u32[]{:S(2)}) collective-permute-start(bf16[320,512]{1,0:T(8,128)(2,1)S(1)} %collective-permute-done.2.refs_2_), channel_id=1, source_target_pairs={{0,1},{1,0},{2,3},{3,2},{4,5},{5,4},{6,7},{7,6},{8,9},{9,8},{10,11... | collective-permute-start | bytes 983048 | tf_op jit(solution)/shard_map/ppermute | solution.py:448
  37.7 2.0 %collective-permute-start.13 = (bf16[320,512]{1,0:T(8,128)(2,1)S(1)}, bf16[320,512]{1,0:T(8,128)(2,1)S(1)}, u32[]{:S(2)}, u32[]{:S(2)}) collective-permute-start(bf16[320,512]{1,0:T(8,128)(2,1)S(1)} %collective-permute-done.5.refs_4_), channel_id=1, source_target_pairs={{0,1},{1,0},{2,3},{3,2},{4,5},{5,4},{6,7},{7,6},{8,9},{9,8},{10,11... | collective-permute-start | bytes 983048 | tf_op jit(solution)/shard_map/ppermute | solution.py:448
  45.1 7.0 %collective-permute-start.14 = (bf16[16,896]{1,0:T(8,128)(2,1)S(1)}, bf16[16,896]{1,0:T(8,128)(2,1)S(1)}, u32[]{:S(2)}, u32[]{:S(2)}) collective-permute-start(bf16[16,896]{1,0:T(8,128)(2,1)S(1)} %get-tuple-element.54), channel_id=1, source_target_pairs={{0,8},{8,16},{16,24},{24,32},{32,40},{40,48},{48,56},{56,64},{64,7... | collective-permute-start | bytes 86024 | tf_op jit(solution)/shard_map/ppermute | solution.py:510
  55.9 25.6 %all-to-all-start = ((bf16[32,8,768]{2,1,0:T(8,128)(2,1)}), bf16[32,8,768]{2,1,0:T(8,128)(2,1)}, u32[]{:S(2)}, u32[]{:S(2)}) async-start(bf16[32,8,768]{2,1,0:T(8,128)(2,1)} %bitcast.16), calls=%async_computation | async-start | bytes 786432 | tf_op jit(solution)/shard_map/all_to_all | solution.py:452
  71.5 17.0 %copy-start.7 = (f32[10]{0:T(128)S(1)}, f32[10]{0:T(128)}, u32[]{:S(2)}) copy-start(f32[10]{0:T(128)} %param.20) | copy-start | bytes 124
  74.1 32.4 %collective-permute-start.15 = (bf16[1280,640]{1,0:T(8,128)(2,1)}, bf16[1280,640]{1,0:T(8,128)(2,1)S(1)}, u32[]{:S(2)}, u32[]{:S(2)}) collective-permute-start(bf16[1280,640]{1,0:T(8,128)(2,1)} %get-tuple-element.68), channel_id=1, source_target_pairs={{0,1},{1,0},{2,3},{3,2},{4,5},{5,4},{6,7},{7,6},{8,9},{9,8},{10,11... | collective-permute-start | bytes 4915208 | tf_op jit(solution)/shard_map/ppermute | solution.py:448
  83.8 16.8 %all-to-all-start.1 = ((bf16[32,8,640]{2,1,0:T(8,128)(2,1)}), bf16[32,8,640]{2,1,0:T(8,128)(2,1)S(1)}, u32[]{:S(2)}, u32[]{:S(2)}) async-start(bf16[32,8,640]{2,1,0:T(8,128)(2,1)} %bitcast.9), calls=%async_computation.1 | async-start | bytes 655360 | tf_op jit(solution)/shard_map/all_to_all | solution.py:452
  100.6 3.4 %copy-start.1 = (bf16[1280,640]{1,0:T(8,128)(2,1)S(1)}, bf16[1280,640]{1,0:T(8,128)(2,1)}, u32[]{:S(2)}) copy-start(bf16[1280,640]{1,0:T(8,128)(2,1)} %copy-done) | copy-start | bytes 4915204
  103.5 3.0 %collective-permute-start.20 = (bf16[640,512]{1,0:T(8,128)(2,1)S(1)}, bf16[640,512]{1,0:T(8,128)(2,1)S(1)}, u32[]{:S(2)}, u32[]{:S(2)}) collective-permute-start(bf16[640,512]{1,0:T(8,128)(2,1)S(1)} %get-tuple-element.73.refs_1_), channel_id=1, source_target_pairs={{0,1},{1,0},{2,3},{3,2},{4,5},{5,4},{6,7},{7,6},{8,9},{9,8},{10,11... | collective-permute-start | bytes 1966088 | tf_op jit(solution)/shard_map/ppermute | solution.py:448
  103.6 6.8 %collective-permute-start.16 = (bf16[640,512]{1,0:T(8,128)(2,1)S(1)}, bf16[640,512]{1,0:T(8,128)(2,1)S(1)}, u32[]{:S(2)}, u32[]{:S(2)}) collective-permute-start(bf16[640,512]{1,0:T(8,128)(2,1)S(1)} %get-tuple-element.67.refs_1_), channel_id=1, source_target_pairs={{0,1},{1,0},{2,3},{3,2},{4,5},{5,4},{6,7},{7,6},{8,9},{9,8},{10,11... | collective-permute-start | bytes 1966088 | tf_op jit(solution)/shard_map/ppermute | solution.py:448
  107.7 10.8 %collective-permute-start.21 = (bf16[320,512]{1,0:T(8,128)(2,1)S(1)}, bf16[320,512]{1,0:T(8,128)(2,1)S(1)}, u32[]{:S(2)}, u32[]{:S(2)}) collective-permute-start(bf16[320,512]{1,0:T(8,128)(2,1)S(1)} %get-tuple-element.76), channel_id=1, source_target_pairs={{0,6},{1,7},{2,0},{3,1},{4,2},{5,3},{6,4},{7,5},{8,14},{9,15},{10,... | collective-permute-start | bytes 983048 | tf_op jit(solution)/shard_map/ppermute | solution.py:445
  111.5 11.9 %collective-permute-start.17 = (bf16[320,512]{1,0:T(8,128)(2,1)S(1)}, bf16[320,512]{1,0:T(8,128)(2,1)S(1)}, u32[]{:S(2)}, u32[]{:S(2)}) collective-permute-start(bf16[320,512]{1,0:T(8,128)(2,1)S(1)} %get-tuple-element.71), channel_id=1, source_target_pairs={{0,2},{1,3},{2,4},{3,5},{4,6},{5,7},{6,0},{7,1},{8,10},{9,11},{10,... | collective-permute-start | bytes 983048 | tf_op jit(solution)/shard_map/ppermute | solution.py:445
  111.6 18.8 %collective-permute-start.23 = (bf16[320,512]{1,0:T(8,128)(2,1)S(1)}, bf16[320,512]{1,0:T(8,128)(2,1)S(1)}, u32[]{:S(2)}, u32[]{:S(2)}) collective-permute-start(bf16[320,512]{1,0:T(8,128)(2,1)S(1)} %get-tuple-element.77), channel_id=1, source_target_pairs={{0,2},{1,3},{2,4},{3,5},{4,6},{5,7},{6,0},{7,1},{8,10},{9,11},{10,... | collective-permute-start | bytes 983048 | tf_op jit(solution)/shard_map/ppermute | solution.py:445
  111.8 20.6 %collective-permute-start.19 = (bf16[320,512]{1,0:T(8,128)(2,1)S(1)}, bf16[320,512]{1,0:T(8,128)(2,1)S(1)}, u32[]{:S(2)}, u32[]{:S(2)}) collective-permute-start(bf16[320,512]{1,0:T(8,128)(2,1)S(1)} %get-tuple-element.72), channel_id=1, source_target_pairs={{0,6},{1,7},{2,0},{3,1},{4,2},{5,3},{6,4},{7,5},{8,14},{9,15},{10,... | collective-permute-start | bytes 983048 | tf_op jit(solution)/shard_map/ppermute | solution.py:445
  118.5 13.1 %collective-permute-start.22 = (bf16[320,512]{1,0:T(8,128)(2,1)S(1)}, bf16[320,512]{1,0:T(8,128)(2,1)S(1)}, u32[]{:S(2)}, u32[]{:S(2)}) collective-permute-start(bf16[320,512]{1,0:T(8,128)(2,1)S(1)} %shard_map.137), channel_id=1, source_target_pairs={{0,6},{1,7},{2,0},{3,1},{4,2},{5,3},{6,4},{7,5},{8,14},{9,15},{10,... | collective-permute-start | bytes 983048 | tf_op jit(solution)/shard_map/ppermute | solution.py:445
  123.5 12.8 %collective-permute-start.18 = (bf16[320,512]{1,0:T(8,128)(2,1)S(1)}, bf16[320,512]{1,0:T(8,128)(2,1)S(1)}, u32[]{:S(2)}, u32[]{:S(2)}) collective-permute-start(bf16[320,512]{1,0:T(8,128)(2,1)S(1)} %shard_map.133), channel_id=1, source_target_pairs={{0,2},{1,3},{2,4},{3,5},{4,6},{5,7},{6,0},{7,1},{8,10},{9,11},{10,... | collective-permute-start | bytes 983048 | tf_op jit(solution)/shard_map/ppermute | solution.py:445
  (2 other events, 1.9 us)
